TPU v7x, 32 devices: a whole 2x2x4 slice. The times are simulated.
32 devices in a mesh: seq: 4 (over x, core), dp: 8 (over z, y).
Axes of the slice: x: 2, y: 2, z: 4, core: 2. Of those that a mesh axis runs over, the one named last changes fastest.
Arguments:
- tokens: bfloat16 [8, 1024, 2048], P('dp', 'seq'), may hold values from -6 to 6
- joint_weight: bfloat16 [2048, 6144], P(('seq', 'dp')), may hold values from -0.125 to 0.125
- output_weight: bfloat16 [2048, 2048], P(('seq', 'dp')), may hold values from -0.5 to 0.5
- up_weight: bfloat16 [2048, 8192], P(('seq', 'dp')), may hold values from -0.125 to 0.125
- down_weight: bfloat16 [2048, 8192], P(('seq', 'dp')), may hold values from -0.0625 to 0.0625
- joint_bias: bfloat16 [6144], P(('seq', 'dp')), may hold values from -1.1953125 to 1.1953125
- output_bias: bfloat16 [2048], P(('seq', 'dp')), may hold values from -1.1953125 to 1.1953125
- up_bias: bfloat16 [8192], P(('seq', 'dp')), may hold values from -1.1953125 to 1.1953125
- down_bias: bfloat16 [2048], P(('seq', 'dp')), may hold values from -1.1953125 to 1.1953125
- norm_gain: bfloat16 [2048], P(('seq', 'dp')), may hold values from 0.5 to 1.5
- norm_shift: bfloat16 [2048], P(('seq', 'dp')), may hold values from -1.1953125 to 1.1953125
- segments: int32 [8, 1024], P('dp', 'seq'), may hold values from 0 to 2, as said below
- positions: int32 [8, 1024], P('dp', 'seq'), may hold values from 0 to 895, as said below
- cotangent: bfloat16 [8, 1024, 2048], P('dp', 'seq'), may hold values from -6 to 6
Outputs:
- layer_out: bfloat16 [8, 1024, 2048], P('dp', 'seq')
- tokens_grad: bfloat16 [8, 1024, 2048], P('dp', 'seq')
- joint_weight_grad: float32 [2048, 6144], P(('seq', 'dp'))
- output_weight_grad: float32 [2048, 2048], P(('seq', 'dp'))
- up_weight_grad: float32 [2048, 8192], P(('seq', 'dp'))
- down_weight_grad: float32 [2048, 8192], P(('seq', 'dp'))
- joint_bias_grad: float32 [6144], P(('seq', 'dp'))
- output_bias_grad: float32 [2048], P(('seq', 'dp'))
- up_bias_grad: float32 [8192], P(('seq', 'dp'))
- down_bias_grad: float32 [2048], P(('seq', 'dp'))
- norm_gain_grad: float32 [2048], P(('seq', 'dp'))
- norm_shift_grad: float32 [2048], P(('seq', 'dp'))
Inputs may be any that keep to these rules, and one draw needn't show every extreme that they name: `segments`: in each sequence the segment numbers never fall and each of 0, 1, 2 occurs; documents 0 and 2 hold fewer than 128 tokens each, at least one. `positions`: A token's place within its document, counting from 0 at the document's first token; document 1 of every sequence holds exactly 1024 - max(2, 128) tokens.
All inputs are finite; a program needn't handle non-finite values.
Results may differ from a plain program's by a relative error of at most 0.0079.
Values may be sent and summed in bfloat16 or wider, within the bound.
No kernel may reach another device: no remote copies, remote signals or barrier semaphores. Data moves between devices by JAX's collectives and lax.ppermute only.
A program may use at most 704 MiB of HBM per device.

v0:
```python
import jax
import jax.numpy as jnp
from jax import lax
from jax.sharding import PartitionSpec as P

H = 32
HD = 64
ROT = 32
HGROUP = 8


NEG_FILL = -1e30
NORM_EPS = 1e-05


def turn_tables(places):
    frequency = 10000.0 ** (-jnp.arange(0, ROT, 2, dtype=jnp.float32) / ROT)
    angles = places.astype(jnp.float32)[:, None] * frequency[None, :]
    angles = jnp.concatenate([angles, angles], 1)
    return (jnp.cos(angles)[:, None, :], jnp.sin(angles)[:, None, :])


def rotate(inputs, cosine_table, sine_table):
    half_rot = ROT // 2
    rotary = inputs[..., :ROT]
    turned = jnp.concatenate([-rotary[..., half_rot:], rotary[..., :half_rot]], -1)
    return jnp.concatenate([rotary * cosine_table + turned * sine_table, inputs[..., ROT:]], -1)


def rotate_back(grads, cosine_table, sine_table):
    half_rot = ROT // 2
    rotary = grads[..., :ROT]
    sined = rotary * sine_table
    turned = jnp.concatenate([sined[..., half_rot:], -sined[..., :half_rot]], -1)
    return jnp.concatenate([rotary * cosine_table + turned, grads[..., ROT:]], -1)


def trans_dot(left, right):
    return lax.dot_general(
        left, right, (((0,), (0,)), ((), ())), preferred_element_type=jnp.float32
    )


def right_dot(left, right):
    return lax.dot_general(
        left, right, (((1,), (1,)), ((), ())), preferred_element_type=jnp.float32
    )


def gelu_tanh(inputs):
    return jax.nn.gelu(inputs, approximate=True)


def body(
    tokens,
    joint_weight,
    output_weight,
    up_weight,
    down_weight,
    joint_bias,
    output_bias,
    up_bias,
    down_bias,
    norm_gain,
    norm_shift,
    segments,
    positions,
    cotangent,
):
    row_count, width = (tokens.shape[1], tokens.shape[2])
    hidden_width = up_weight.shape[1]
    head_blocks = H // HGROUP
    score_scale = HD ** (-0.5)
    inputs = tokens.reshape(row_count, width).astype(jnp.float32)
    joint_full, output_full, up_full, down_full, gain_full, shift_full = (
        lax.all_gather(joint_bias, ("seq", "dp"), axis=0, tiled=True),
        lax.all_gather(output_bias, ("seq", "dp"), axis=0, tiled=True),
        lax.all_gather(up_bias, ("seq", "dp"), axis=0, tiled=True),
        lax.all_gather(down_bias, ("seq", "dp"), axis=0, tiled=True),
        lax.all_gather(norm_gain, ("seq", "dp"), axis=0, tiled=True),
        lax.all_gather(norm_shift, ("seq", "dp"), axis=0, tiled=True),
    )
    gain_wide = gain_full.astype(jnp.float32)
    centered = inputs - jnp.mean(inputs, 1, keepdims=True)
    inv_std = lax.rsqrt(jnp.mean(centered * centered, 1, keepdims=True) + NORM_EPS)
    normalized = centered * inv_std
    normed = (normalized * gain_wide + shift_full.astype(jnp.float32)).astype(jnp.bfloat16)
    pieces = (
        lax.all_gather(joint_weight, ("seq", "dp"), axis=0, tiled=True),
        lax.all_gather(up_weight, ("seq", "dp"), axis=0, tiled=True),
    )
    columns = normed
    joint_sum = jnp.dot(columns, pieces[0], preferred_element_type=jnp.float32)
    up_sum = jnp.dot(columns, pieces[1], preferred_element_type=jnp.float32)
    joint_out = joint_sum + joint_full.astype(jnp.float32)
    up_pre = up_sum + up_full.astype(jnp.float32)
    cosine_table, sine_table = turn_tables(positions.reshape(row_count))
    query_low = rotate(
        joint_out[:, :width].reshape(row_count, H, HD), cosine_table, sine_table
    ).astype(jnp.bfloat16)
    key_low = (
        rotate(joint_out[:, width : 2 * width].reshape(row_count, H, HD), cosine_table, sine_table)
        .astype(jnp.bfloat16)
        .reshape(row_count, width)
    )
    value_low = joint_out[:, 2 * width :].astype(jnp.bfloat16)
    own_documents = segments.reshape(row_count).astype(jnp.bfloat16)
    keys_all, values_all, documents_all = (
        lax.all_gather(key_low, "seq", axis=0, tiled=True),
        lax.all_gather(value_low, "seq", axis=0, tiled=True),
        lax.all_gather(own_documents, "seq", axis=0, tiled=True),
    )
    key_count = keys_all.shape[0]
    query_place = lax.axis_index("seq") * row_count + jnp.arange(row_count)
    allowed = (own_documents[:, None] == documents_all[None, :]) & (
        jnp.arange(key_count)[None, :] <= query_place[:, None]
    )

    def to_blocks(array, count):
        return jnp.moveaxis(array.reshape(count, head_blocks, HGROUP, HD), 1, 0)

    def from_blocks(array, count):
        return jnp.moveaxis(array, 0, 1).reshape(count, width)

    query_blocks = to_blocks(query_low.reshape(row_count, width), row_count)
    key_blocks = to_blocks(keys_all, key_count)
    value_blocks = to_blocks(values_all, key_count)

    def block_scores(queries, key_part):
        scores = (
            jnp.einsum("qhd,khd->hqk", queries, key_part, preferred_element_type=jnp.float32)
            * score_scale
        )
        return jnp.where(allowed[None], scores, NEG_FILL)

    def attend(pieces):
        queries, key_part, value_part = pieces
        scores = block_scores(queries, key_part)
        row_max = jnp.max(scores, -1, keepdims=True)
        exps = jnp.exp(scores - row_max)
        row_total = jnp.sum(exps, -1, keepdims=True)
        softmaxed = (exps / row_total).astype(jnp.bfloat16)
        result = jnp.einsum(
            "hqk,khd->qhd", softmaxed, value_part, preferred_element_type=jnp.float32
        )
        return (result, (row_max + jnp.log(row_total))[..., 0])

    attended_blocks, log_totals = lax.map(attend, (query_blocks, key_blocks, value_blocks))
    attended_low = from_blocks(attended_blocks, row_count).astype(jnp.bfloat16)
    hidden_low = gelu_tanh(up_pre).astype(jnp.bfloat16)
    pieces = (
        lax.all_gather(output_weight, ("seq", "dp"), axis=0, tiled=True),
        lax.all_gather(down_weight, ("seq", "dp"), axis=0, tiled=True),
    )
    columns = attended_low
    branch = jnp.dot(columns, pieces[0], preferred_element_type=jnp.float32)
    feed_sum = right_dot(hidden_low, pieces[1])
    layer_out = (
        inputs
        + (branch + output_full.astype(jnp.float32))
        + (feed_sum + down_full.astype(jnp.float32))
    )
    layer_out = layer_out.astype(jnp.bfloat16).reshape(1, row_count, width)
    grad_low = cotangent.reshape(row_count, width)
    grad_full = grad_low.astype(jnp.float32)
    pieces = (
        lax.all_gather(output_weight, ("seq", "dp"), axis=0, tiled=True),
        lax.all_gather(down_weight, ("seq", "dp"), axis=0, tiled=True),
    )
    columns = grad_low
    updated = right_dot(grad_low, pieces[0])
    hidden_grad = jnp.dot(columns, pieces[1], preferred_element_type=jnp.float32)
    attended_grad_low = updated.astype(jnp.bfloat16)
    gelu_value, gelu_pull = jax.vjp(gelu_tanh, up_pre)
    up_grad_low = gelu_pull(hidden_grad)[0].astype(jnp.bfloat16)

    def attend_back(pieces):
        queries, key_part, value_part, out_grad, log_total = pieces
        scores = block_scores(queries, key_part)
        softmaxed = jnp.exp(scores - log_total[..., None])
        probs_grad = jnp.einsum(
            "qhd,khd->hqk", out_grad, value_part, preferred_element_type=jnp.float32
        )
        inner = jnp.sum(softmaxed * probs_grad, -1, keepdims=True)
        score_grad = (softmaxed * (probs_grad - inner)).astype(jnp.bfloat16)
        query_grad = (
            jnp.einsum("hqk,khd->qhd", score_grad, key_part, preferred_element_type=jnp.float32)
            * score_scale
        )
        key_grad = (
            jnp.einsum("hqk,qhd->khd", score_grad, queries, preferred_element_type=jnp.float32)
            * score_scale
        )
        value_grad = jnp.einsum(
            "hqk,qhd->khd",
            softmaxed.astype(jnp.bfloat16),
            out_grad,
            preferred_element_type=jnp.float32,
        )
        return (query_grad, key_grad, value_grad)

    query_grads, key_grads, value_grads = lax.map(
        attend_back,
        (
            query_blocks,
            key_blocks,
            value_blocks,
            to_blocks(attended_grad_low, row_count),
            log_totals,
        ),
    )
    key_own, value_own = (
        lax.psum_scatter(
            from_blocks(key_grads, key_count).astype(jnp.bfloat16),
            "seq",
            scatter_dimension=0,
            tiled=True,
        ).astype(jnp.float32),
        lax.psum_scatter(
            from_blocks(value_grads, key_count).astype(jnp.bfloat16),
            "seq",
            scatter_dimension=0,
            tiled=True,
        ).astype(jnp.float32),
    )
    query_back = rotate_back(
        from_blocks(query_grads, row_count).reshape(row_count, H, HD), cosine_table, sine_table
    ).reshape(row_count, width)
    key_back = rotate_back(key_own.reshape(row_count, H, HD), cosine_table, sine_table).reshape(
        row_count, width
    )
    joint_grad_low = jnp.concatenate([query_back, key_back, value_own], 1).astype(jnp.bfloat16)
    pieces = (
        lax.all_gather(joint_weight, ("seq", "dp"), axis=0, tiled=True),
        lax.all_gather(up_weight, ("seq", "dp"), axis=0, tiled=True),
    )
    produced = right_dot(joint_grad_low, pieces[0]) + right_dot(up_grad_low, pieces[1])
    scaled = produced * gain_wide
    input_part = inv_std * (
        scaled
        - jnp.mean(scaled, 1, keepdims=True)
        - normalized * jnp.mean(scaled * normalized, 1, keepdims=True)
    )
    tokens_grad = (grad_full + input_part).astype(jnp.bfloat16).reshape(1, row_count, width)
    joint_bias_grad, grad_total, up_bias_grad, norm_gain_grad, norm_shift_grad = (
        lax.psum_scatter(
            jnp.sum(joint_grad_low.astype(jnp.float32), 0),
            ("seq", "dp"),
            scatter_dimension=0,
            tiled=True,
        ),
        lax.psum_scatter(jnp.sum(grad_full, 0), ("seq", "dp"), scatter_dimension=0, tiled=True),
        lax.psum_scatter(
            jnp.sum(up_grad_low.astype(jnp.float32), 0),
            ("seq", "dp"),
            scatter_dimension=0,
            tiled=True,
        ),
        lax.psum_scatter(
            jnp.sum(produced * normalized, 0), ("seq", "dp"), scatter_dimension=0, tiled=True
        ),
        lax.psum_scatter(jnp.sum(produced, 0), ("seq", "dp"), scatter_dimension=0, tiled=True),
    )
    inner_part = jnp.concatenate(
        [trans_dot(normed, joint_grad_low), trans_dot(normed, up_grad_low)], 1
    )
    outer_part = jnp.concatenate(
        [trans_dot(attended_low, grad_low), trans_dot(grad_low, hidden_low)], 1
    )
    every_rows = lax.psum_scatter(
        jnp.concatenate([inner_part, outer_part], 1), ("seq", "dp"), scatter_dimension=0, tiled=True
    )
    joint_weight_grad = every_rows[:, : 3 * width]
    up_weight_grad = every_rows[:, 3 * width : 3 * width + hidden_width]
    output_weight_grad = every_rows[:, 3 * width + hidden_width : 4 * width + hidden_width]
    down_weight_grad = every_rows[:, 4 * width + hidden_width :]
    return (
        layer_out,
        tokens_grad,
        joint_weight_grad,
        output_weight_grad,
        up_weight_grad,
        down_weight_grad,
        joint_bias_grad,
        grad_total,
        up_bias_grad,
        grad_total,
        norm_gain_grad,
        norm_shift_grad,
    )


def solution(mesh):
    in_specs = (
        P("dp", "seq", None),
        P(("seq", "dp"), None),
        P(("seq", "dp"), None),
        P(("seq", "dp"), None),
        P(("seq", "dp"), None),
        P(("seq", "dp")),
        P(("seq", "dp")),
        P(("seq", "dp")),
        P(("seq", "dp")),
        P(("seq", "dp")),
        P(("seq", "dp")),
        P("dp", "seq"),
        P("dp", "seq"),
        P("dp", "seq", None),
    )
    out_specs = (
        P("dp", "seq", None),
        P("dp", "seq", None),
        P(("seq", "dp"), None),
        P(("seq", "dp"), None),
        P(("seq", "dp"), None),
        P(("seq", "dp"), None),
        P(("seq", "dp")),
        P(("seq", "dp")),
        P(("seq", "dp")),
        P(("seq", "dp")),
        P(("seq", "dp")),
        P(("seq", "dp")),
    )
    return jax.shard_map(body, mesh=mesh, in_specs=in_specs, out_specs=out_specs, check_vma=False)
```

profile of v0, /device:TPU:0, one launch (start us, length us, event | category | flops | bytes accessed | tf_op | source)
XLA Modules:
  0.0 2736.9 jit_solution(839510406913041583)
XLA Ops:
  13.0 44.1 %all-reduce.11 = (bf16[6144]{0:T(1024)(128)(2,1)S(1)}, bf16[2048]{0:T(1024)(128)(2,1)S(1)}, bf16[2048]{0:T(1024)(128)(2,1)S(1)}, bf16[2048]{0:T(1024)(128)(2,1)}, bf16[2048]{0:T(1024)(128)(2,1)}) all-reduce(bf16[6144]{0:T(1024)(128)(2,1)S(1)} %dynamic-update-slice.2, ...), channel_id=1, replica_groups=mesh['seq'=4,'dp'=8] {'seq','dp'}, use_global_device_ids=true, to_apply=%add.2 | all-reduce | flops 14336 | bytes 57344
  60.3 109.7 %all-gather.9.cloned.1.call-done = bf16[2048,6144]{1,0:T(8,128)(2,1)} async-done(((bf16[64,6144]{1,0:T(8,128)(2,1)}), bf16[2048,6144]{1,0:T(8,128)(2,1)}) %all-gather.9.cloned.1.call-update) | async-done | bytes 25165840 | tf_op jit(solution)/shard_map/all_gather | solution.py:89
  170.0 12.1 convolution_add_fusion.1
  182.1 2.6 copy-done.10
  186.2 4.7 fusion.105
  196.3 2.3 slice_negate_fusion.2
  201.5 5.1 all-gather
  206.7 41.8 %all-gather.15.cloned.1.call-done = bf16[2048,2048]{1,0:T(8,128)(2,1)} async-done(((bf16[64,2048]{1,0:T(8,128)(2,1)}), bf16[2048,2048]{1,0:T(8,128)(2,1)}) %all-gather.15.cloned.1.call-update) | async-done | bytes 8388624 | tf_op jit(solution)/shard_map/all_gather | solution.py:152
  248.6 5.7 convolution_convert_fusion
  257.6 26.2 all-gather.11.cloned.1.call-done
  283.8 6.5 copy.44
  290.3 30.6 %all-gather.13.cloned.1.call-done = bf16[1024,2048]{0,1:T(8,128)(2,1)} async-done(((bf16[256,2048]{0,1:T(8,128)(2,1)}), bf16[1024,2048]{0,1:T(8,128)(2,1)}) %all-gather.13.cloned.1.call-update) | async-done | bytes 4194320 | tf_op jit(solution)/shard_map/all_gather | solution.py:109
  320.9 36.2 %while.30 = (s32[]{:T(128)}, bf16[4,256,8,64]{1,3,2,0:T(8,128)(2,1)S(1)}, f32[4,8,256]{2,1,0:T(8,128)S(1)}, bf16[4,1024,8,64]{1,3,2,0:T(8,128)(2,1)}, bf16[4,256...) while((s32[]{:T(128)}, ...), condition=%wide.region_5.6_spmd.clone.clone, body=%wide.region_2.5_spmd.clone.sunk.clone | while | flops 563345408 | bytes 29169256 | solution.py:148
  321.2 2.8 fusion.156
  326.2 3.7 fusion.158
  330.3 2.8 fusion.156
  333.1 2.1 fusion.157
  335.3 3.7 fusion.158
  339.4 2.8 fusion.156
  344.3 3.7 fusion.158
  348.4 2.8 fusion.156
  351.2 2.1 fusion.157
  353.4 3.7 fusion.158
  357.1 78.0 %while.31 = (s32[]{:T(128)}, f32[4,256,8,64]{1,3,2,0:T(8,128)}, bf16[4,1024,8,64]{1,3,2,0:T(8,128)(2,1)}, bf16[4,1024,8,64]{1,3,2,0:T(8,128)(2,1)}, bf16[4,1024,...) while((s32[]{:T(128)}, f32[4,256,8,64]{1,3,2,0:T(8,128)}, ...), condition=%wide.region_8.9_spmd.clone.clone, body=%wide.region_6.8_spmd.clone.sunk.clone | while | flops 1375598592 | bytes 106496704 | solution.py:202
  357.5 2.5 fusion.167
  360.0 3.4 bitcast_dynamic-update-slice_fusion.11
  363.4 4.5 multiply_reduce_fusion.4
  367.9 2.3 multiply_convert_fusion.6
  370.2 3.6 fusion.169
  377.0 2.5 fusion.167
  379.5 3.4 bitcast_dynamic-update-slice_fusion.11
  382.9 4.5 multiply_reduce_fusion.4
  387.4 2.3 multiply_convert_fusion.6
  389.8 3.6 fusion.169
  396.5 2.5 fusion.167
  399.0 3.4 bitcast_dynamic-update-slice_fusion.11
  402.4 4.5 multiply_reduce_fusion.4
  406.9 2.3 multiply_convert_fusion.6
  409.2 3.6 fusion.169
  416.0 2.5 fusion.167
  418.5 3.4 bitcast_dynamic-update-slice_fusion.11
  421.9 4.5 multiply_reduce_fusion.4
  426.4 2.3 multiply_convert_fusion.6
  428.7 3.6 fusion.169
  437.3 67.9 %all-gather.1 = bf16[32,1,256]{2,1,0:T(2,128)(2,1)S(1)} all-gather(bf16[1,1,256]{2,1,0:T(2,128)(2,1)S(1)} %reshape.228), channel_id=1, replica_groups=mesh['seq'=4,'dp'=8] {'seq','dp'}, dimensions={0}, use_global_device_ids=true | all-gather | bytes 16896 | tf_op jit(solution)/shard_map/all_gather | solution.py:78
  506.5 8.1 fusion.88
  518.7 8.2 reduce-scatter.6.cloned.1.call-done
  526.9 2.6 convert_reduce_fusion.1
  529.5 13.7 fusion.98
  543.2 19.4 fusion.97
  562.6 162.2 %all-gather.17.cloned.1.call-done = bf16[2048,8192]{1,0:T(8,128)(2,1)} async-done(((bf16[64,8192]{1,0:T(8,128)(2,1)}), bf16[2048,8192]{1,0:T(8,128)(2,1)}) %all-gather.17.cloned.1.call-update) | async-done | bytes 33554448 | tf_op jit(solution)/shard_map/all_gather | solution.py:90
  724.8 18.0 convolution_add_fusion
  742.7 28.5 %convolution_bitcast_fusion = f32[2048,8192]{1,0:T(8,128)} fusion(bf16[1,256,2048]{2,1,0:T(8,128)(2,1)S(1)} %copy-done.8, f32[256,8192]{1,0:T(8,128)} %convolution_add_fusion), kind=kOutput, calls=%fused_computation.62 | convolution fusion | flops 8608808960 | bytes 76546048 | tf_op jit(solution)/shard_map/dot_general | solution.py:39
  771.2 149.5 %all-gather.19.cloned.1.call-done = bf16[2048,8192]{1,0:T(8,128)(2,1)} async-done(((bf16[64,8192]{1,0:T(8,128)(2,1)}), bf16[2048,8192]{1,0:T(8,128)(2,1)}) %all-gather.19.cloned.1.call-update) | async-done | bytes 33554448 | tf_op jit(solution)/shard_map/all_gather | solution.py:153
  920.8 22.3 convert_reduce_fusion
  943.1 25.4 fusion.99
  968.5 18.9 fusion.76
  987.4 4.3 convert_reduce_fusion.2
  991.8 132.1 %pad_maximum_fusion = f32[2048,24576]{1,0:T(8,128)} fusion(f32[2048,8192]{1,0:T(8,128)} %convolution_bitcast_fusion, f32[2048,2048]{1,0:T(8,128)} %fusion.88, f32[2048,8192]{1,0:T(8,128)} %fusion.99, f32[2048,6144]{1,0:T(8,128)} %fusion.97), kind=kLoop, calls=%fused_computation.61 | loop fusion | flops 150994944 | bytes 402653184 | tf_op jit(solution)/shard_map/concatenate | solution.py:271
  1125.4 8.1 fusion.60
  1133.5 27.1 fusion.70
  1166.5 1553.7 %reduce-scatter.8.cloned.1.call-done = f32[64,24576]{1,0:T(8,128)} async-done(((f32[2048,24576]{1,0:T(8,128)}), f32[64,24576]{1,0:T(8,128)}) %reduce-scatter.8.cloned.1.call-update) | async-done | bytes 6291472 | tf_op jit(solution)/shard_map/reduce_scatter | solution.py:270
  2722.1 2.7 slice.124
  2724.7 4.6 fusion.104
  (183 shorter events, 57.6 us)
Async XLA Ops:
  7.2 162.8 %all-gather.9.cloned.1.call-start = ((), (), s32[]{:S(2)}) async-start(), calls=%async_computation.3 | async-start | bytes 25952256 | tf_op jit(solution)/shard_map/all_gather | solution.py:89
  7.9 240.7 %all-gather.15.cloned.1.call-start = ((), (), s32[]{:S(2)}) async-start(), calls=%async_computation.6 | async-start | bytes 8650752 | tf_op jit(solution)/shard_map/all_gather | solution.py:152
  8.7 275.2 %all-gather.11.cloned.1.call-start = ((), (), s32[]{:S(2)}) async-start(), calls=%async_computation.4 | async-start | bytes 5242880 | tf_op jit(solution)/shard_map/all_gather | solution.py:110
  57.1 125.0 %copy-start.15 = (f32[2048]{0:T(1024)}, f32[2048]{0:T(1024)S(1)}, u32[]{:S(2)}) copy-start(f32[2048]{0:T(1024)S(1)} %convert_element_type.122) | copy-start | bytes 24580
  57.1 125.0 %copy-start.18 = (f32[2048]{0:T(1024)}, f32[2048]{0:T(1024)S(1)}, u32[]{:S(2)}) copy-start(f32[2048]{0:T(1024)S(1)} %convert_element_type.123) | copy-start | bytes 24580
  58.6 123.5 %copy-start.20 = (f32[256]{0:T(256)}, f32[256]{0:T(256)S(1)}, u32[]{:S(2)}) copy-start(f32[256]{0:T(256)S(1)} %broadcast_multiply_fusion.3) | copy-start | bytes 3076
  60.2 121.9 %copy-start.26 = (f32[256]{0:T(256)}, f32[256]{0:T(256)S(1)}, u32[]{:S(2)}) copy-start(f32[256]{0:T(256)S(1)} %add_rsqrt_fusion) | copy-start | bytes 3076
  60.2 125.7 %copy-start.30 = (s32[1,256]{1,0:T(1,128)S(1)}, s32[1,256]{1,0:T(1,128)}, u32[]{:S(2)}) copy-start(s32[1,256]{1,0:T(1,128)} %param.30) | copy-start | bytes 3076
  182.1 2.7 copy-start.10
  185.9 135.0 %all-gather.13.cloned.1.call-start = ((), (), s32[]{:S(2)}) async-start(), calls=%async_computation.5 | async-start | bytes 5242880 | tf_op jit(solution)/shard_map/all_gather | solution.py:109
  186.1 12.4 copy-start.22
  186.1 12.4 copy-start.24
  192.8 1.5 copy-start.5
  196.2 4.0 copy-start.4
  196.3 2.7 copy-start.6
  196.3 4.0 copy-start.17
  199.0 2.5 copy-start.31
  199.0 49.6 %copy-start.7 = (bf16[1,256,2048]{2,1,0:T(8,128)(2,1)S(1)}, bf16[1,256,2048]{2,1,0:T(8,128)(2,1)}, u32[]{:S(2)}) copy-start(bf16[1,256,2048]{2,1,0:T(8,128)(2,1)} %param.31) | copy-start | bytes 3145732
  201.4 313.2 %reduce-scatter.4.cloned.1.call-start = ((), (), s32[]{:S(2)}) async-start(), calls=%async_computation.9 | async-start | bytes 5242880 | tf_op jit(solution)/shard_map/reduce_scatter | solution.py:213
  357.1 149.4 %copy-start.2 = (bf16[4,256,8,64]{1,3,2,0:T(8,128)(2,1)}, bf16[4,256,8,64]{1,3,2,0:T(8,128)(2,1)S(1)}, u32[]{:S(2)}) copy-start(bf16[4,256,8,64]{1,3,2,0:T(8,128)(2,1)S(1)} %get-tuple-element.104) | copy-start | bytes 3145732
  370.2 3.6 copy-start.11
  374.7 1.9 copy-start.12
  389.7 3.6 copy-start.11
  394.2 1.9 copy-start.12
  409.2 3.6 copy-start.11
  413.7 1.9 copy-start.12
  428.7 3.6 copy-start.11
  433.1 1.9 copy-start.12
  435.1 2.2 copy-start.32
  435.1 71.4 %copy-start.8 = (bf16[1,256,2048]{2,1,0:T(8,128)(2,1)S(1)}, bf16[1,256,2048]{2,1,0:T(8,128)(2,1)}, u32[]{:S(2)}) copy-start(bf16[1,256,2048]{2,1,0:T(8,128)(2,1)} %param.31) | copy-start | bytes 3145732
  435.1 91.8 %reduce-scatter.6.cloned.1.call-start = ((), (), s32[]{:S(2)}) async-start(), calls=%async_computation.10 | async-start | bytes 5242880 | tf_op jit(solution)/shard_map/reduce_scatter | solution.py:219
  435.7 289.1 %all-gather.17.cloned.1.call-start = ((), (), s32[]{:S(2)}) async-start(), calls=%async_computation.7 | async-start | bytes 34603008 | tf_op jit(solution)/shard_map/all_gather | solution.py:90
  436.5 484.3 %all-gather.19.cloned.1.call-start = ((), (), s32[]{:S(2)}) async-start(), calls=%async_computation.8 | async-start | bytes 34603008 | tf_op jit(solution)/shard_map/all_gather | solution.py:153
  437.2 723.4 %all-reduce.14.cloned.1.call-start = ((), (), s32[]{:S(2)}) async-start(), calls=%async_computation.12 | async-start | bytes 163840
  506.5 9.2 copy-start.25
  515.7 2.1 copy-start.13
  515.7 2.3 copy-start.14
  515.7 2.3 copy-start.23
  518.7 8.2 copy-start.9
  529.5 13.7 copy-start
  529.5 13.7 copy-start.16
  529.5 13.7 copy-start.19
  529.5 13.7 copy-start.21
  529.5 13.7 copy-start.27
  991.8 1728.4 %reduce-scatter.8.cloned.1.call-start = ((), (), s32[]{:S(2)}) async-start(), calls=%async_computation.11 | async-start | bytes 207618048 | tf_op jit(solution)/shard_map/reduce_scatter | solution.py:270
  1123.9 0.7 copy-start.29
  1123.9 0.7 copy-start.28
  1123.9 1.2 copy-start.1
  1123.9 1.5 copy-start.3
  1161.3 1568.0 %copy-start.33 = (f32[64]{0:T(128)}, f32[64]{0:T(128)S(1)}, u32[]{:S(2)}) copy-start(f32[64]{0:T(128)S(1)} %dynamic-slice.1) | copy-start | bytes 772
Sparse Core Ops, SparseCore 0:
  10.9 159.0 all-gather.8
  173.0 75.5 all-gather.14
  250.7 33.0 all-gather.10
  285.8 35.0 all-gather.12
  435.2 44.5 reduce-scatter.3
  482.3 44.5 reduce-scatter.5
  529.9 194.8 all-gather.16
  727.7 192.9 all-gather.18
  991.9 120.6 all-reduce.13
  1124.1 1596.0 reduce-scatter.7
where the time goes:
time: 2750 us; the launch traced here: 2740 us
  waiting for transfers between devices  2090 us (76%)
  matrix products  293 us (11%)
  other arithmetic  172 us (6%)
  blocking collectives  117 us (4%)
  local copies, waits for them, and re-layouts  54.7 us (2%)
    reduce_scatter x1, waiting for transfers between devices, body(): lax.psum_scatter(jnp.concatenate([inner_part, outer_part], 1), ('seq', 'd...  1550 us
    all_gather x1, waiting for transfers between devices, body(): lax.all_gather(up_weight, ('seq', 'dp'), axis=0, tiled=True)  162 us
    all_gather x1, waiting for transfers between devices, body(): lax.all_gather(down_weight, ('seq', 'dp'), axis=0, tiled=True)  150 us
    concatenate x1, other arithmetic, body(): jnp.concatenate([inner_part, outer_part], 1)  132 us
    all_gather x1, waiting for transfers between devices, body(): lax.all_gather(joint_weight, ('seq', 'dp'), axis=0, tiled=True)  110 us
    dot_general x4, matrix products, trans_dot(): lax.dot_general(left, right, (((0,), (0,)), ((), ())), preferred_element_...  81.4 us
    all_gather x1, blocking collectives, body(): lax.all_gather(up_bias, ('seq', 'dp'), axis=0, tiled=True)  67.9 us
    dot_general x4, matrix products, right_dot(): lax.dot_general(left, right, (((1,), (1,)), ((), ())), preferred_element_...  65.4 us
  transfers between devices with their start and end apart: 10, of which 8 were waited for; matrix products, arithmetic and copies ran while one was open for 12% of the time, Pallas kernels for 0%

commit v1 on v0

v1 whole, which is shorter than its diff:
```python
import functools

import jax
import jax.numpy as jnp
from jax import lax
from jax.experimental import pallas as pl
from jax.experimental.pallas import tpu as pltpu
from jax.sharding import Mesh
from jax.sharding import PartitionSpec as P

ALL = ("x", "c", "zh", "zl", "y")
H = 32
HD = 64
ROT = 32
PAIR = 2 * HD
NEG_FILL = -1e30
NORM_EPS = 1e-05
F32 = jnp.float32
BF16 = jnp.bfloat16


def dot(left, right, left_dim, right_dim):
    return lax.dot_general(
        left, right, (((left_dim,), (right_dim,)), ((), ())), preferred_element_type=F32
    )


def swap(value, axis):
    return lax.ppermute(value, axis, [(0, 1), (1, 0)])


def in_order(own, other, place, dim):
    return jnp.where(
        place == 0, jnp.stack([own, other], dim), jnp.stack([other, own], dim)
    )


def pick(value, place, dim):
    return lax.dynamic_index_in_dim(value, place, dim, keepdims=False)


def exchange(value, axes_dims):
    for axis, dim in axes_dims:
        place = lax.axis_index(axis)
        other = swap(pick(value, 1 - place, dim), axis)
        value = in_order(pick(value, place, dim), other, place, dim)
    return value


TEAM = (("c", 1), ("x", 0), ("zl", 2))


def team_gather(value):
    value = jnp.stack([value, swap(value, "zl")])
    value = jnp.stack([value, swap(value, "x")])
    return jnp.stack([value, swap(value, "c")])


def team_sum(value):
    for axis in ("c", "x", "zl"):
        other = swap(value[1].astype(BF16), axis)
        value = value[0].astype(F32) + other.astype(F32)
    return value


def rows_gather(value, mesh):
    place = lax.axis_index("zh")
    value = in_order(value, swap(value, "zh"), place, 2)
    if mesh.shape["y"] == 2:
        return in_order(value, swap(value, "y"), lax.axis_index("y"), 4)
    return lax.all_gather(value, "y", axis=4)


def rows_sum(value, mesh):
    if mesh.shape["y"] == 2:
        place = lax.axis_index("y")
        other = swap(pick(value, 1 - place, 4).astype(BF16), "y")
        value = pick(value, place, 4).astype(F32) + other.astype(F32)
    else:
        value = lax.psum_scatter(value.astype(BF16), "y", scatter_dimension=4).astype(F32)
    place = lax.axis_index("zh")
    other = swap(pick(value, 1 - place, 2).astype(BF16), "zh")
    return pick(value, place, 2).astype(F32) + other.astype(F32)


def turn(value, cosine, sine, lane, sign):
    half = ROT // 2
    width = value.shape[-1]
    up = pltpu.roll(value, width - half, 1)
    down = pltpu.roll(value, half, 1)
    turned = jnp.where(lane < half, -up, down)
    return value * cosine + (sign * turned) * sine


def attend_kernel(
    order, q_ref, k_ref, v_ref, do_ref, cos_ref, sin_ref, segc_ref, segr_ref,
    out_ref, grad_ref, qs, ks, vs, ds, kt, vt, segc, segr, dq, dk, dv,
):
    rows = q_ref.shape[2]
    blocks = q_ref.shape[0]
    pair = pl.program_id(1)
    scale = HD ** (-0.5)
    lane = lax.broadcasted_iota(jnp.int32, (rows, PAIR), 1) % HD

    def place(block):
        return pl.ds(pl.multiple_of(order[block] * rows, rows), rows)

    for block in range(blocks):
        at = place(block)
        cosine, sine = cos_ref[block, 0], sin_ref[block, 0]
        query = turn(q_ref[block, 0], cosine, sine, lane, 1.0).astype(BF16)
        qs[at, :] = query * jnp.asarray(scale, BF16)
        key = turn(k_ref[block, 0], cosine, sine, lane, 1.0)
        ks[at, :] = key.astype(BF16)
        kt[:, at] = key.T.astype(BF16)
        value = v_ref[block, 0]
        vs[at, :] = value.astype(BF16)
        vt[:, at] = value.T.astype(BF16)
        ds[at, :] = do_ref[block, 0]
        segc[at, :] = segc_ref[block, 0]
        segr[:, at] = segr_ref[block, 0]
    dk[...] = jnp.zeros_like(dk)
    dv[...] = jnp.zeros_like(dv)
    side = lax.broadcasted_iota(jnp.int32, (rows, PAIR), 1) // HD
    causal = lax.broadcasted_iota(jnp.int32, (rows, rows), 0) <= lax.broadcasted_iota(
        jnp.int32, (rows, rows), 1
    )
    for block in range(blocks):
        here = slice(block * rows, (block + 1) * rows)
        count = (block + 1) * rows
        same = segc[:count, :1] == segr[:1, here]
        if block == 0:
            allowed = same & causal
        else:
            allowed = jnp.concatenate([same[: count - rows], same[count - rows :] & causal], 0)
        query, grad = qs[here, :], ds[here, :]
        tops = []
        turns = []
        for head in range(2):
            lanes = slice(head * HD, (head + 1) * HD)
            query_one = jnp.where(side == head, query, jnp.zeros_like(query))
            grad_one = jnp.where(side == head, grad, jnp.zeros_like(grad))
            scores = dot(ks[:count, :], query_one, 1, 1)
            scores = jnp.where(allowed, scores, NEG_FILL)
            exps = jnp.exp(scores - jnp.max(scores, 0, keepdims=True))
            probs = exps * (1.0 / jnp.sum(exps, 0, keepdims=True))
            probs_low = probs.astype(BF16)
            tops.append(dot(vt[lanes, :count], probs_low, 1, 0))
            dv[:count, :] += dot(probs_low, grad_one, 1, 0)
            probs_grad = dot(vs[:count, :], grad_one, 1, 1)
            inner = jnp.sum(probs * probs_grad, 0, keepdims=True)
            score_grad = (probs * (probs_grad - inner)).astype(BF16)
            dk[:count, :] += dot(score_grad, query_one, 1, 0)
            turns.append(dot(kt[lanes, :count], score_grad, 1, 0))
        ds[here, :] = jnp.concatenate(tops, 0).T.astype(BF16)
        dq[here, :] = (jnp.concatenate(turns, 0) * scale).T
    for block in range(blocks):
        at = place(block)
        cosine, sine = cos_ref[block, 0], sin_ref[block, 0]
        out_ref[block, 0] = ds[at, :]
        for part, source in enumerate((dq, dk)):
            spot = pl.ds(pl.multiple_of(part * 2 * PAIR + pair * PAIR, PAIR), PAIR)
            grad_ref[block, 0, :, spot] = turn(source[at, :], cosine, sine, lane, -1.0).astype(BF16)
        spot = pl.ds(pl.multiple_of(4 * PAIR + pair * PAIR, PAIR), PAIR)
        grad_ref[block, 0, :, spot] = dv[at, :].astype(BF16)


def attend(order, joint, grad, cosine, sine, segc, segr):
    blocks, seqs, rows, width = joint.shape
    span = blocks * rows
    third = width // 3

    def part(first):
        return pl.BlockSpec((blocks, 1, rows, PAIR), lambda s, p, o: (0, s, 0, first + p))

    def table(height, wide):
        return pl.BlockSpec((blocks, 1, height, wide), lambda s, p, o: (0, s, 0, 0))

    return pl.pallas_call(
        attend_kernel,
        grid_spec=pltpu.PrefetchScalarGridSpec(
            num_scalar_prefetch=1,
            grid=(seqs, third // PAIR),
            in_specs=[
                part(0),
                part(third // PAIR),
                part(2 * third // PAIR),
                part(0),
                table(rows, PAIR),
                table(rows, PAIR),
                table(rows, PAIR),
                table(8, rows),
            ],
            out_specs=[part(0), table(rows, width)],
            scratch_shapes=[
                pltpu.VMEM((span, PAIR), BF16),
                pltpu.VMEM((span, PAIR), BF16),
                pltpu.VMEM((span, PAIR), BF16),
                pltpu.VMEM((span, PAIR), BF16),
                pltpu.VMEM((PAIR, span), BF16),
                pltpu.VMEM((PAIR, span), BF16),
                pltpu.VMEM((span, PAIR), jnp.int32),
                pltpu.VMEM((8, span), jnp.int32),
                pltpu.VMEM((span, PAIR), F32),
                pltpu.VMEM((span, PAIR), F32),
                pltpu.VMEM((span, PAIR), F32),
            ],
        ),
        out_shape=[
            jax.ShapeDtypeStruct((blocks, seqs, rows, third), BF16),
            jax.ShapeDtypeStruct((blocks, seqs, rows, width), BF16),
        ],
        compiler_params=pltpu.CompilerParams(vmem_limit_bytes=48 * 1024 * 1024),
        cost_estimate=pl.CostEstimate(
            flops=20_000_000_000, bytes_accessed=20_000_000, transcendentals=5_000_000
        ),
    )(order, joint, joint, joint, grad, cosine, sine, segc, segr)


def gelu_tanh(inputs):
    return jax.nn.gelu(inputs, approximate=True)


def body(
    mesh,
    tokens,
    joint_weight,
    output_weight,
    up_weight,
    down_weight,
    joint_bias,
    output_bias,
    up_bias,
    down_bias,
    norm_gain,
    norm_shift,
    segments,
    positions,
    cotangent,
):
    rows, width = tokens.shape[1], tokens.shape[2]
    hidden_width = up_weight.shape[1]
    own_rows = joint_weight.shape[0]
    devices = mesh.size
    ix, ic, izl = lax.axis_index("x"), lax.axis_index("c"), lax.axis_index("zl")
    count = 8 * rows
    heads_wide = width // 8
    units = hidden_width // 8
    own_tokens = tokens.reshape(rows, width)
    own_grad = cotangent.reshape(rows, width)

    sizes = [v.shape[0] for v in (joint_bias, up_bias, output_bias, down_bias, norm_gain, norm_shift)]
    small = lax.all_gather(
        jnp.concatenate([joint_bias, up_bias, output_bias, down_bias, norm_gain, norm_shift]), ALL
    )
    cuts = [sum(sizes[:i]) for i in range(len(sizes) + 1)]
    joint_full, up_full, output_full, down_full, gain_full, shift_full = (
        small[:, cuts[i] : cuts[i + 1]].reshape(-1).astype(F32) for i in range(6)
    )

    tokens_all = team_gather(own_tokens).reshape(count, width)
    grad_all = team_gather(own_grad).reshape(count, width)
    marks = team_gather(jnp.stack([segments.reshape(rows), positions.reshape(rows)]))

    def columns(weight):
        return weight.reshape(own_rows, 2, 2, 2, units).transpose(1, 2, 3, 0, 4)

    joint_cols = (
        joint_weight.reshape(own_rows, 3, 2, 2, 2, 2, PAIR)
        .transpose(2, 3, 5, 0, 1, 4, 6)
        .reshape(2, 2, 2, own_rows, 3 * heads_wide)
    )
    up_mine = rows_gather(exchange(columns(up_weight), TEAM), mesh).reshape(width, units)
    down_mine = rows_gather(exchange(columns(down_weight), TEAM), mesh).reshape(width, units)
    joint_mine = rows_gather(exchange(joint_cols, TEAM), mesh).reshape(width, 3 * heads_wide)
    output_mine = rows_gather(
        output_weight.reshape(1, 1, 1, own_rows, width), mesh
    ).reshape(heads_wide, width)

    joint_bias_mine = pick(
        pick(pick(joint_full.reshape(3, 2, 2, 2, 2, PAIR), ix, 1), ic, 1), izl, 2
    ).reshape(3 * heads_wide)
    up_bias_mine = pick(up_full.reshape(8, units), (ix * 2 + ic) * 2 + izl, 0)

    wide = tokens_all.astype(F32)
    centered = wide - jnp.mean(wide, 1, keepdims=True)
    inv_std = lax.rsqrt(jnp.mean(centered * centered, 1, keepdims=True) + NORM_EPS)
    normed = (centered * inv_std * gain_full + shift_full).astype(BF16)

    up_pre = dot(normed, up_mine, 1, 0) + up_bias_mine
    hidden_low = gelu_tanh(up_pre).astype(BF16)
    hidden_grad = dot(grad_all, down_mine, 1, 0)
    up_grad_low = jax.vjp(gelu_tanh, up_pre)[1](hidden_grad)[0].astype(BF16)

    joint_out = dot(normed, joint_mine, 1, 0) + joint_bias_mine
    attended_grad = dot(grad_all, output_mine, 1, 1).astype(BF16)

    marks = marks.reshape(4, 2, 2, rows)
    seg, pos = marks[:, :, 0], marks[:, :, 1]
    frequency = 10000.0 ** (-jnp.arange(0, ROT, 2, dtype=F32) / ROT)
    angles = pos.astype(F32)[..., None] * frequency
    angles = jnp.concatenate([angles, angles], -1)
    rest = angles.shape[:-1] + (HD - ROT,)
    cosine = jnp.concatenate([jnp.cos(angles), jnp.ones(rest, F32)] * 2, -1)
    sine = jnp.concatenate([jnp.sin(angles), jnp.zeros(rest, F32)] * 2, -1)
    segc = jnp.broadcast_to(seg[..., None], seg.shape + (PAIR,))
    segr = jnp.broadcast_to(seg[:, :, None], (4, 2, 8, rows))
    rel = jnp.arange(4, dtype=jnp.int32)
    order = 2 * ((rel % 2) ^ ix) + ((rel // 2) ^ ic)
    attended_low, joint_grad_low = attend(
        order.astype(jnp.int32),
        joint_out.reshape(4, 2, rows, 3 * heads_wide),
        attended_grad.reshape(4, 2, rows, heads_wide),
        cosine,
        sine,
        segc,
        segr,
    )
    attended_low = attended_low.reshape(count, heads_wide)
    joint_grad_low = joint_grad_low.reshape(count, 3 * heads_wide)

    shape = (2, 2, 2, rows, width)
    branch = dot(hidden_low, down_mine, 1, 1) + dot(attended_low, output_mine, 1, 0)
    layer_sum = team_sum(branch.astype(BF16).reshape(shape))
    layer_out = (own_tokens.astype(F32) + output_full + down_full + layer_sum).astype(BF16)
    back = dot(joint_grad_low, joint_mine, 1, 1) + dot(up_grad_low, up_mine, 1, 1)
    produced = team_sum(back.astype(BF16).reshape(shape))

    own_wide = own_tokens.astype(F32)
    own_centered = own_wide - jnp.mean(own_wide, 1, keepdims=True)
    own_inv = lax.rsqrt(jnp.mean(own_centered * own_centered, 1, keepdims=True) + NORM_EPS)
    normalized = own_centered * own_inv
    scaled = produced * gain_full
    tokens_grad = own_grad.astype(F32) + own_inv * (
        scaled
        - jnp.mean(scaled, 1, keepdims=True)
        - normalized * jnp.mean(scaled * normalized, 1, keepdims=True)
    )
    tokens_grad = tokens_grad.astype(BF16)

    rows_shape = (2, 2, 2, 2, mesh.shape["y"], own_rows)

    def to_owner(partial):
        summed = rows_sum(partial.reshape(rows_shape + (partial.shape[1],)), mesh)
        return exchange(summed.astype(BF16), TEAM).astype(F32)

    def uncolumns(value):
        return value.transpose(3, 0, 1, 2, 4).reshape(own_rows, hidden_width)

    up_weight_grad = uncolumns(to_owner(dot(normed, up_grad_low, 0, 0)))
    down_weight_grad = uncolumns(to_owner(dot(grad_all, hidden_low, 0, 0)))
    joint_weight_grad = (
        to_owner(dot(normed, joint_grad_low, 0, 0))
        .reshape(2, 2, 2, own_rows, 3, 2, PAIR)
        .transpose(3, 4, 0, 1, 5, 2, 6)
        .reshape(own_rows, 3 * width)
    )
    output_weight_grad = rows_sum(
        dot(attended_low, grad_all, 0, 0).reshape(1, 1, 2, 1, mesh.shape["y"], own_rows, width), mesh
    ).reshape(own_rows, width)

    joint_sum = jnp.sum(joint_grad_low.astype(F32), 0).reshape(3, 1, 1, 2, 1, PAIR)
    joint_sum = lax.dynamic_update_slice(
        jnp.zeros((3, 2, 2, 2, 2, PAIR), F32), joint_sum, (0, ix, ic, 0, izl, 0)
    )
    up_sum = lax.dynamic_update_slice(
        jnp.zeros((8, units), F32),
        jnp.sum(up_grad_low.astype(F32), 0)[None],
        ((ix * 2 + ic) * 2 + izl, 0),
    )
    sums = [
        joint_sum,
        up_sum,
        jnp.sum(own_grad.astype(F32), 0),
        jnp.sum(produced * normalized, 0),
        jnp.sum(produced, 0),
    ]
    sums = jnp.concatenate([v.reshape(devices, -1) for v in sums], 1)
    sums = lax.psum_scatter(sums, ALL, scatter_dimension=0)
    joint_bias_grad = sums[: cuts[1]]
    up_bias_grad = sums[cuts[1] : cuts[2]]
    grad_total, norm_gain_grad, norm_shift_grad = (
        sums[cuts[2] + i * own_rows : cuts[2] + (i + 1) * own_rows] for i in range(3)
    )
    return (
        layer_out.reshape(1, rows, width),
        tokens_grad.reshape(1, rows, width),
        joint_weight_grad,
        output_weight_grad,
        up_weight_grad,
        down_weight_grad,
        joint_bias_grad,
        grad_total,
        up_bias_grad,
        grad_total,
        norm_gain_grad,
        norm_shift_grad,
    )


def solution(mesh):
    seq, dp = mesh.shape["seq"], mesh.shape["dp"]
    fine = Mesh(mesh.devices.reshape(2, seq // 2, 2, 2, dp // 4), ALL)
    row = P(ALL, None)
    one = P(ALL)
    dp_axes, seq_axes = ("zh", "zl", "y"), ("x", "c")
    token = P(dp_axes, seq_axes, None)
    mark = P(dp_axes, seq_axes)
    return jax.shard_map(
        functools.partial(body, fine),
        mesh=fine,
        in_specs=(token,) + (row,) * 4 + (one,) * 6 + (mark, mark, token),
        out_specs=(token, token) + (row,) * 4 + (one,) * 6,
        check_vma=False,
    )
```

time: 2750 us -> 1140 us (0.41)
  waiting for transfers between devices: 2090 us -> 639 us
  matrix products: 293 us -> 137 us
  blocking collectives: 117 us -> 42.5 us
  other arithmetic: 172 us -> 107 us
  local copies, waits for them, and re-layouts: 54.7 us -> 119 us
  starting transfers between devices: 0.4 us -> 40.4 us
  Pallas kernels: 0 us -> 35.3 us
    reduce_scatter x3 -> x0, waiting for transfers between devices: 1560 us -> none  [the longest x1 1550 us: body(): lax.psum_scatter(jnp.concatenate([inner_part, outer_part], 1), ('seq', 'd...]
    ppermute x0 -> x49, waiting for transfers between devices: none -> 543 us  [swap(): return lax.ppermute(value, axis, [(0, 1), (1, 0)])]
    all_gather x6 -> x0, waiting for transfers between devices: 520 us -> none  [the longest x1 162 us: body(): lax.all_gather(up_weight, ('seq', 'dp'), axis=0, tiled=True)]
    dot_general x40 -> x12, matrix products: 293 us -> 137 us  [dot(): lax.dot_general(left, right, (((left_dim,), (right_dim,)), ((), ())), pre...]
    concatenate x4 -> x2, other arithmetic: 133 us -> 1.75 us  [the longest x1 0.88 us: body(): sine = jnp.concatenate([jnp.sin(angles), jnp.zeros(rest, F32)] * 2, -1)]
    unnamed x11 -> x2, waiting for transfers between devices: 3.37 us -> 96.2 us
    all_gather x2 -> x0, blocking collectives: 72.9 us -> none  [the longest x1 67.9 us: body(): lax.all_gather(up_bias, ('seq', 'dp'), axis=0, tiled=True)]
    ppermute x0 -> x49, starting transfers between devices: none -> 40.4 us  [swap(): return lax.ppermute(value, axis, [(0, 1), (1, 0)])]
  transfers between devices with their start and end apart: 10 -> 50, of which waited for: 8 -> 20; matrix products, arithmetic and copies ran while one was open for 12% -> 22% of each run, Pallas kernels for 0% -> 0%
where the time goes in v1:
time: 1140 us
  waiting for transfers between devices  639 us (56%)
  matrix products  137 us (12%)
  local copies, waits for them, and re-layouts  119 us (10%)
  other arithmetic  107 us (9%)
  blocking collectives  42.5 us (4%)
  starting transfers between devices  40.4 us (4%)
  Pallas kernels  35.3 us (3%)
  between operations  15.7 us (1%)
    ppermute x49, waiting for transfers between devices, swap(): return lax.ppermute(value, axis, [(0, 1), (1, 0)])  543 us
    dot_general x12, matrix products, dot(): lax.dot_general(left, right, (((left_dim,), (right_dim,)), ((), ())), pre...  137 us
    unnamed x2, waiting for transfers between devices  96.2 us
    unnamed x1, blocking collectives  42.5 us
    ppermute x49, starting transfers between devices, swap(): return lax.ppermute(value, axis, [(0, 1), (1, 0)])  40.4 us
    pallas_call x1, Pallas kernels, attend(): pl.pallas_call(attend_kernel, grid_spec=pltpu.PrefetchScalarGridSpec(num_...  35.3 us
    select_n x29, other arithmetic, in_order(): jnp.where(place == 0, jnp.stack([own, other], dim), jnp.stack([other, own...  28.8 us
    dot_general x3, local copies, waits for them, and re-layouts, dot(): lax.dot_general(left, right, (((left_dim,), (right_dim,)), ((), ())), pre...  25.2 us
  transfers between devices with their start and end apart: 50, of which 20 were waited for; matrix products, arithmetic and copies ran while one was open for 22% of the time, Pallas kernels for 0%

profile of v1, /device:TPU:0, one launch (start us, length us, event | category | flops | bytes accessed | tf_op | source)
XLA Modules:
  0.0 1135.9 jit_solution(8415112254718789333)
XLA Ops:
  8.0 3.0 collective-permute-start.23
  11.0 2.6 reshape.1325
  22.5 4.1 concatenate.223
  26.8 42.5 %all-reduce = bf16[22528]{0:T(1024)(128)(2,1)S(1)} all-reduce(bf16[22528]{0:T(1024)(128)(2,1)S(1)} %dynamic-update-slice), channel_id=2, replica_groups=mesh['x'=2,'c'=2,'zh'=2,'zl'=2,'y'=2] {'x','c','zh','zl','y'}, use_global_device_ids=true, to_apply=%add | all-reduce | flops 22528 | bytes 90112
  90.4 3.5 fusion.64
  103.5 5.4 collective-permute-done.4
  111.0 53.7 %collective-permute-done.9 = bf16[2,2,64,1024]{3,2,1,0:T(8,128)(2,1)} collective-permute-done((bf16[2,2,64,1024]{3,2,1,0:T(8,128)(2,1)}, bf16[2,2,64,1024]{3,2,1,0:T(8,128)(2,1)}, u32[]{:S(2)}, u32[]{:S(2)}) %collective-permute-start.9) | collective-permute-done | bytes 524320 | tf_op jit(solution)/shard_map/ppermute | solution.py:29
  173.4 32.0 %collective-permute-done.10 = bf16[2,2,64,1024]{3,2,1,0:T(8,128)(2,1)S(1)} collective-permute-done((bf16[2,2,64,1024]{3,2,1,0:T(8,128)(2,1)S(1)}, bf16[2,2,64,1024]{3,2,1,0:T(8,128)(2,1)S(1)}, u32[]{:S(2)}, u32[]{:S(2)}) %collective-permute-start.10) | collective-permute-done | bytes 524320 | tf_op jit(solution)/shard_map/ppermute | solution.py:29
  206.0 3.0 collective-permute-start.6
  211.4 42.4 %collective-permute-done.16 = bf16[2,2,2,64,768]{4,3,2,1,0:T(8,128)(2,1)S(1)} collective-permute-done((bf16[2,2,2,64,768]{4,3,2,1,0:T(8,128)(2,1)S(1)}, bf16[2,2,2,64,768]{4,3,2,1,0:T(8,128)(2,1)S(1)}, u32[]{:S(2)}, u32[]{:S(2)}) %collective-permute-start.16) | collective-permute-done | bytes 786464 | tf_op jit(solution)/shard_map/ppermute | solution.py:29
  254.0 43.8 %collective-permute-done.6 = bf16[2,2,2,64,1024]{4,3,2,1,0:T(8,128)(2,1)S(1)} collective-permute-done((bf16[2,2,2,64,1024]{4,3,2,1,0:T(8,128)(2,1)S(1)}, bf16[2,2,2,64,1024]{4,3,2,1,0:T(8,128)(2,1)S(1)}, u32[]{:S(2)}, u32[]{:S(2)}) %collective-permute-start.6) | collective-permute-done | bytes 1048608 | tf_op jit(solution)/shard_map/ppermute | solution.py:29
  303.1 4.0 fusion.66
  310.6 24.7 %collective-permute-done.17 = bf16[2,2,2,2,64,768]{5,4,3,1,0,2:T(8,128)(2,1)} collective-permute-done((bf16[2,2,2,2,64,768]{5,4,3,1,0,2:T(8,128)(2,1)S(1)}, bf16[2,2,2,2,64,768]{5,4,3,1,0,2:T(8,128)(2,1)}, u32[]{:S(2)}, u32[]{:S(2)}) %collective-permute-start.17) | collective-permute-done | bytes 1572896 | tf_op jit(solution)/shard_map/ppermute | solution.py:29
  339.6 40.5 %collective-permute-done.7 = bf16[2,2,2,2,64,1024]{5,4,3,1,0,2:T(8,128)(2,1)S(1)} collective-permute-done((bf16[2,2,2,2,64,1024]{5,4,3,1,0,2:T(8,128)(2,1)S(1)}, bf16[2,2,2,2,64,1024]{5,4,3,1,0,2:T(8,128)(2,1)S(1)}, u32[]{:S(2)}, u32[]{:S(2)}) %collective-permute-start.7) | collective-permute-done | bytes 2097184 | tf_op jit(solution)/shard_map/ppermute | solution.py:29
  381.5 3.1 maximum_select_fusion
  384.5 2.5 copy.127
  387.1 36.5 %collective-permute-done.12 = bf16[2,2,2,2,64,1024]{5,4,3,1,0,2:T(8,128)(2,1)} collective-permute-done((bf16[2,2,2,2,64,1024]{5,4,3,1,0,2:T(8,128)(2,1)}, bf16[2,2,2,2,64,1024]{5,4,3,1,0,2:T(8,128)(2,1)}, u32[]{:S(2)}, u32[]{:S(2)}) %collective-permute-start.12) | collective-permute-done | bytes 2097184 | tf_op jit(solution)/shard_map/ppermute | solution.py:29
  423.6 3.0 maximum_select_fusion.1
  431.1 2.7 multiply_reduce_fusion
  433.8 7.5 pad_maximum_fusion.1
  441.3 5.3 add_convert_fusion.2
  446.6 11.0 fusion.73
  457.6 18.9 %fusion.68 = f32[2048,2048]{1,0:T(8,128)} fusion(bf16[2048,1024]{1,0:T(8,128)(2,1)} %bitcast.373, f32[2048,1024]{1,0:T(8,128)} %fusion.73, f32[1024]{0:T(1024)S(1)} %bitcast.408), kind=kOutput, calls=%fused_computation.235 | convolution fusion | flops 8610906112 | bytes 29364224 | tf_op jit(solution)/shard_map/dot_general | solution.py:23
  476.5 17.8 %convert_reduce_fusion.1 = (f32[1024]{0:T(1024)}, bf16[2048,1024]{1,0:T(8,128)(2,1)}) fusion(f32[2048,1024]{1,0:T(8,128)} %fusion.73, f32[1024]{0:T(1024)S(1)} %bitcast.409, bf16[2048,2048]{1,0:T(8,128)(2,1)S(1)} %bitcast.334, bf16[2048,1024]{1,0:T(8,128)(2,1)S(1)} %bitcast.374), kind=kOutput, calls=%fused_computation.23 | convolution fusion | flops 8638168064 | bytes 25174016 | tf_op jit(solution)/shard_map/dot_general | solution.py:23
  494.3 3.5 convolution_convert_fusion
  497.8 7.5 fusion.3
  505.3 12.3 %copy.145 = bf16[2048,2048]{1,0:T(8,128)(2,1)} copy(bf16[2048,2048]{0,1:T(8,128)(2,1)} %bitcast.336) | data formatting | bytes 16777216 | tf_op jit(solution)/shard_map/dot_general | solution.py:23
  517.6 11.7 %broadcast_add_fusion = f32[2048,768]{1,0:T(8,128)} fusion(f32[768]{0:T(1024)S(1)} %add.305, bf16[2048,2048]{1,0:T(8,128)(2,1)} %bitcast.354, bf16[2048,768]{1,0:T(8,128)(2,1)} %bitcast.379), kind=kOutput, calls=%fused_computation.47 | convolution fusion | flops 6444023808 | bytes 17828864 | tf_op jit(solution)/shard_map/dot_general | solution.py:23
  529.7 35.3 %shard_map.229 = (bf16[4,2,256,256]{3,2,1,0:T(8,128)(2,1)S(1)}, bf16[4,2,256,768]{3,2,1,0:T(8,128)(2,1)}) custom-call(s32[4]{0:T(128)S(1)} %fusion.58.order, f32[4,2,256,768]{3,2,1,0:T(8,128)} %bitcast.416, f32[4,2,256,768]{3,2,1,0:T(8,128)} %bitcast.417, f32[4,2,256,768]{3,2,1,0:T(8,128)} %bitcast.418, bf16[4,2,256,256]{3,2,1,0:T(8,128)(2,1)S(1)} %bitcast.325, ...), custom_call_target="tpu_custom_call" | custom-call | flops 20000000000 | bytes 20000000 | tf_op jit(solution)/shard_map/pallas_call | solution.py:179
  565.7 5.9 fusion.76
  573.5 9.4 fusion.75
  583.0 9.1 fusion.15
  598.7 12.3 %copy.149 = bf16[2048,2048]{1,0:T(8,128)(2,1)} copy(bf16[2048,2048]{0,1:T(8,128)(2,1)} %bitcast.331) | data formatting | bytes 16777216 | tf_op jit(solution)/shard_map/dot_general | solution.py:23
  611.0 14.4 %fusion.13 = f32[2,2,2,2,2,64,1024]{6,5,4,3,2,1,0:T(8,128)S(1)} fusion(bf16[2,2,2,2,2,64,2048]{6,5,4,3,2,1,0:T(8,128)(2,1)} %bitcast.355, f32[2048,1024]{1,0:T(8,128)} %fusion.73, f32[1024]{0:T(1024)S(1)} %bitcast.410), kind=kOutput, calls=%fused_computation.37 | convolution fusion | flops 8610906112 | bytes 25169920 | tf_op jit(solution)/shard_map/dot_general | solution.py:23
  625.4 3.2 copy-done.13
  631.2 11.4 %add_convert_fusion.1 = bf16[2048,2048]{1,0:T(8,128)(2,1)} fusion(f32[2048,2048]{1,0:T(8,128)} %fusion.68, bf16[2048,256]{1,0:T(8,128)(2,1)S(1)} %bitcast.324, bf16[256,2048]{1,0:T(8,128)(2,1)S(1)} %bitcast.378), kind=kOutput, calls=%fused_computation.6 | convolution fusion | flops 2155872256 | bytes 27262976 | tf_op jit(solution)/shard_map/dot_general | solution.py:23
  642.6 7.1 fusion.71
  650.8 9.5 fusion.74
  660.4 14.4 %add_convert_fusion = bf16[2048,2048]{1,0:T(8,128)(2,1)S(1)} fusion(f32[2048,2048]{1,0:T(8,128)} %fusion.74, bf16[2048,1024]{1,0:T(8,128)(2,1)} %get-tuple-element.21, bf16[2048,1024]{1,0:T(8,128)(2,1)} %bitcast.371), kind=kOutput, calls=%fused_computation.5 | convolution fusion | flops 8598323200 | bytes 33554432 | tf_op jit(solution)/shard_map/dot_general | solution.py:23
  674.8 3.8 fusion.70
  681.6 2.9 bitcast_add_fusion.2
  684.6 3.0 collective-permute-start.33
  687.6 3.5 bitcast_add_fusion.1
  691.3 27.7 %collective-permute-done.44 = bf16[2,2,2,2,64,1024]{5,4,3,1,0,2:T(8,128)(2,1)} collective-permute-done((bf16[2,2,2,2,64,1024]{5,4,3,1,0,2:T(8,128)(2,1)}, bf16[2,2,2,2,64,1024]{5,4,3,1,0,2:T(8,128)(2,1)}, u32[]{:S(2)}, u32[]{:S(2)}) %collective-permute-start.44) | collective-permute-done | bytes 2097184 | tf_op jit(solution)/shard_map/ppermute | solution.py:29
  719.0 2.6 bitcast_add_fusion
  721.8 30.4 %collective-permute-done.33 = bf16[2,2,2,64,768]{4,3,2,1,0:T(8,128)(2,1)S(1)} collective-permute-done((bf16[2,2,2,64,768]{4,3,2,1,0:T(8,128)(2,1)S(1)}, bf16[2,2,2,64,768]{4,3,2,1,0:T(8,128)(2,1)S(1)}, u32[]{:S(2)}, u32[]{:S(2)}) %collective-permute-start.33) | collective-permute-done | bytes 786464 | tf_op jit(solution)/shard_map/ppermute | solution.py:29
  755.6 41.6 %collective-permute-done.40 = bf16[2,2,2,64,1024]{4,3,2,1,0:T(8,128)(2,1)S(1)} collective-permute-done((bf16[2,2,2,64,1024]{4,3,2,1,0:T(8,128)(2,1)S(1)}, bf16[2,2,2,64,1024]{4,3,2,1,0:T(8,128)(2,1)S(1)}, u32[]{:S(2)}, u32[]{:S(2)}) %collective-permute-start.40) | collective-permute-done | bytes 1048608 | tf_op jit(solution)/shard_map/ppermute | solution.py:29
  799.4 20.3 %collective-permute-done.45 = bf16[2,2,2,64,1024]{4,3,2,1,0:T(8,128)(2,1)S(1)} collective-permute-done((bf16[2,2,2,64,1024]{4,3,2,1,0:T(8,128)(2,1)S(1)}, bf16[2,2,2,64,1024]{4,3,2,1,0:T(8,128)(2,1)S(1)}, u32[]{:S(2)}, u32[]{:S(2)}) %collective-permute-start.45) | collective-permute-done | bytes 1048608 | tf_op jit(solution)/shard_map/ppermute | solution.py:29
  821.1 7.1 collective-permute-done.36
  833.5 4.0 convert_add_fusion
  840.0 2.7 copy-done.7
  842.7 4.0 convert_add_fusion.1
  859.9 87.8 %collective-permute-done.47 = bf16[2,2,64,1024]{3,2,1,0:T(8,128)(2,1)} collective-permute-done((bf16[2,2,64,1024]{3,2,1,0:T(8,128)(2,1)}, bf16[2,2,64,1024]{3,2,1,0:T(8,128)(2,1)}, u32[]{:S(2)}, u32[]{:S(2)}) %collective-permute-start.47) | collective-permute-done | bytes 524320 | tf_op jit(solution)/shard_map/ppermute | solution.py:29
  949.1 3.6 fusion.11
  958.2 20.8 %collective-permute-done.31 = bf16[256,2048]{1,0:T(8,128)(2,1)S(1)} collective-permute-done((bf16[256,2048]{1,0:T(8,128)(2,1)S(1)}, bf16[256,2048]{1,0:T(8,128)(2,1)S(1)}, u32[]{:S(2)}, u32[]{:S(2)}) %collective-permute-start.31) | collective-permute-done | bytes 1048608 | tf_op jit(solution)/shard_map/ppermute | solution.py:29
  980.2 21.3 %collective-permute-done.28 = bf16[256,2048]{1,0:T(8,128)(2,1)S(1)} collective-permute-done((bf16[256,2048]{1,0:T(8,128)(2,1)S(1)}, bf16[256,2048]{1,0:T(8,128)(2,1)S(1)}, u32[]{:S(2)}, u32[]{:S(2)}) %collective-permute-start.28) | collective-permute-done | bytes 1048608 | tf_op jit(solution)/shard_map/ppermute | solution.py:29
  1001.5 4.1 convert_reduce_fusion.4
  1006.5 4.5 collective-permute-done.48
  1011.0 2.7 convert_bitcast_fusion
  1013.8 2.9 copy.148
  1016.7 4.4 reshape.1363
  1021.1 2.9 copy.152
  1024.0 4.0 reshape.1365
  1028.1 96.2 %all-reduce.4.cloned.1.call-done = f32[32,640]{1,0:T(8,128)} async-done(((f32[32,640]{1,0:T(8,128)}), f32[32,640]{1,0:T(8,128)}) %all-reduce.4.cloned.1.call-update) | async-done | bytes 81936
  (333 shorter events, 131.0 us)
Async XLA Ops:
  7.2 1117.1 %all-reduce.4.cloned.1.call-start = ((), (), s32[]{:S(2)}) async-start(), calls=%async_computation | async-start | bytes 163840
  8.0 63.1 %collective-permute-start.23 = (s32[2,256]{1,0:T(2,128)S(1)}, s32[2,256]{1,0:T(2,128)S(1)}, u32[]{:S(2)}, u32[]{:S(2)}) collective-permute-start(s32[2,256]{1,0:T(2,128)S(1)} %get-tuple-element.91), channel_id=1, source_target_pairs={{0,2},{2,0},{1,3},{3,1},{4,6},{6,4},{5,7},{7,5},{8,10},{10,8},{9,1... | collective-permute-start | bytes 6152 | tf_op jit(solution)/shard_map/ppermute | solution.py:29
  15.2 68.2 %collective-permute-start.13 = (bf16[2,2,64,768]{3,2,1,0:T(8,128)(2,1)}, bf16[2,2,64,768]{3,2,1,0:T(8,128)(2,1)}, u32[]{:S(2)}, u32[]{:S(2)}) collective-permute-start(bf16[2,2,64,768]{3,2,1,0:T(8,128)(2,1)} %get-tuple-element.74), channel_id=1, source_target_pairs={{0,8},{8,0},{1,9},{9,1},{2,10},{10,2},{3,11},{11,3},{4,12},{12,4},... | collective-permute-start | bytes 1179656 | tf_op jit(solution)/shard_map/ppermute | solution.py:29
  17.9 69.6 %collective-permute-start.3 = (bf16[2,2,64,1024]{3,2,1,0:T(8,128)(2,1)}, bf16[2,2,64,1024]{3,2,1,0:T(8,128)(2,1)}, u32[]{:S(2)}, u32[]{:S(2)}) collective-permute-start(bf16[2,2,64,1024]{3,2,1,0:T(8,128)(2,1)} %bitcast.321), channel_id=1, source_target_pairs={{0,8},{8,0},{1,9},{9,1},{2,10},{10,2},{3,11},{11,3},{4,12},{12,4},... | collective-permute-start | bytes 1572872 | tf_op jit(solution)/shard_map/ppermute | solution.py:29
  22.2 73.7 %collective-permute-start.8 = (bf16[2,2,64,1024]{3,2,1,0:T(8,128)(2,1)}, bf16[2,2,64,1024]{3,2,1,0:T(8,128)(2,1)}, u32[]{:S(2)}, u32[]{:S(2)}) collective-permute-start(bf16[2,2,64,1024]{3,2,1,0:T(8,128)(2,1)} %bitcast.319), channel_id=1, source_target_pairs={{0,8},{8,0},{1,9},{9,1},{2,10},{10,2},{3,11},{11,3},{4,12},{12,4},... | collective-permute-start | bytes 1572872 | tf_op jit(solution)/shard_map/ppermute | solution.py:29
  22.2 68.2 %collective-permute-start = (bf16[256,2048]{1,0:T(8,128)(2,1)S(1)}, bf16[256,2048]{1,0:T(8,128)(2,1)}, u32[]{:S(2)}, u32[]{:S(2)}) collective-permute-start(bf16[256,2048]{1,0:T(8,128)(2,1)S(1)} %bitcast.337), channel_id=1, source_target_pairs={{0,2},{2,0},{1,3},{3,1},{4,6},{6,4},{5,7},{7,5},{8,10},{10,8},{9,1... | collective-permute-start | bytes 3145736 | tf_op jit(solution)/shard_map/ppermute | solution.py:29
  71.1 3.9 collective-permute-start.24
  75.0 4.2 collective-permute-start.25
  76.0 421.8 %copy-start.31 = (f32[2048]{0:T(1024)}, f32[2048]{0:T(1024)S(1)}, u32[]{:S(2)}) copy-start(f32[2048]{0:T(1024)S(1)} %reshape.1353) | copy-start | bytes 24580
  79.2 87.4 %collective-permute-start.18 = (bf16[256,2048]{1,0:T(8,128)(2,1)}, bf16[256,2048]{1,0:T(8,128)(2,1)}, u32[]{:S(2)}, u32[]{:S(2)}) collective-permute-start(bf16[256,2048]{1,0:T(8,128)(2,1)} %bitcast.57), channel_id=1, source_target_pairs={{0,2},{2,0},{1,3},{3,1},{4,6},{6,4},{5,7},{7,5},{8,10},{10,8},{9,1... | collective-permute-start | bytes 3145736 | tf_op jit(solution)/shard_map/ppermute | solution.py:29
  85.5 15.9 %collective-permute-start.14 = (bf16[2,2,64,768]{3,2,1,0:T(8,128)(2,1)}, bf16[2,2,64,768]{3,2,1,0:T(8,128)(2,1)}, u32[]{:S(2)}, u32[]{:S(2)}) collective-permute-start(bf16[2,2,64,768]{3,2,1,0:T(8,128)(2,1)} %get-tuple-element.72), channel_id=1, source_target_pairs={{0,16},{16,0},{1,17},{17,1},{2,18},{18,2},{3,19},{19,3},{4,20},{20... | collective-permute-start | bytes 1179656 | tf_op jit(solution)/shard_map/ppermute | solution.py:29
  90.4 18.6 %collective-permute-start.4 = (bf16[2,2,64,1024]{3,2,1,0:T(8,128)(2,1)}, bf16[2,2,64,1024]{3,2,1,0:T(8,128)(2,1)}, u32[]{:S(2)}, u32[]{:S(2)}) collective-permute-start(bf16[2,2,64,1024]{3,2,1,0:T(8,128)(2,1)} %get-tuple-element.54), channel_id=1, source_target_pairs={{0,16},{16,0},{1,17},{17,1},{2,18},{18,2},{3,19},{19,3},{4,20},{20... | collective-permute-start | bytes 1572872 | tf_op jit(solution)/shard_map/ppermute | solution.py:29
  93.9 115.1 %collective-permute-start.1 = (bf16[2,256,2048]{2,1,0:T(8,128)(2,1)}, bf16[2,256,2048]{2,1,0:T(8,128)(2,1)}, u32[]{:S(2)}, u32[]{:S(2)}) collective-permute-start(bf16[2,256,2048]{2,1,0:T(8,128)(2,1)} %get-tuple-element.33), channel_id=1, source_target_pairs={{0,16},{16,0},{1,17},{17,1},{2,18},{18,2},{3,19},{19,3},{4,20},{20... | collective-permute-start | bytes 6291464 | tf_op jit(solution)/shard_map/ppermute | solution.py:29
  98.2 66.5 %collective-permute-start.9 = (bf16[2,2,64,1024]{3,2,1,0:T(8,128)(2,1)}, bf16[2,2,64,1024]{3,2,1,0:T(8,128)(2,1)}, u32[]{:S(2)}, u32[]{:S(2)}) collective-permute-start(bf16[2,2,64,1024]{3,2,1,0:T(8,128)(2,1)} %get-tuple-element.60), channel_id=1, source_target_pairs={{0,16},{16,0},{1,17},{17,1},{2,18},{18,2},{3,19},{19,3},{4,20},{20... | collective-permute-start | bytes 1572872 | tf_op jit(solution)/shard_map/ppermute | solution.py:29
  101.4 68.7 %collective-permute-start.21 = (bf16[1,1,1,64,2048]{4,3,2,1,0:T(8,128)(2,1)}, bf16[1,1,1,64,2048]{4,3,2,1,0:T(8,128)(2,1)S(1)}, u32[]{:S(2)}, u32[]{:S(2)}) collective-permute-start(bf16[1,1,1,64,2048]{4,3,2,1,0:T(8,128)(2,1)} %bitcast.393), channel_id=1, source_target_pairs={{0,4},{4,0},{1,5},{5,1},{2,6},{6,2},{3,7},{7,3},{8,12},{12,8},{9,1... | collective-permute-start | bytes 786440 | tf_op jit(solution)/shard_map/ppermute | solution.py:29
  109.0 63.0 %collective-permute-start.15 = (bf16[2,2,64,768]{3,2,1,0:T(8,128)(2,1)S(1)}, bf16[2,2,64,768]{3,2,1,0:T(8,128)(2,1)S(1)}, u32[]{:S(2)}, u32[]{:S(2)}) collective-permute-start(bf16[2,2,64,768]{3,2,1,0:T(8,128)(2,1)S(1)} %get-tuple-element.69), channel_id=1, source_target_pairs={{0,2},{2,0},{1,3},{3,1},{4,6},{6,4},{5,7},{7,5},{8,10},{10,8},{9,1... | collective-permute-start | bytes 1179656 | tf_op jit(solution)/shard_map/ppermute | solution.py:29
  164.7 41.2 %collective-permute-start.5 = (bf16[2,2,64,1024]{3,2,1,0:T(8,128)(2,1)S(1)}, bf16[2,2,64,1024]{3,2,1,0:T(8,128)(2,1)S(1)}, u32[]{:S(2)}, u32[]{:S(2)}) collective-permute-start(bf16[2,2,64,1024]{3,2,1,0:T(8,128)(2,1)S(1)} %get-tuple-element.52), channel_id=1, source_target_pairs={{0,2},{2,0},{1,3},{3,1},{4,6},{6,4},{5,7},{7,5},{8,10},{10,8},{9,1... | collective-permute-start | bytes 1572872 | tf_op jit(solution)/shard_map/ppermute | solution.py:29
  166.7 38.7 %collective-permute-start.10 = (bf16[2,2,64,1024]{3,2,1,0:T(8,128)(2,1)S(1)}, bf16[2,2,64,1024]{3,2,1,0:T(8,128)(2,1)S(1)}, u32[]{:S(2)}, u32[]{:S(2)}) collective-permute-start(bf16[2,2,64,1024]{3,2,1,0:T(8,128)(2,1)S(1)} %get-tuple-element.57), channel_id=1, source_target_pairs={{0,2},{2,0},{1,3},{3,1},{4,6},{6,4},{5,7},{7,5},{8,10},{10,8},{9,1... | collective-permute-start | bytes 1572872 | tf_op jit(solution)/shard_map/ppermute | solution.py:29
  170.1 131.9 %collective-permute-start.19 = (bf16[2,256,2048]{2,1,0:T(8,128)(2,1)S(1)}, bf16[2,256,2048]{2,1,0:T(8,128)(2,1)S(1)}, u32[]{:S(2)}, u32[]{:S(2)}) collective-permute-start(bf16[2,256,2048]{2,1,0:T(8,128)(2,1)S(1)} %get-tuple-element.31), channel_id=1, source_target_pairs={{0,16},{16,0},{1,17},{17,1},{2,18},{18,2},{3,19},{19,3},{4,20},{20... | collective-permute-start | bytes 6291464 | tf_op jit(solution)/shard_map/ppermute | solution.py:29
  171.9 37.1 %copy-start.10 = (bf16[1,2,256,2048]{3,2,1,0:T(8,128)(2,1)S(1)}, bf16[1,2,256,2048]{3,2,1,0:T(8,128)(2,1)}, u32[]{:S(2)}) copy-start(bf16[1,2,256,2048]{3,2,1,0:T(8,128)(2,1)} %get-tuple-element.32) | copy-start | bytes 6291460
  172.2 81.6 %collective-permute-start.16 = (bf16[2,2,2,64,768]{4,3,2,1,0:T(8,128)(2,1)S(1)}, bf16[2,2,2,64,768]{4,3,2,1,0:T(8,128)(2,1)S(1)}, u32[]{:S(2)}, u32[]{:S(2)}) collective-permute-start(bf16[2,2,2,64,768]{4,3,2,1,0:T(8,128)(2,1)S(1)} %maximum_select_fusion.26), channel_id=1, source_target_pairs={{0,4},{4,0},{1,5},{5,1},{2,6},{6,2},{3,7},{7,3},{8,12},{12,8},{9,1... | collective-permute-start | bytes 2359304 | tf_op jit(solution)/shard_map/ppermute | solution.py:29
  205.8 93.6 %collective-permute-start.11 = (bf16[2,2,2,64,1024]{4,3,2,1,0:T(8,128)(2,1)S(1)}, bf16[2,2,2,64,1024]{4,3,2,1,0:T(8,128)(2,1)S(1)}, u32[]{:S(2)}, u32[]{:S(2)}) collective-permute-start(bf16[2,2,2,64,1024]{4,3,2,1,0:T(8,128)(2,1)S(1)} %maximum_select_fusion.15), channel_id=1, source_target_pairs={{0,4},{4,0},{1,5},{5,1},{2,6},{6,2},{3,7},{7,3},{8,12},{12,8},{9,1... | collective-permute-start | bytes 3145736 | tf_op jit(solution)/shard_map/ppermute | solution.py:29
  206.0 91.9 %collective-permute-start.6 = (bf16[2,2,2,64,1024]{4,3,2,1,0:T(8,128)(2,1)S(1)}, bf16[2,2,2,64,1024]{4,3,2,1,0:T(8,128)(2,1)S(1)}, u32[]{:S(2)}, u32[]{:S(2)}) collective-permute-start(bf16[2,2,2,64,1024]{4,3,2,1,0:T(8,128)(2,1)S(1)} %maximum_select_fusion.11), channel_id=1, source_target_pairs={{0,4},{4,0},{1,5},{5,1},{2,6},{6,2},{3,7},{7,3},{8,12},{12,8},{9,1... | collective-permute-start | bytes 3145736 | tf_op jit(solution)/shard_map/ppermute | solution.py:29
  210.8 218.2 %collective-permute-start.2 = (bf16[2,2,256,2048]{3,2,1,0:T(8,128)(2,1)S(1)}, bf16[2,2,256,2048]{3,2,1,0:T(8,128)(2,1)S(1)}, u32[]{:S(2)}, u32[]{:S(2)}) collective-permute-start(bf16[2,2,256,2048]{3,2,1,0:T(8,128)(2,1)S(1)} %get-tuple-element.29), channel_id=1, source_target_pairs={{0,8},{8,0},{1,9},{9,1},{2,10},{10,2},{3,11},{11,3},{4,12},{12,4},... | collective-permute-start | bytes 12582920 | tf_op jit(solution)/shard_map/ppermute | solution.py:29
  253.8 53.4 %collective-permute-start.22 = (bf16[1,1,2,1,64,2048]{5,4,2,3,1,0:T(8,128)(2,1)S(1)}, bf16[1,1,2,1,64,2048]{5,4,2,3,1,0:T(8,128)(2,1)S(1)}, u32[]{:S(2)}, u32[]{:S(2)}) collective-permute-start(bf16[1,1,2,1,64,2048]{5,4,2,3,1,0:T(8,128)(2,1)S(1)} %maximum_select_fusion.30), channel_id=1, source_target_pairs={{0,1},{1,0},{2,3},{3,2},{4,5},{5,4},{6,7},{7,6},{8,9},{9,8},{10,11... | collective-permute-start | bytes 1572872 | tf_op jit(solution)/shard_map/ppermute | solution.py:29
  297.9 37.4 %collective-permute-start.17 = (bf16[2,2,2,2,64,768]{5,4,3,1,0,2:T(8,128)(2,1)S(1)}, bf16[2,2,2,2,64,768]{5,4,3,1,0,2:T(8,128)(2,1)}, u32[]{:S(2)}, u32[]{:S(2)}) collective-permute-start(bf16[2,2,2,2,64,768]{5,4,3,1,0,2:T(8,128)(2,1)S(1)} %maximum_select_fusion.8), channel_id=1, source_target_pairs={{0,1},{1,0},{2,3},{3,2},{4,5},{5,4},{6,7},{7,6},{8,9},{9,8},{10,11... | collective-permute-start | bytes 4718600 | tf_op jit(solution)/shard_map/ppermute | solution.py:29
  299.4 80.8 %collective-permute-start.7 = (bf16[2,2,2,2,64,1024]{5,4,3,1,0,2:T(8,128)(2,1)S(1)}, bf16[2,2,2,2,64,1024]{5,4,3,1,0,2:T(8,128)(2,1)S(1)}, u32[]{:S(2)}, u32[]{:S(2)}) collective-permute-start(bf16[2,2,2,2,64,1024]{5,4,3,1,0,2:T(8,128)(2,1)S(1)} %maximum_select_fusion.4), channel_id=1, source_target_pairs={{0,1},{1,0},{2,3},{3,2},{4,5},{5,4},{6,7},{7,6},{8,9},{9,8},{10,11... | collective-permute-start | bytes 6291464 | tf_op jit(solution)/shard_map/ppermute | solution.py:29
  302.0 121.6 %collective-permute-start.12 = (bf16[2,2,2,2,64,1024]{5,4,3,1,0,2:T(8,128)(2,1)}, bf16[2,2,2,2,64,1024]{5,4,3,1,0,2:T(8,128)(2,1)}, u32[]{:S(2)}, u32[]{:S(2)}) collective-permute-start(bf16[2,2,2,2,64,1024]{5,4,3,1,0,2:T(8,128)(2,1)} %maximum_select_fusion.6), channel_id=1, source_target_pairs={{0,1},{1,0},{2,3},{3,2},{4,5},{5,4},{6,7},{7,6},{8,9},{9,8},{10,11... | collective-permute-start | bytes 6291464 | tf_op jit(solution)/shard_map/ppermute | solution.py:29
  307.2 126.6 %collective-permute-start.20 = (bf16[2,2,256,2048]{3,2,1,0:T(8,128)(2,1)}, bf16[2,2,256,2048]{3,2,1,0:T(8,128)(2,1)}, u32[]{:S(2)}, u32[]{:S(2)}) collective-permute-start(bf16[2,2,256,2048]{3,2,1,0:T(8,128)(2,1)} %get-tuple-element.27), channel_id=1, source_target_pairs={{0,8},{8,0},{1,9},{9,1},{2,10},{10,2},{3,11},{11,3},{4,12},{12,4},... | collective-permute-start | bytes 12582920 | tf_op jit(solution)/shard_map/ppermute | solution.py:29
  446.6 29.9 %slice-start = ((s8[8388608]{0:T(1024)(128)(4,1)}), s8[4194304]{0:T(1024)(128)(4,1)S(1)}, s32[]{:S(2)}) async-start(s8[8388608]{0:T(1024)(128)(4,1)} %bitcast.332), calls=%async_computation.1 | async-start | bytes 8388608
  457.6 18.9 %slice-start.1 = ((s8[8388608]{0:T(1024)(128)(4,1)}), s8[4194304]{0:T(1024)(128)(4,1)S(1)}, s32[]{:S(2)}) async-start(s8[8388608]{0:T(1024)(128)(4,1)} %bitcast.332), calls=%async_computation.2 | async-start | bytes 8388608
  457.6 18.9 %copy-start.16 = (bf16[2,2,2,2,2,64,1024]{6,5,4,3,2,1,0:T(8,128)(2,1)S(1)}, bf16[2,2,2,2,2,64,1024]{6,5,4,3,2,1,0:T(8,128)(2,1)}, u32[]{:S(2)}) copy-start(bf16[2,2,2,2,2,64,1024]{6,5,4,3,2,1,0:T(8,128)(2,1)} %copy.133) | copy-start | bytes 12582916
  571.6 108.0 %collective-permute-start.37 = (bf16[1,1,2,1,64,2048]{5,4,2,3,1,0:T(8,128)(2,1)S(1)}, bf16[1,1,2,1,64,2048]{5,4,2,3,1,0:T(8,128)(2,1)S(1)}, u32[]{:S(2)}, u32[]{:S(2)}) collective-permute-start(bf16[1,1,2,1,64,2048]{5,4,2,3,1,0:T(8,128)(2,1)S(1)} %fusion.48), channel_id=1, source_target_pairs={{0,1},{1,0},{2,3},{3,2},{4,5},{5,4},{6,7},{7,6},{8,9},{9,8},{10,11... | collective-permute-start | bytes 1572872 | tf_op jit(solution)/shard_map/ppermute | solution.py:29
  593.6 88.0 %collective-permute-start.32 = (bf16[2,2,2,2,64,768]{5,4,3,2,1,0:T(8,128)(2,1)}, bf16[2,2,2,2,64,768]{5,4,3,2,1,0:T(8,128)(2,1)}, u32[]{:S(2)}, u32[]{:S(2)}) collective-permute-start(bf16[2,2,2,2,64,768]{5,4,3,2,1,0:T(8,128)(2,1)} %fusion.39), channel_id=1, source_target_pairs={{0,1},{1,0},{2,3},{3,2},{4,5},{5,4},{6,7},{7,6},{8,9},{9,8},{10,11... | collective-permute-start | bytes 4718600 | tf_op jit(solution)/shard_map/ppermute | solution.py:29
  597.5 87.1 %collective-permute-start.39 = (bf16[2,2,2,2,64,1024]{5,4,3,2,1,0:T(8,128)(2,1)}, bf16[2,2,2,2,64,1024]{5,4,3,2,1,0:T(8,128)(2,1)}, u32[]{:S(2)}, u32[]{:S(2)}) collective-permute-start(bf16[2,2,2,2,64,1024]{5,4,3,2,1,0:T(8,128)(2,1)} %fusion.31), channel_id=1, source_target_pairs={{0,1},{1,0},{2,3},{3,2},{4,5},{5,4},{6,7},{7,6},{8,9},{9,8},{10,11... | collective-permute-start | bytes 6291464 | tf_op jit(solution)/shard_map/ppermute | solution.py:29
  630.3 88.7 %collective-permute-start.44 = (bf16[2,2,2,2,64,1024]{5,4,3,1,0,2:T(8,128)(2,1)}, bf16[2,2,2,2,64,1024]{5,4,3,1,0,2:T(8,128)(2,1)}, u32[]{:S(2)}, u32[]{:S(2)}) collective-permute-start(bf16[2,2,2,2,64,1024]{5,4,3,1,0,2:T(8,128)(2,1)} %fusion.32), channel_id=1, source_target_pairs={{0,1},{1,0},{2,3},{3,2},{4,5},{5,4},{6,7},{7,6},{8,9},{9,8},{10,11... | collective-permute-start | bytes 6291464 | tf_op jit(solution)/shard_map/ppermute | solution.py:29
  679.6 160.5 %collective-permute-start.26 = (bf16[2,2,256,2048]{3,2,1,0:T(8,128)(2,1)}, bf16[2,2,256,2048]{3,2,1,0:T(8,128)(2,1)}, u32[]{:S(2)}, u32[]{:S(2)}) collective-permute-start(bf16[2,2,256,2048]{3,2,1,0:T(8,128)(2,1)} %bitcast.375), channel_id=1, source_target_pairs={{0,8},{8,0},{1,9},{9,1},{2,10},{10,2},{3,11},{11,3},{4,12},{12,4},... | collective-permute-start | bytes 12582920 | tf_op jit(solution)/shard_map/ppermute | solution.py:29
  679.6 153.8 %collective-permute-start.29 = (bf16[2,2,256,2048]{3,2,1,0:T(8,128)(2,1)}, bf16[2,2,256,2048]{3,2,1,0:T(8,128)(2,1)}, u32[]{:S(2)}, u32[]{:S(2)}) collective-permute-start(bf16[2,2,256,2048]{3,2,1,0:T(8,128)(2,1)} %bitcast.376), channel_id=1, source_target_pairs={{0,8},{8,0},{1,9},{9,1},{2,10},{10,2},{3,11},{11,3},{4,12},{12,4},... | collective-permute-start | bytes 12582920 | tf_op jit(solution)/shard_map/ppermute | solution.py:29
  681.5 71.0 %collective-permute-start.38 = (bf16[1,1,1,64,2048]{4,3,2,1,0:T(8,128)(2,1)S(1)}, bf16[1,1,1,64,2048]{4,3,2,1,0:T(8,128)(2,1)S(1)}, u32[]{:S(2)}, u32[]{:S(2)}) collective-permute-start(bf16[1,1,1,64,2048]{4,3,2,1,0:T(8,128)(2,1)S(1)} %fusion.51), channel_id=1, source_target_pairs={{0,4},{4,0},{1,5},{5,1},{2,6},{6,2},{3,7},{7,3},{8,12},{12,8},{9,1... | collective-permute-start | bytes 786440 | tf_op jit(solution)/shard_map/ppermute | solution.py:29
  681.6 37.4 %slice-start.6 = ((s8[8388608]{0:T(1024)(128)(4,1)}), s8[4194304]{0:T(1024)(128)(4,1)S(1)}, s32[]{:S(2)}) async-start(s8[8388608]{0:T(1024)(128)(4,1)} %bitcast.364), calls=%async_computation.7 | async-start | bytes 8388608
  684.6 34.4 %slice-start.7 = ((s8[8388608]{0:T(1024)(128)(4,1)}), s8[4194304]{0:T(1024)(128)(4,1)S(1)}, s32[]{:S(2)}) async-start(s8[8388608]{0:T(1024)(128)(4,1)} %bitcast.364), calls=%async_computation.8 | async-start | bytes 8388608
  684.6 67.6 %collective-permute-start.33 = (bf16[2,2,2,64,768]{4,3,2,1,0:T(8,128)(2,1)S(1)}, bf16[2,2,2,64,768]{4,3,2,1,0:T(8,128)(2,1)S(1)}, u32[]{:S(2)}, u32[]{:S(2)}) collective-permute-start(bf16[2,2,2,64,768]{4,3,2,1,0:T(8,128)(2,1)S(1)} %fusion.47), channel_id=1, source_target_pairs={{0,4},{4,0},{1,5},{5,1},{2,6},{6,2},{3,7},{7,3},{8,12},{12,8},{9,1... | collective-permute-start | bytes 2359304 | tf_op jit(solution)/shard_map/ppermute | solution.py:29
  719.0 78.2 %collective-permute-start.40 = (bf16[2,2,2,64,1024]{4,3,2,1,0:T(8,128)(2,1)S(1)}, bf16[2,2,2,64,1024]{4,3,2,1,0:T(8,128)(2,1)S(1)}, u32[]{:S(2)}, u32[]{:S(2)}) collective-permute-start(bf16[2,2,2,64,1024]{4,3,2,1,0:T(8,128)(2,1)S(1)} %fusion.41), channel_id=1, source_target_pairs={{0,4},{4,0},{1,5},{5,1},{2,6},{6,2},{3,7},{7,3},{8,12},{12,8},{9,1... | collective-permute-start | bytes 3145736 | tf_op jit(solution)/shard_map/ppermute | solution.py:29
  752.3 67.4 %collective-permute-start.45 = (bf16[2,2,2,64,1024]{4,3,2,1,0:T(8,128)(2,1)S(1)}, bf16[2,2,2,64,1024]{4,3,2,1,0:T(8,128)(2,1)S(1)}, u32[]{:S(2)}, u32[]{:S(2)}) collective-permute-start(bf16[2,2,2,64,1024]{4,3,2,1,0:T(8,128)(2,1)S(1)} %fusion.42), channel_id=1, source_target_pairs={{0,4},{4,0},{1,5},{5,1},{2,6},{6,2},{3,7},{7,3},{8,12},{12,8},{9,1... | collective-permute-start | bytes 3145736 | tf_op jit(solution)/shard_map/ppermute | solution.py:29
  752.5 1.8 collective-permute-start.34
  754.5 44.0 %collective-permute-start.35 = (bf16[2,2,64,768]{3,2,1,0:T(8,128)(2,1)S(1)}, bf16[2,2,64,768]{3,2,1,0:T(8,128)(2,1)S(1)}, u32[]{:S(2)}, u32[]{:S(2)}) collective-permute-start(bf16[2,2,64,768]{3,2,1,0:T(8,128)(2,1)S(1)} %get-tuple-element.66), channel_id=1, source_target_pairs={{0,16},{16,0},{1,17},{17,1},{2,18},{18,2},{3,19},{19,3},{4,20},{20... | collective-permute-start | bytes 1179656 | tf_op jit(solution)/shard_map/ppermute | solution.py:29
  798.4 31.5 %collective-permute-start.41 = (bf16[2,2,64,1024]{3,2,1,0:T(8,128)(2,1)}, bf16[2,2,64,1024]{3,2,1,0:T(8,128)(2,1)}, u32[]{:S(2)}, u32[]{:S(2)}) collective-permute-start(bf16[2,2,64,1024]{3,2,1,0:T(8,128)(2,1)} %get-tuple-element.48), channel_id=1, source_target_pairs={{0,8},{8,0},{1,9},{9,1},{2,10},{10,2},{3,11},{11,3},{4,12},{12,4},... | collective-permute-start | bytes 1572872 | tf_op jit(solution)/shard_map/ppermute | solution.py:29
  799.4 28.7 %collective-permute-start.36 = (bf16[2,2,64,768]{3,2,1,0:T(8,128)(2,1)}, bf16[2,2,64,768]{3,2,1,0:T(8,128)(2,1)}, u32[]{:S(2)}, u32[]{:S(2)}) collective-permute-start(bf16[2,2,64,768]{3,2,1,0:T(8,128)(2,1)} %get-tuple-element.64), channel_id=1, source_target_pairs={{0,2},{2,0},{1,3},{3,1},{4,6},{6,4},{5,7},{7,5},{8,10},{10,8},{9,1... | collective-permute-start | bytes 1179656 | tf_op jit(solution)/shard_map/ppermute | solution.py:29
  821.0 28.3 %collective-permute-start.46 = (bf16[2,2,64,1024]{3,2,1,0:T(8,128)(2,1)}, bf16[2,2,64,1024]{3,2,1,0:T(8,128)(2,1)}, u32[]{:S(2)}, u32[]{:S(2)}) collective-permute-start(bf16[2,2,64,1024]{3,2,1,0:T(8,128)(2,1)} %get-tuple-element.42), channel_id=1, source_target_pairs={{0,8},{8,0},{1,9},{9,1},{2,10},{10,2},{3,11},{11,3},{4,12},{12,4},... | collective-permute-start | bytes 1572872 | tf_op jit(solution)/shard_map/ppermute | solution.py:29
  832.4 26.0 %collective-permute-start.42 = (bf16[2,2,64,1024]{3,2,1,0:T(8,128)(2,1)}, bf16[2,2,64,1024]{3,2,1,0:T(8,128)(2,1)}, u32[]{:S(2)}, u32[]{:S(2)}) collective-permute-start(bf16[2,2,64,1024]{3,2,1,0:T(8,128)(2,1)} %get-tuple-element.46), channel_id=1, source_target_pairs={{0,16},{16,0},{1,17},{17,1},{2,18},{18,2},{3,19},{19,3},{4,20},{20... | collective-permute-start | bytes 1572872 | tf_op jit(solution)/shard_map/ppermute | solution.py:29
  839.1 110.0 %collective-permute-start.30 = (bf16[2,256,2048]{2,1,0:T(8,128)(2,1)}, bf16[2,256,2048]{2,1,0:T(8,128)(2,1)}, u32[]{:S(2)}, u32[]{:S(2)}) collective-permute-start(bf16[2,256,2048]{2,1,0:T(8,128)(2,1)} %fusion.34), channel_id=1, source_target_pairs={{0,16},{16,0},{1,17},{17,1},{2,18},{18,2},{3,19},{19,3},{4,20},{20... | collective-permute-start | bytes 6291464 | tf_op jit(solution)/shard_map/ppermute | solution.py:29
  848.3 104.6 %collective-permute-start.27 = (bf16[2,256,2048]{2,1,0:T(8,128)(2,1)}, bf16[2,256,2048]{2,1,0:T(8,128)(2,1)}, u32[]{:S(2)}, u32[]{:S(2)}) collective-permute-start(bf16[2,256,2048]{2,1,0:T(8,128)(2,1)} %fusion.33), channel_id=1, source_target_pairs={{0,16},{16,0},{1,17},{17,1},{2,18},{18,2},{3,19},{19,3},{4,20},{20... | collective-permute-start | bytes 6291464 | tf_op jit(solution)/shard_map/ppermute | solution.py:29
  852.3 95.4 %collective-permute-start.47 = (bf16[2,2,64,1024]{3,2,1,0:T(8,128)(2,1)}, bf16[2,2,64,1024]{3,2,1,0:T(8,128)(2,1)}, u32[]{:S(2)}, u32[]{:S(2)}) collective-permute-start(bf16[2,2,64,1024]{3,2,1,0:T(8,128)(2,1)} %get-tuple-element.40), channel_id=1, source_target_pairs={{0,16},{16,0},{1,17},{17,1},{2,18},{18,2},{3,19},{19,3},{4,20},{20... | collective-permute-start | bytes 1572872 | tf_op jit(solution)/shard_map/ppermute | solution.py:29
  859.7 93.3 %slice-start.2 = ((s8[8388608]{0:T(1024)(128)(4,1)}), s8[4194304]{0:T(1024)(128)(4,1)S(1)}, s32[]{:S(2)}) async-start(s8[8388608]{0:T(1024)(128)(4,1)} %bitcast.338), calls=%async_computation.3 | async-start | bytes 8388608
  859.8 98.3 %collective-permute-start.43 = (bf16[2,2,64,1024]{3,2,1,0:T(8,128)(2,1)S(1)}, bf16[2,2,64,1024]{3,2,1,0:T(8,128)(2,1)S(1)}, u32[]{:S(2)}, u32[]{:S(2)}) collective-permute-start(bf16[2,2,64,1024]{3,2,1,0:T(8,128)(2,1)S(1)} %get-tuple-element.44), channel_id=1, source_target_pairs={{0,2},{2,0},{1,3},{3,1},{4,6},{6,4},{5,7},{7,5},{8,10},{10,8},{9,1... | collective-permute-start | bytes 1572872 | tf_op jit(solution)/shard_map/ppermute | solution.py:29
  952.8 26.2 %collective-permute-start.31 = (bf16[256,2048]{1,0:T(8,128)(2,1)S(1)}, bf16[256,2048]{1,0:T(8,128)(2,1)S(1)}, u32[]{:S(2)}, u32[]{:S(2)}) collective-permute-start(bf16[256,2048]{1,0:T(8,128)(2,1)S(1)} %fusion.44), channel_id=1, source_target_pairs={{0,2},{2,0},{1,3},{3,1},{4,6},{6,4},{5,7},{7,5},{8,10},{10,8},{9,1... | collective-permute-start | bytes 3145736 | tf_op jit(solution)/shard_map/ppermute | solution.py:29
  955.6 23.4 %copy-start.4 = (bf16[1,256,2048]{2,1,0:T(8,128)(2,1)S(1)}, bf16[1,256,2048]{2,1,0:T(8,128)(2,1)}, u32[]{:S(2)}) copy-start(bf16[1,256,2048]{2,1,0:T(8,128)(2,1)} %param.14) | copy-start | bytes 3145732
  955.6 23.4 %copy-start.32 = (f32[2048]{0:T(1024)S(1)}, f32[2048]{0:T(1024)}, u32[]{:S(2)}) copy-start(f32[2048]{0:T(1024)} %copy-done.31) | copy-start | bytes 24580
  955.6 23.4 %copy-start.38 = (f32[256]{0:T(256)S(1)}, f32[256]{0:T(256)}, u32[]{:S(2)}) copy-start(f32[256]{0:T(256)} %copy-done.37) | copy-start | bytes 3076
  955.6 23.4 %copy-start.39 = (f32[256]{0:T(256)S(1)}, f32[256]{0:T(256)}, u32[]{:S(2)}) copy-start(f32[256]{0:T(256)} %add_rsqrt_fusion.1) | copy-start | bytes 3076
  955.8 45.7 %collective-permute-start.28 = (bf16[256,2048]{1,0:T(8,128)(2,1)S(1)}, bf16[256,2048]{1,0:T(8,128)(2,1)S(1)}, u32[]{:S(2)}, u32[]{:S(2)}) collective-permute-start(bf16[256,2048]{1,0:T(8,128)(2,1)S(1)} %fusion.43), channel_id=1, source_target_pairs={{0,2},{2,0},{1,3},{3,1},{4,6},{6,4},{5,7},{7,5},{8,10},{10,8},{9,1... | collective-permute-start | bytes 3145736 | tf_op jit(solution)/shard_map/ppermute | solution.py:29
  957.8 43.7 %copy-start.35 = (f32[2048]{0:T(1024)S(1)}, f32[2048]{0:T(1024)}, u32[]{:S(2)}) copy-start(f32[2048]{0:T(1024)} %reshape.1351) | copy-start | bytes 24580
  957.8 43.6 %copy-start.36 = (f32[2048]{0:T(1024)S(1)}, f32[2048]{0:T(1024)}, u32[]{:S(2)}) copy-start(f32[2048]{0:T(1024)} %reshape.1352) | copy-start | bytes 24580
  957.8 53.2 %collective-permute-start.48 = (bf16[2,2,64,1024]{3,2,1,0:T(8,128)(2,1)S(1)}, bf16[2,2,64,1024]{3,2,1,0:T(8,128)(2,1)}, u32[]{:S(2)}, u32[]{:S(2)}) collective-permute-start(bf16[2,2,64,1024]{3,2,1,0:T(8,128)(2,1)S(1)} %get-tuple-element.38), channel_id=1, source_target_pairs={{0,2},{2,0},{1,3},{3,1},{4,6},{6,4},{5,7},{7,5},{8,10},{10,8},{9,1... | collective-permute-start | bytes 1572872 | tf_op jit(solution)/shard_map/ppermute | solution.py:29
  (38 other events, 256.8 us)
Sparse Core Ops, SparseCore 0:
  1006.6 117.6 all-reduce.3

commit v2 on v1

--- a/solution.py
+++ b/solution.py
@@ -25,8 +25,24 @@
     )
 
 
+MIB = 1024 * 1024
+SCALE = 0.0
+
+
+def after(value, *others):
+    return lax.optimization_barrier((value,) + others)[0]
+
+
+def fence(*values):
+    return lax.optimization_barrier(values)
+
+
 def swap(value, axis):
     return lax.ppermute(value, axis, [(0, 1), (1, 0)])
+
+
+def pick(value, place, dim):
+    return lax.dynamic_index_in_dim(value, place, dim, keepdims=False)
 
 
 def in_order(own, other, place, dim):
@@ -35,52 +51,478 @@
     )
 
 
-def pick(value, place, dim):
-    return lax.dynamic_index_in_dim(value, place, dim, keepdims=False)
-
-
-def exchange(value, axes_dims):
-    for axis, dim in axes_dims:
-        place = lax.axis_index(axis)
-        other = swap(pick(value, 1 - place, dim), axis)
-        value = in_order(pick(value, place, dim), other, place, dim)
-    return value
-
-
-TEAM = (("c", 1), ("x", 0), ("zl", 2))
-
-
-def team_gather(value):
-    value = jnp.stack([value, swap(value, "zl")])
-    value = jnp.stack([value, swap(value, "x")])
-    return jnp.stack([value, swap(value, "c")])
-
-
-def team_sum(value):
-    for axis in ("c", "x", "zl"):
-        other = swap(value[1].astype(BF16), axis)
-        value = value[0].astype(F32) + other.astype(F32)
-    return value
-
-
-def rows_gather(value, mesh):
+def flip(value, place, dim):
+    return jnp.where(place == 0, value, jnp.flip(value, dim))
+
+
+def exchange(value):
+    _, rows, n = value.shape
+    return lax.all_to_all(value, ("x", "c", "zl"), 0, 0, tiled=True).reshape(4, 2, rows, n)
+
+
+def fold_first(keep, other):
+    value = keep.astype(F32) + other.astype(F32)
+    rows, half = value.shape[0] // 4, value.shape[1] // 2
+    value = value.reshape(2, 2, rows, 2 * half)
+    one, two = value[..., :half], value[..., half:]
+    one = one[0] + swap(one[1].astype(BF16), "x").astype(F32)
+    two = two[:, 0] + swap(two[:, 1].astype(BF16), "zl").astype(F32)
+    return one, two
+
+
+def fold_second(halves):
+    one, two = halves
+    one = one[0] + swap(one[1].astype(BF16), "zl").astype(F32)
+    two = two[0] + swap(two[1].astype(BF16), "x").astype(F32)
+    return jnp.concatenate([one, two], 1)
+
+
+def rows_first(part, mesh):
+    return swap(part, "zh"), swap(part, "y") if mesh.shape["y"] == 2 else part
+
+
+def rows_last(far, mesh):
+    return swap(far, "y") if mesh.shape["y"] == 2 else far
+
+
+def rows_pieces(part, far, side, last, mesh):
+    if mesh.shape["y"] == 2:
+        return part, far, side, last
+    value = in_order(part, far, lax.axis_index("zh"), 1)
+    return (lax.all_gather(value, "y", axis=3).reshape(-1, part.shape[-1]),)
+
+
+def zh_halves(value):
     place = lax.axis_index("zh")
-    value = in_order(value, swap(value, "zh"), place, 2)
-    if mesh.shape["y"] == 2:
-        return in_order(value, swap(value, "y"), lax.axis_index("y"), 4)
-    return lax.all_gather(value, "y", axis=4)
+    return pick(value, place, 2).astype(F32), pick(value, 1 - place, 2).astype(BF16)
+
+
+def to_owner(summed):
+    value = summed.astype(BF16).reshape((8,) + summed.shape[3:])
+    return lax.all_to_all(value, ("x", "c", "zl"), 0, 0, tiled=True)
 
 
 def rows_sum(value, mesh):
-    if mesh.shape["y"] == 2:
+    if mesh.shape["y"] != 2:
+        value = lax.psum_scatter(value.astype(BF16), "y", scatter_dimension=4)
+    else:
         place = lax.axis_index("y")
         other = swap(pick(value, 1 - place, 4).astype(BF16), "y")
         value = pick(value, place, 4).astype(F32) + other.astype(F32)
+    keep, send = zh_halves(value)
+    return keep + swap(send, "zh").astype(F32)
+
+
+def spread(value, devices):
+    return lax.all_to_all(
+        jnp.broadcast_to(value[None], (devices,) + value.shape), ALL, 0, 0, tiled=True
+    )
+
+
+def params(**kind):
+    return pltpu.CompilerParams(vmem_limit_bytes=56 * MIB, **kind)
+
+
+def cost(units):
+    return pl.CostEstimate(flops=int(units * SCALE * 1e9), bytes_accessed=0, transcendentals=0)
+
+
+HBM = pl.BlockSpec(memory_space=pl.ANY)
+SCALARS = pl.BlockSpec(memory_space=pltpu.SMEM)
+
+
+def load_rows(place, pieces, out, sems):
+    if len(pieces) == 1:
+        copies = [pltpu.make_async_copy(pieces[0], out, sems.at[0])]
     else:
-        value = lax.psum_scatter(value.astype(BF16), "y", scatter_dimension=4).astype(F32)
-    place = lax.axis_index("zh")
-    other = swap(pick(value, 1 - place, 2).astype(BF16), "zh")
-    return pick(value, place, 2).astype(F32) + other.astype(F32)
+        xc, zl, rows, _ = pieces[0].shape
+        copies = []
+        for i, piece in enumerate(pieces):
+            zh, y = place[0] ^ (i % 2), place[1] ^ (i // 2)
+            for j in range(xc):
+                for k in range(zl):
+                    row = (((j * 2 + zh) * zl + k) * 2 + y) * rows
+                    row = pl.ds(pl.multiple_of(row, rows), rows)
+                    copies.append(
+                        pltpu.make_async_copy(
+                            piece.at[j, k], out.at[row, :], sems.at[len(copies)]
+                        )
+                    )
+    for copy in copies:
+        copy.start()
+    return copies
+
+
+def weight_specs(*weights):
+    return [HBM for weight in weights for _ in weight]
+
+
+def weight_scratch(*weights):
+    shapes = []
+    for weight in weights:
+        n = weight[0].shape[-1]
+        rows = sum(piece.size for piece in weight) // n
+        shapes += [pltpu.VMEM((rows, n), BF16), pltpu.SemaphoreType.DMA((32,))]
+    return shapes
+
+
+def own_place():
+    return jnp.stack([lax.axis_index("zh"), lax.axis_index("y")]).astype(jnp.int32)
+
+
+def at_first(refs, place, counts, scratch):
+    @pl.when(pl.program_id(0) == 0)
+    def _():
+        copies, first = [], 0
+        for i, count in enumerate(counts):
+            copies += load_rows(place, refs[first : first + count], *scratch[2 * i : 2 * i + 2])
+            first += count
+        for copy in copies:
+            copy.wait()
+
+
+GELU_A = 0.7978845608028654
+GELU_B = 0.044715
+CHUNK = 256
+
+
+def up_kernel(place, normed, bias, *refs):
+    count = len(refs) - 4
+    pieces, (pre, hidden, weight, sems) = refs[:count], refs[count:]
+    at_first(pieces, place, (count,), (weight, sems))
+    for first in range(0, weight.shape[1], CHUNK):
+        part = slice(first, first + CHUNK)
+        value = dot(normed[...], weight[:, part], 1, 0) + bias[:, part]
+        pre[:, part] = value
+        inner = jnp.tanh(GELU_A * (value + GELU_B * (value * value * value)))
+        hidden[:, part] = (0.5 * value * (1.0 + inner)).astype(BF16)
+
+
+def up_forward(normed, bias, weight, block):
+    count, width = normed.shape
+    n = weight[0].shape[-1]
+    return pl.pallas_call(
+        up_kernel,
+        grid=(count // block,),
+        in_specs=[
+            SCALARS,
+            pl.BlockSpec((block, width), lambda i: (i, 0)),
+            pl.BlockSpec((1, n), lambda i: (0, 0)),
+        ]
+        + weight_specs(weight),
+        out_specs=[pl.BlockSpec((block, n), lambda i: (i, 0))] * 2,
+        out_shape=[jax.ShapeDtypeStruct((count, n), F32), jax.ShapeDtypeStruct((count, n), BF16)],
+        scratch_shapes=weight_scratch(weight),
+        compiler_params=params(),
+        cost_estimate=cost(17),
+    )(own_place(), normed, bias, *weight)
+
+
+def hidden_grad_kernel(place, grad, pre, *refs):
+    count = len(refs) - 4
+    pieces, (out, total, weight, sems) = refs[:count], refs[count:]
+    at_first(pieces, place, (count,), (weight, sems))
+
+    @pl.when(pl.program_id(0) == 0)
+    def _():
+        total[...] = jnp.zeros_like(total)
+
+    for first in range(0, weight.shape[1], CHUNK):
+        part = slice(first, first + CHUNK)
+        value = pre[:, part]
+        square = value * value
+        inner = jnp.tanh(GELU_A * (value + GELU_B * (square * value)))
+        slope = 0.5 * (1.0 + inner) + 0.5 * value * (1.0 - inner * inner) * (
+            GELU_A * (1.0 + 3.0 * GELU_B * square)
+        )
+        low = (dot(grad[...], weight[:, part], 1, 0) * slope).astype(BF16)
+        out[:, part] = low
+        total[:, part] += jnp.sum(low.astype(F32), 0, keepdims=True)
+
+
+def hidden_backward(grad, pre, weight, block):
+    count, width = grad.shape
+    n = weight[0].shape[-1]
+    return pl.pallas_call(
+        hidden_grad_kernel,
+        grid=(count // block,),
+        in_specs=[
+            SCALARS,
+            pl.BlockSpec((block, width), lambda i: (i, 0)),
+            pl.BlockSpec((block, n), lambda i: (i, 0)),
+        ]
+        + weight_specs(weight),
+        out_specs=[
+            pl.BlockSpec((block, n), lambda i: (i, 0)),
+            pl.BlockSpec((1, n), lambda i: (0, 0)),
+        ],
+        out_shape=[jax.ShapeDtypeStruct((count, n), BF16), jax.ShapeDtypeStruct((1, n), F32)],
+        scratch_shapes=weight_scratch(weight),
+        compiler_params=params(),
+        cost_estimate=cost(20),
+    )(own_place(), grad, pre, *weight)
+
+
+def weight_grad_kernel(place, left, right, keep, send):
+    xc, zh, zl, rows, n = keep.shape
+    value = dot(left[...], right[...], 0, 0).astype(BF16).reshape(zl, 2, rows, n)
+    own = place[1] == 0
+    keep[0, 0] = jnp.where(own, value[:, 0], value[:, 1])
+    send[0, 0] = jnp.where(own, value[:, 1], value[:, 0])
+
+
+def weight_grad_plain_kernel(left, right, out):
+    out[...] = dot(left[...], right[...], 0, 0).astype(BF16)
+
+
+def weight_grad(left, right, mesh):
+    count, width = left.shape
+    n = right.shape[1]
+    y = mesh.shape["y"]
+    rows = width // (16 * y)
+    block = width // 8
+    specs = [
+        pl.BlockSpec((count, block), lambda i: (0, i)),
+        pl.BlockSpec((count, n), lambda i: (0, 0), pipeline_mode=pl.Buffered(1)),
+    ]
+    if y != 2:
+        full = pl.pallas_call(
+            weight_grad_plain_kernel,
+            grid=(8,),
+            in_specs=specs,
+            out_specs=pl.BlockSpec((block, n), lambda i: (i, 0)),
+            out_shape=jax.ShapeDtypeStruct((width, n), BF16),
+            compiler_params=params(),
+            cost_estimate=cost(14 * n / 1024),
+        )(left, right)
+        return full, full
+    out = pl.BlockSpec((1, 1, 2, rows, n), lambda i: (i // 2, i % 2, 0, 0, 0))
+    shape = jax.ShapeDtypeStruct((4, 2, 2, rows, n), BF16)
+    keep, send = pl.pallas_call(
+        weight_grad_kernel,
+        grid=(8,),
+        in_specs=[SCALARS] + specs,
+        out_specs=[out, out],
+        out_shape=[shape, shape],
+        compiler_params=params(),
+        cost_estimate=cost(14 * n / 1024),
+    )(own_place(), left, right)
+
+    return keep, send
+
+
+def sum_first(send, mesh):
+    if mesh.shape["y"] == 2:
+        return swap(send, "y")
+    y, n = mesh.shape["y"], send.shape[-1]
+    rows = send.shape[0] // (16 * y)
+    return lax.psum_scatter(send.reshape(2, 2, 2, 2, y, rows, n), "y", scatter_dimension=4)
+
+
+def sum_halves(keep, other, mesh):
+    if mesh.shape["y"] != 2:
+        return zh_halves(other)
+    value = keep.astype(F32) + other.astype(F32)
+    return zh_halves(value.reshape((2, 2, 2, 2) + value.shape[3:]))
+
+
+def joint_kernel(place, normed, bias, cosine, sine, *refs):
+    count = len(refs) - 3
+    pieces, (out, weight, sems) = refs[:count], refs[count:]
+    at_first(pieces, place, (count,), (weight, sems))
+    value = dot(normed[...], weight[...], 1, 0) + bias[...]
+    third = value.shape[1] // 3
+    lane = lax.broadcasted_iota(jnp.int32, (value.shape[0], PAIR), 1) % HD
+    for first in range(0, 2 * third, PAIR):
+        piece = turn(value[:, first : first + PAIR], cosine[...], sine[...], lane, 1.0).astype(BF16)
+        if first < third:
+            piece = piece * jnp.asarray(HD ** (-0.5), BF16)
+        out[:, first : first + PAIR] = piece
+    out[:, 2 * third :] = value[:, 2 * third :].astype(BF16)
+
+
+def joint_forward(normed, bias, cosine, sine, weight, block):
+    count, width = normed.shape
+    n = weight[0].shape[-1]
+    return pl.pallas_call(
+        joint_kernel,
+        grid=(count // block,),
+        in_specs=[
+            SCALARS,
+            pl.BlockSpec((block, width), lambda i: (i, 0)),
+            pl.BlockSpec((1, n), lambda i: (0, 0)),
+            pl.BlockSpec((block, PAIR), lambda i: (i, 0)),
+            pl.BlockSpec((block, PAIR), lambda i: (i, 0)),
+        ]
+        + weight_specs(weight),
+        out_specs=pl.BlockSpec((block, n), lambda i: (i, 0)),
+        out_shape=jax.ShapeDtypeStruct((count, n), BF16),
+        scratch_shapes=weight_scratch(weight),
+        compiler_params=params(),
+        cost_estimate=cost(13.5),
+    )(own_place(), normed, bias, cosine, sine, *weight)
+
+
+def pair_kernel(dims, counts, place, one, two, *refs):
+    total = sum(counts)
+    pieces, (keep, send), scratch = refs[:total], refs[total : total + 2], refs[total + 2 :]
+    at_first(pieces, place, counts, scratch)
+
+    def step(out):
+        for first in range(0, out.shape[1], 2 * CHUNK):
+            part = slice(first, first + 2 * CHUNK)
+            value = 0.0
+            for left, right, dim in zip((one, two), (scratch[0], scratch[2]), dims):
+                right = right[part, :] if dim == 1 else right[:, part]
+                value = value + dot(left[...], right, 1, dim)
+            out[:, part] = value.astype(BF16)
+
+    half = pl.num_programs(0) // 2
+    pl.when(pl.program_id(0) < half)(lambda: step(keep))
+    pl.when(pl.program_id(0) >= half)(lambda: step(send))
+
+
+def pair_product(one, first, two, second, dims, block, units):
+    count = one.shape[0]
+    width = first[0].shape[-1] if dims[0] == 0 else sum(p.size for p in first) // first[0].shape[-1]
+    steps = count // block
+    shape = jax.ShapeDtypeStruct((count // 2, width), BF16)
+    return pl.pallas_call(
+        functools.partial(pair_kernel, dims, (len(first), len(second))),
+        grid=(steps,),
+        in_specs=[
+            SCALARS,
+            pl.BlockSpec((block, one.shape[1]), lambda i: (i, 0)),
+            pl.BlockSpec((block, two.shape[1]), lambda i: (i, 0)),
+        ]
+        + weight_specs(first, second),
+        out_specs=[
+            pl.BlockSpec((block, width), lambda i: (jnp.minimum(i, steps // 2 - 1), 0)),
+            pl.BlockSpec((block, width), lambda i: (jnp.maximum(i - steps // 2, 0), 0)),
+        ],
+        out_shape=[shape, shape],
+        scratch_shapes=weight_scratch(first, second),
+        compiler_params=params(),
+        cost_estimate=cost(units),
+    )(own_place(), one, two, *first, *second)
+
+
+def norm_kernel(*refs):
+    blocks, (gain_ref, shift_ref, out_ref) = refs[:8], refs[8:]
+
+    def one(ref):
+        wide = ref[...].astype(F32)
+        centered = wide - jnp.mean(wide, 1, keepdims=True)
+        inv_std = lax.rsqrt(jnp.mean(centered * centered, 1, keepdims=True) + NORM_EPS)
+        out_ref[...] = (centered * inv_std * gain_ref[...] + shift_ref[...]).astype(BF16)
+
+    for i, ref in enumerate(blocks):
+        pl.when(pl.program_id(0) == i)(functools.partial(one, ref))
+
+
+def grad_kernel(*refs):
+    blocks, (weight_ref, out_ref, attended_ref) = refs[:8], refs[8:]
+
+    def one(ref):
+        out_ref[...] = ref[...]
+        attended_ref[...] = dot(ref[...], weight_ref[...], 1, 1).astype(BF16)
+
+    for i, ref in enumerate(blocks):
+        pl.when(pl.program_id(0) == i)(functools.partial(one, ref))
+
+
+def rows_of_team(kernel, blocks, rest, widths):
+    rows = blocks[0].shape[0]
+    return pl.pallas_call(
+        kernel,
+        grid=(8,),
+        in_specs=[
+            pl.BlockSpec(value.shape, lambda i: (0, 0), pipeline_mode=pl.Buffered(1))
+            for value in (*blocks, *rest)
+        ],
+        out_specs=[pl.BlockSpec((rows, wide), lambda i: (i, 0)) for wide in widths],
+        out_shape=[jax.ShapeDtypeStruct((8 * rows, wide), BF16) for wide in widths],
+        compiler_params=params(),
+        cost_estimate=cost(11),
+    )(*blocks, *rest)
+
+
+def split_kernel(value, out):
+    n = out.shape[2]
+    for i in range(8):
+        out[i] = value[:, i * n : (i + 1) * n]
+
+
+def join_kernel(value, out):
+    n = value.shape[2]
+    for i in range(8):
+        out[:, i * n : (i + 1) * n] = value[i].astype(F32)
+
+
+def by_columns(weight):
+    rows, n = weight.shape[0], weight.shape[1] // 8
+    return pl.pallas_call(
+        split_kernel,
+        out_shape=jax.ShapeDtypeStruct((8, rows, n), weight.dtype),
+        cost_estimate=cost(2),
+    )(weight)
+
+
+def from_columns(value):
+    _, rows, n = value.shape
+    return pl.pallas_call(
+        join_kernel,
+        out_shape=jax.ShapeDtypeStruct((rows, 8 * n), F32),
+        cost_estimate=cost(3),
+    )(value)
+
+
+def head_places():
+    for third in range(3):
+        for x in range(2):
+            for c in range(2):
+                for zh in range(2):
+                    for zl in range(2):
+                        pair = ((x * 2 + c) * 2 + zh) * 2 + zl
+                        yield (x * 2 + c) * 2 + zl, (third * 2 + zh) * PAIR, (third * 16 + pair) * PAIR
+
+
+def split_heads_kernel(value, out):
+    for place, own, whole in head_places():
+        out[place, :, own : own + PAIR] = value[:, whole : whole + PAIR]
+
+
+def join_heads_kernel(value, out):
+    for place, own, whole in head_places():
+        out[:, whole : whole + PAIR] = value[place, :, own : own + PAIR].astype(F32)
+
+
+def by_heads(weight):
+    rows, n = weight.shape[0], weight.shape[1] // 8
+    return pl.pallas_call(
+        split_heads_kernel,
+        out_shape=jax.ShapeDtypeStruct((8, rows, n), weight.dtype),
+        cost_estimate=cost(2),
+    )(weight)
+
+
+def from_heads(value):
+    _, rows, n = value.shape
+    return pl.pallas_call(
+        join_heads_kernel,
+        out_shape=jax.ShapeDtypeStruct((rows, 8 * n), F32),
+        cost_estimate=cost(3),
+    )(value)
+
+
+def rows_sorted(pieces, mesh):
+    if len(pieces) == 1:
+        return pieces[0]
+    zh, y = lax.axis_index("zh"), lax.axis_index("y")
+    n = pieces[0].shape[-1]
+    near = in_order(pieces[0], pieces[1], zh, 1)
+    side = in_order(pieces[2], pieces[3], zh, 1)
+    return in_order(near, side, y, 3).reshape(-1, n)
 
 
 def turn(value, cosine, sine, lane, sign):
@@ -107,15 +549,11 @@
 
     for block in range(blocks):
         at = place(block)
-        cosine, sine = cos_ref[block, 0], sin_ref[block, 0]
-        query = turn(q_ref[block, 0], cosine, sine, lane, 1.0).astype(BF16)
-        qs[at, :] = query * jnp.asarray(scale, BF16)
-        key = turn(k_ref[block, 0], cosine, sine, lane, 1.0)
-        ks[at, :] = key.astype(BF16)
-        kt[:, at] = key.T.astype(BF16)
-        value = v_ref[block, 0]
-        vs[at, :] = value.astype(BF16)
-        vt[:, at] = value.T.astype(BF16)
+        qs[at, :] = q_ref[block, 0]
+        ks[at, :] = k_ref[block, 0]
+        kt[:, at] = k_ref[block, 0].T
+        vs[at, :] = v_ref[block, 0]
+        vt[:, at] = v_ref[block, 0].T
         ds[at, :] = do_ref[block, 0]
         segc[at, :] = segc_ref[block, 0]
         segr[:, at] = segr_ref[block, 0]
@@ -210,15 +648,9 @@
             jax.ShapeDtypeStruct((blocks, seqs, rows, third), BF16),
             jax.ShapeDtypeStruct((blocks, seqs, rows, width), BF16),
         ],
-        compiler_params=pltpu.CompilerParams(vmem_limit_bytes=48 * 1024 * 1024),
-        cost_estimate=pl.CostEstimate(
-            flops=20_000_000_000, bytes_accessed=20_000_000, transcendentals=5_000_000
-        ),
+        compiler_params=params(),
+        cost_estimate=cost(33),
     )(order, joint, joint, joint, grad, cosine, sine, segc, segr)
-
-
-def gelu_tanh(inputs):
-    return jax.nn.gelu(inputs, approximate=True)
 
 
 def body(
@@ -242,7 +674,7 @@
     hidden_width = up_weight.shape[1]
     own_rows = joint_weight.shape[0]
     devices = mesh.size
-    ix, ic, izl = lax.axis_index("x"), lax.axis_index("c"), lax.axis_index("zl")
+    ix, ic, izl = (lax.axis_index(axis) for axis in ("x", "c", "zl"))
     count = 8 * rows
     heads_wide = width // 8
     units = hidden_width // 8
@@ -250,55 +682,55 @@
     own_grad = cotangent.reshape(rows, width)
 
     sizes = [v.shape[0] for v in (joint_bias, up_bias, output_bias, down_bias, norm_gain, norm_shift)]
-    small = lax.all_gather(
-        jnp.concatenate([joint_bias, up_bias, output_bias, down_bias, norm_gain, norm_shift]), ALL
-    )
     cuts = [sum(sizes[:i]) for i in range(len(sizes) + 1)]
+    small = jnp.concatenate(
+        [
+            value.astype(F32)
+            for value in (joint_bias, up_bias, output_bias, down_bias, norm_gain, norm_shift)
+        ]
+        + [segments.reshape(rows).astype(F32), positions.reshape(rows).astype(F32)]
+    )
+    lines = -(-small.shape[0] // 128)
+    small = jnp.pad(small, (0, lines * 128 - small.shape[0])).reshape(lines, 128)
+    block = 2 * rows
+    output_part = output_weight.reshape(1, 1, own_rows, width)
+    up_part = exchange(by_columns(up_weight))
+    output_far, output_side = rows_first(output_part, mesh)
+    others = jnp.concatenate([by_columns(down_weight), by_heads(joint_weight)], 2)
+    small = spread(small, devices)
+    up_part, output_far, output_side, others, token, small = fence(
+        up_part, output_far, output_side, others, own_tokens, small
+    )
+
+    up_far, up_side = rows_first(up_part, mesh)
+    token_near, token_far = swap(token, "zl"), swap(token, "x")
+    output_last = rows_last(output_far, mesh)
+    others = exchange(others)
+    up_far, up_side, token_near, token_far, output_last, grad, others = fence(
+        up_far, up_side, token_near, token_far, output_last, own_grad, others
+    )
+    down_part, joint_part = others[..., :units], others[..., units:]
+
+    down_far, down_side = rows_first(down_part, mesh)
+    up_last = rows_last(up_far, mesh)
+    both = swap(jnp.stack([token_near, grad]), "x")
+    grad_near = swap(grad, "zl")
+    small = small.reshape(devices, lines * 128)
     joint_full, up_full, output_full, down_full, gain_full, shift_full = (
-        small[:, cuts[i] : cuts[i + 1]].reshape(-1).astype(F32) for i in range(6)
-    )
-
-    tokens_all = team_gather(own_tokens).reshape(count, width)
-    grad_all = team_gather(own_grad).reshape(count, width)
-    marks = team_gather(jnp.stack([segments.reshape(rows), positions.reshape(rows)]))
-
-    def columns(weight):
-        return weight.reshape(own_rows, 2, 2, 2, units).transpose(1, 2, 3, 0, 4)
-
-    joint_cols = (
-        joint_weight.reshape(own_rows, 3, 2, 2, 2, 2, PAIR)
-        .transpose(2, 3, 5, 0, 1, 4, 6)
-        .reshape(2, 2, 2, own_rows, 3 * heads_wide)
-    )
-    up_mine = rows_gather(exchange(columns(up_weight), TEAM), mesh).reshape(width, units)
-    down_mine = rows_gather(exchange(columns(down_weight), TEAM), mesh).reshape(width, units)
-    joint_mine = rows_gather(exchange(joint_cols, TEAM), mesh).reshape(width, 3 * heads_wide)
-    output_mine = rows_gather(
-        output_weight.reshape(1, 1, 1, own_rows, width), mesh
-    ).reshape(heads_wide, width)
-
+        small[:, cuts[i] : cuts[i + 1]].reshape(-1) for i in range(6)
+    )
+    marks = small[:, cuts[6] : cuts[6] + 2 * rows].reshape(2, 2, 2, 2, mesh.shape["y"], 2, rows)
+    marks = pick(pick(marks, lax.axis_index("zh"), 2), lax.axis_index("y"), 3)
+    marks = flip(flip(flip(marks, ix, 0), ic, 1), izl, 2)
+    marks = marks.transpose(1, 0, 2, 3, 4).reshape(4, 2, 2, rows)
     joint_bias_mine = pick(
         pick(pick(joint_full.reshape(3, 2, 2, 2, 2, PAIR), ix, 1), ic, 1), izl, 2
-    ).reshape(3 * heads_wide)
-    up_bias_mine = pick(up_full.reshape(8, units), (ix * 2 + ic) * 2 + izl, 0)
-
-    wide = tokens_all.astype(F32)
-    centered = wide - jnp.mean(wide, 1, keepdims=True)
-    inv_std = lax.rsqrt(jnp.mean(centered * centered, 1, keepdims=True) + NORM_EPS)
-    normed = (centered * inv_std * gain_full + shift_full).astype(BF16)
-
-    up_pre = dot(normed, up_mine, 1, 0) + up_bias_mine
-    hidden_low = gelu_tanh(up_pre).astype(BF16)
-    hidden_grad = dot(grad_all, down_mine, 1, 0)
-    up_grad_low = jax.vjp(gelu_tanh, up_pre)[1](hidden_grad)[0].astype(BF16)
-
-    joint_out = dot(normed, joint_mine, 1, 0) + joint_bias_mine
-    attended_grad = dot(grad_all, output_mine, 1, 1).astype(BF16)
-
-    marks = marks.reshape(4, 2, 2, rows)
-    seg, pos = marks[:, :, 0], marks[:, :, 1]
+    ).reshape(1, 3 * heads_wide)
+    up_bias_mine = pick(up_full.reshape(8, 1, units), (ix * 2 + ic) * 2 + izl, 0)
+    gain_row, shift_row = gain_full.reshape(1, width), shift_full.reshape(1, width)
+    seg, pos = marks[:, :, 0].astype(jnp.int32), marks[:, :, 1]
     frequency = 10000.0 ** (-jnp.arange(0, ROT, 2, dtype=F32) / ROT)
-    angles = pos.astype(F32)[..., None] * frequency
+    angles = pos[..., None] * frequency
     angles = jnp.concatenate([angles, angles], -1)
     rest = angles.shape[:-1] + (HD - ROT,)
     cosine = jnp.concatenate([jnp.cos(angles), jnp.ones(rest, F32)] * 2, -1)
@@ -306,10 +738,69 @@
     segc = jnp.broadcast_to(seg[..., None], seg.shape + (PAIR,))
     segr = jnp.broadcast_to(seg[:, :, None], (4, 2, 8, rows))
     rel = jnp.arange(4, dtype=jnp.int32)
-    order = 2 * ((rel % 2) ^ ix) + ((rel // 2) ^ ic)
+    order = (2 * ((rel % 2) ^ ix) + ((rel // 2) ^ ic)).astype(jnp.int32)
+    output_mine = rows_sorted(
+        rows_pieces(output_part, output_far, output_side, output_last, mesh), mesh
+    )
+    (
+        down_far, down_side, up_last, both, joint_part, grad_near,
+        cosine, sine, segc, segr, output_mine, gain_row, shift_row, up_bias_mine,
+    ) = fence(
+        down_far, down_side, up_last, both, joint_part, grad_near,
+        cosine, sine, segc, segr, output_mine, gain_row, shift_row, up_bias_mine,
+    )
+    tokens = (token, token_near, token_far, both[0])
+    tokens += tuple(swap(v, "c") for v in tokens)
+    tokens, down_far, joint_part, grad, grad_near, grad_far = fence(
+        tokens, down_far, joint_part, grad, grad_near, both[1]
+    )
+
+    joint_far, joint_side = rows_first(joint_part, mesh)
+    down_last = rows_last(down_far, mesh)
+    grad_last = swap(grad_near, "x")
+    (normed,) = rows_of_team(norm_kernel, tokens, (gain_row, shift_row), (width,))
+    up_mine = rows_pieces(up_part, up_far, up_side, up_last, mesh)
+    up_pre, hidden_low = up_forward(normed, up_bias_mine, up_mine, block)
+    joint_far, joint_side, down_last, grad_last, hidden_low, normed = fence(
+        joint_far, joint_side, down_last, grad_last, hidden_low, normed
+    )
+    grads = (grad, grad_near, grad_far, grad_last)
+    grads += tuple(swap(v, "c") for v in grads)
+    grads, joint_far = fence(grads, joint_far)
+
+    joint_last = rows_last(joint_far, mesh)
+    grad_all, attended_grad = rows_of_team(
+        grad_kernel,
+        grads,
+        (output_mine,),
+        (width, heads_wide),
+    )
+    down_mine = rows_pieces(down_part, down_far, down_side, down_last, mesh)
+    down_keep, down_send = weight_grad(grad_all, hidden_low, mesh)
+    down_send, grad_all, attended_grad, joint_last = fence(
+        down_send, grad_all, attended_grad, joint_last
+    )
+
+    down_other = sum_first(down_send, mesh)
+    up_grad_low, up_total = hidden_backward(grad_all, up_pre, down_mine, block)
+    up_keep, up_send = weight_grad(normed, up_grad_low, mesh)
+    joint_mine = rows_pieces(joint_part, joint_far, joint_side, joint_last, mesh)
+    joint_low = joint_forward(
+        after(normed, up_send),
+        joint_bias_mine,
+        cosine.reshape(count, PAIR),
+        sine.reshape(count, PAIR),
+        joint_mine,
+        block,
+    )
+    down_other, up_send, joint_low, up_grad_low = fence(down_other, up_send, joint_low, up_grad_low)
+
+    up_other = sum_first(up_send, mesh)
+    down_keep, down_send = sum_halves(down_keep, down_other, mesh)
+    down_other = swap(down_send, "zh")
     attended_low, joint_grad_low = attend(
-        order.astype(jnp.int32),
-        joint_out.reshape(4, 2, rows, 3 * heads_wide),
+        order,
+        joint_low.reshape(4, 2, rows, 3 * heads_wide),
         attended_grad.reshape(4, 2, rows, heads_wide),
         cosine,
         sine,
@@ -318,14 +809,45 @@
     )
     attended_low = attended_low.reshape(count, heads_wide)
     joint_grad_low = joint_grad_low.reshape(count, 3 * heads_wide)
-
-    shape = (2, 2, 2, rows, width)
-    branch = dot(hidden_low, down_mine, 1, 1) + dot(attended_low, output_mine, 1, 0)
-    layer_sum = team_sum(branch.astype(BF16).reshape(shape))
+    joint_keep, joint_send = weight_grad(normed, joint_grad_low, mesh)
+    up_other, down_other, down_keep, attended_low, joint_grad_low, joint_send = fence(
+        up_other, down_other, down_keep, attended_low, joint_grad_low, joint_send
+    )
+
+    joint_other = sum_first(joint_send, mesh)
+    up_keep, up_send = sum_halves(up_keep, up_other, mesh)
+    up_other = swap(up_send, "zh")
+    down_moved = to_owner(down_keep + down_other.astype(F32))
+    back_keep, back_send = pair_product(
+        joint_grad_low, joint_mine, up_grad_low, up_mine, (1, 1), block, 24
+    )
+    out_keep, out_send = pair_product(
+        after(hidden_low, back_send), down_mine, attended_low, (output_mine,), (1, 0), block, 19
+    )
+    back_other = swap(back_send, "c")
+    joint_other, up_other, up_keep, down_moved, back_keep, back_other, out_send = fence(
+        joint_other, up_other, up_keep, down_moved, back_keep, back_other, out_send
+    )
+
+    joint_keep, joint_send = sum_halves(joint_keep, joint_other, mesh)
+    joint_other = swap(joint_send, "zh")
+    up_moved = to_owner(up_keep + up_other.astype(F32))
+    out_other = swap(out_send, "c")
+    back = fold_first(back_keep, back_other)
+    output_grad = dot(attended_low, grad_all, 0, 0).astype(BF16)
+    joint_other, joint_keep, up_moved, out_other, back, output_grad = fence(
+        joint_other, joint_keep, up_moved, out_other, back, output_grad
+    )
+
+    joint_moved = to_owner(joint_keep + joint_other.astype(F32))
+    produced = fold_second(back)
+    out = fold_first(out_keep, out_other)
+    output_weight_grad = rows_sum(
+        output_grad.reshape(1, 1, 2, 1, mesh.shape["y"], own_rows, width), mesh
+    ).reshape(own_rows, width)
+    joint_moved, out, produced = fence(joint_moved, out, produced)
+    layer_sum = fold_second(out)
     layer_out = (own_tokens.astype(F32) + output_full + down_full + layer_sum).astype(BF16)
-    back = dot(joint_grad_low, joint_mine, 1, 1) + dot(up_grad_low, up_mine, 1, 1)
-    produced = team_sum(back.astype(BF16).reshape(shape))
-
     own_wide = own_tokens.astype(F32)
     own_centered = own_wide - jnp.mean(own_wide, 1, keepdims=True)
     own_inv = lax.rsqrt(jnp.mean(own_centered * own_centered, 1, keepdims=True) + NORM_EPS)
@@ -338,35 +860,15 @@
     )
     tokens_grad = tokens_grad.astype(BF16)
 
-    rows_shape = (2, 2, 2, 2, mesh.shape["y"], own_rows)
-
-    def to_owner(partial):
-        summed = rows_sum(partial.reshape(rows_shape + (partial.shape[1],)), mesh)
-        return exchange(summed.astype(BF16), TEAM).astype(F32)
-
-    def uncolumns(value):
-        return value.transpose(3, 0, 1, 2, 4).reshape(own_rows, hidden_width)
-
-    up_weight_grad = uncolumns(to_owner(dot(normed, up_grad_low, 0, 0)))
-    down_weight_grad = uncolumns(to_owner(dot(grad_all, hidden_low, 0, 0)))
-    joint_weight_grad = (
-        to_owner(dot(normed, joint_grad_low, 0, 0))
-        .reshape(2, 2, 2, own_rows, 3, 2, PAIR)
-        .transpose(3, 4, 0, 1, 5, 2, 6)
-        .reshape(own_rows, 3 * width)
-    )
-    output_weight_grad = rows_sum(
-        dot(attended_low, grad_all, 0, 0).reshape(1, 1, 2, 1, mesh.shape["y"], own_rows, width), mesh
-    ).reshape(own_rows, width)
-
+    down_weight_grad = from_columns(down_moved)
+    joint_weight_grad = from_heads(joint_moved)
+    up_weight_grad = from_columns(up_moved)
     joint_sum = jnp.sum(joint_grad_low.astype(F32), 0).reshape(3, 1, 1, 2, 1, PAIR)
     joint_sum = lax.dynamic_update_slice(
         jnp.zeros((3, 2, 2, 2, 2, PAIR), F32), joint_sum, (0, ix, ic, 0, izl, 0)
     )
     up_sum = lax.dynamic_update_slice(
-        jnp.zeros((8, units), F32),
-        jnp.sum(up_grad_low.astype(F32), 0)[None],
-        ((ix * 2 + ic) * 2 + izl, 0),
+        jnp.zeros((8, units), F32), up_total, ((ix * 2 + ic) * 2 + izl, 0)
     )
     sums = [
         joint_sum,
@@ -376,7 +878,8 @@
         jnp.sum(produced, 0),
     ]
     sums = jnp.concatenate([v.reshape(devices, -1) for v in sums], 1)
-    sums = lax.psum_scatter(sums, ALL, scatter_dimension=0)
+    sums = lax.all_to_all(sums, ALL, 0, 0, tiled=True)
+    sums = jnp.sum(sums, 0)
     joint_bias_grad = sums[: cuts[1]]
     up_bias_grad = sums[cuts[1] : cuts[2]]
     grad_total, norm_gain_grad, norm_shift_grad = (

time: 1140 us -> 610 us (0.54)
  waiting for transfers between devices: 639 us -> 198 us
  Pallas kernels: 35.3 us -> 204 us
  matrix products: 137 us -> 6.81 us
  local copies, waits for them, and re-layouts: 119 us -> 48.2 us
  other arithmetic: 107 us -> 62.9 us
  blocking collectives: 42.5 us -> 0 us
  starting transfers between devices: 40.4 us -> 76.6 us
  between operations: 15.7 us -> 1.87 us
    ppermute x49 -> x43, waiting for transfers between devices: 543 us -> 187 us  [swap(): return lax.ppermute(value, axis, [(0, 1), (1, 0)])]
    pallas_call x0 -> x16, Pallas kernels: none -> 171 us  [the longest x2 42 us: pair_product(): pl.pallas_call(functools.partial(pair_kernel, dims, (len(first), len(seco...]
    dot_general x12 -> x1, matrix products: 137 us -> 6.81 us  [dot(): lax.dot_general(left, right, (((left_dim,), (right_dim,)), ((), ())), pre...]
    unnamed x2 -> x0, waiting for transfers between devices: 96.2 us -> none
    unnamed x1 -> x0, blocking collectives: 42.5 us -> none
    all_to_all x0 -> x7, starting transfers between devices: none -> 32.8 us  [the longest x3 13.2 us: to_owner(): return lax.all_to_all(value, ('x', 'c', 'zl'), 0, 0, tiled=True)]
    select_n x29 -> x3, other arithmetic: 28.8 us -> 1.38 us  [in_order(): jnp.where(place == 0, jnp.stack([own, other], dim), jnp.stack([other, own...]
    dot_general x3 -> x0, local copies, waits for them, and re-layouts: 25.2 us -> none  [dot(): lax.dot_general(left, right, (((left_dim,), (right_dim,)), ((), ())), pre...]
  transfers between devices with their start and end apart: 50 -> 50, of which waited for: 20 -> 22; matrix products, arithmetic and copies ran while one was open for 22% -> 16% of each run, Pallas kernels for 0% -> 30%
where the time goes in v2:
time: 610 us; the launch traced here: 598 us
  Pallas kernels  204 us (33%)
  waiting for transfers between devices  198 us (32%)
  starting transfers between devices  76.6 us (13%)
  other arithmetic  62.9 us (10%)
  local copies, waits for them, and re-layouts  48.2 us (8%)
  matrix products  6.81 us (1%)
    ppermute x43, waiting for transfers between devices, swap(): return lax.ppermute(value, axis, [(0, 1), (1, 0)])  187 us
    ppermute x43, starting transfers between devices, swap(): return lax.ppermute(value, axis, [(0, 1), (1, 0)])  43.8 us
    pallas_call x2, Pallas kernels, pair_product(): pl.pallas_call(functools.partial(pair_kernel, dims, (len(first), len(seco...  42 us
    pallas_call x3, Pallas kernels, weight_grad(): pl.pallas_call(weight_grad_kernel, grid=(8,), in_specs=[SCALARS] + specs,...  41 us
    pallas_call x1, Pallas kernels, attend(): pl.pallas_call(attend_kernel, grid_spec=pltpu.PrefetchScalarGridSpec(num_...  33.3 us
    pallas_call x2, Pallas kernels, rows_of_team(): pl.pallas_call(kernel, grid=(8,), in_specs=[pl.BlockSpec(value.shape, lam...  21.9 us
    pallas_call x1, Pallas kernels, hidden_backward(): pl.pallas_call(hidden_grad_kernel, grid=(count // block,), in_specs=[SCAL...  19.8 us
    pallas_call x1, Pallas kernels, up_forward(): pl.pallas_call(up_kernel, grid=(count // block,), in_specs=[SCALARS, pl.B...  17.4 us
  transfers between devices with their start and end apart: 50, of which 22 were waited for; matrix products, arithmetic and copies ran while one was open for 16% of the time, Pallas kernels for 30%

profile of v2, /device:TPU:0, one launch (start us, length us, event | category | flops | bytes accessed | tf_op | source)
XLA Modules:
  0.0 598.4 jit_solution(8241627054977795408)
XLA Ops:
  2.0 4.1 concatenate.82
  6.8 7.3 %all-to-all-start.1 = ((f32[32,10,128]{2,1,0:T(8,128)}), f32[32,10,128]{2,1,0:T(8,128)S(1)}, u32[]{:S(2)}, u32[]{:S(2)}) async-start(f32[32,10,128]{2,1,0:T(8,128)} %broadcast_in_dim.17), calls=%async_computation.1 | async-start | bytes 524288 | tf_op jit(solution)/shard_map/all_to_all | solution.py:117
  14.1 2.3 shard_map.229
  16.4 8.3 %all-to-all-done.1 = f32[32,10,128]{2,1,0:T(8,128)S(1)} async-done(((f32[32,10,128]{2,1,0:T(8,128)}), f32[32,10,128]{2,1,0:T(8,128)S(1)}, u32[]{:S(2)}, u32[]{:S(2)}) %all-to-all-start.1) | async-done | bytes 163872 | tf_op jit(solution)/shard_map/all_to_all | solution.py:117
  24.8 3.6 all-to-all-start
  29.8 2.3 shard_map.230
  32.1 2.2 shard_map.231
  34.3 2.5 pad_maximum_fusion.2
  36.8 9.4 %collective-permute-done = bf16[1,1,64,2048]{3,2,1,0:T(8,128)(2,1)S(1)} collective-permute-done((bf16[1,1,64,2048]{3,2,1,0:T(8,128)(2,1)S(1)}, bf16[1,1,64,2048]{3,2,1,0:T(8,128)(2,1)S(1)}, u32[]{:S(2)}, u32[]{:S(2)}) %collective-permute-start) | collective-permute-done | bytes 262176 | tf_op jit(solution)/shard_map/ppermute | solution.py:41
  46.2 2.6 all-to-all-done
  48.8 4.5 all-to-all-start.2
  61.2 24.4 %collective-permute-done.6 = bf16[1,1,64,2048]{3,2,1,0:T(8,128)(2,1)S(1)} collective-permute-done((bf16[1,1,64,2048]{3,2,1,0:T(8,128)(2,1)}, bf16[1,1,64,2048]{3,2,1,0:T(8,128)(2,1)S(1)}, u32[]{:S(2)}, u32[]{:S(2)}) %collective-permute-start.6) | collective-permute-done | bytes 262176 | tf_op jit(solution)/shard_map/ppermute | solution.py:41
  85.6 16.7 %collective-permute-done.2.refs_1_.refs_5_ = bf16[4,2,64,1024]{3,2,1,0:T(8,128)(2,1)} collective-permute-done((bf16[4,2,64,1024]{3,2,1,0:T(8,128)(2,1)S(1)}, bf16[4,2,64,1024]{3,2,1,0:T(8,128)(2,1)}, u32[]{:S(2)}, u32[]{:S(2)}) %collective-permute-start.2) | collective-permute-done | bytes 1048608 | tf_op jit(solution)/shard_map/ppermute | solution.py:41
  102.4 18.8 %collective-permute-done.4.refs_1_ = bf16[256,2048]{1,0:T(8,128)(2,1)} collective-permute-done((bf16[256,2048]{1,0:T(8,128)(2,1)S(1)}, bf16[256,2048]{1,0:T(8,128)(2,1)}, u32[]{:S(2)}, u32[]{:S(2)}) %collective-permute-start.4) | collective-permute-done | bytes 1048608 | tf_op jit(solution)/shard_map/ppermute | solution.py:41
  121.2 2.8 pad_maximum_fusion
  132.9 2.3 copy.66
  139.4 3.0 pad_maximum_fusion.3
  145.1 30.0 %collective-permute-done.7.refs_1_ = bf16[4,2,64,1024]{3,2,1,0:T(8,128)(2,1)} collective-permute-done((bf16[4,2,64,1024]{3,2,1,0:T(8,128)(2,1)S(1)}, bf16[4,2,64,1024]{3,2,1,0:T(8,128)(2,1)}, u32[]{:S(2)}, u32[]{:S(2)}) %collective-permute-start.7) | collective-permute-done | bytes 1048608 | tf_op jit(solution)/shard_map/ppermute | solution.py:41
  186.4 11.3 %shard_map.232.normed.left = bf16[2048,2048]{1,0:T(8,128)(2,1)} custom-call(bf16[256,2048]{1,0:T(8,128)(2,1)} %bitcast.158, bf16[256,2048]{1,0:T(8,128)(2,1)} %collective-permute-done.4.refs_1_, bf16[256,2048]{1,0:T(8,128)(2,1)} %collective-permute-done.5.refs_2_, bf16[256,2048]{1,0:T(8,128)(2,1)} %copy-done.20, bf16[256,2048]{1,0:T(8,128)(2,1)} %copy-done.32, ...), custom_call_target="tpu_custom_call" | custom-call | tf_op jit(solution)/shard_map/pallas_call | solution.py:436
  197.7 17.4 %shard_map.233 = (f32[2048,1024]{1,0:T(8,128)}, bf16[2048,1024]{1,0:T(8,128)(2,1)}) custom-call(s32[2]{0:T(128)} %pad_add_fusion.place, bf16[2048,2048]{1,0:T(8,128)(2,1)} %shard_map.232.normed.left, f32[1,1024]{1,0:T(1,128)} %dynamic-slice_bitcast_fusion.5.bias, bf16[4,2,64,1024]{3,2,1,0:T(8,128)(2,1)} %bitcast.179, ...), custom_call_target="tpu_custom_call" | custom-call | tf_op jit(solution)/shard_map/pallas_call | solution.py:204
  215.1 5.2 collective-permute-done.16.refs_1_
  220.4 4.8 collective-permute-done.17.refs_2_
  225.8 2.5 collective-permute-done.22.refs_6_
  230.7 10.6 %shard_map.234 = (bf16[2048,2048]{1,0:T(8,128)(2,1)}, bf16[2048,256]{1,0:T(8,128)(2,1)}) custom-call(bf16[256,2048]{1,0:T(8,128)(2,1)} %bitcast.181, bf16[256,2048]{1,0:T(8,128)(2,1)} %collective-permute-done.11.refs_1_, bf16[256,2048]{1,0:T(8,128)(2,1)} %copy-done.19, bf16[256,2048]{1,0:T(8,128)(2,1)} %collective-permute-done.19.refs_3_, ...), custom_call_target="tpu_custom_call" | custom-call | tf_op jit(solution)/shard_map/pallas_call | solution.py:436
  241.3 14.2 %shard_map.235 = (bf16[4,2,2,64,1024]{4,3,2,1,0:T(8,128)(2,1)}, bf16[4,2,2,64,1024]{4,3,2,1,0:T(8,128)(2,1)}) custom-call(s32[2]{0:T(128)} %pad_add_fusion.place, bf16[2048,2048]{1,0:T(8,128)(2,1)} %get-tuple-element.172.left.grad, bf16[2048,1024]{1,0:T(8,128)(2,1)} %get-tuple-element.203.right.one), custom_call_target="tpu_custom_call" | custom-call | tf_op jit(solution)/shard_map/pallas_call | solution.py:301
  258.0 19.8 %shard_map.236 = (bf16[2048,1024]{1,0:T(8,128)(2,1)}, f32[1,1024]{1,0:T(1,128)}) custom-call(s32[2]{0:T(128)} %pad_add_fusion.place, bf16[2048,2048]{1,0:T(8,128)(2,1)} %get-tuple-element.172.left.grad, f32[2048,1024]{1,0:T(8,128)} %get-tuple-element.173.pre, bf16[4,2,64,1024]{3,2,1,0:T(8,128)(2,1)} %copy-done.11, ...), custom_call_target="tpu_custom_call" | custom-call | tf_op jit(solution)/shard_map/pallas_call | solution.py:246
  277.9 14.2 %shard_map.237 = (bf16[4,2,2,64,1024]{4,3,2,1,0:T(8,128)(2,1)}, bf16[4,2,2,64,1024]{4,3,2,1,0:T(8,128)(2,1)}) custom-call(s32[2]{0:T(128)} %pad_add_fusion.place, bf16[2048,2048]{1,0:T(8,128)(2,1)} %shard_map.232.normed.left, bf16[2048,1024]{1,0:T(8,128)(2,1)} %get-tuple-element.200.right.two), custom_call_target="tpu_custom_call" | custom-call | tf_op jit(solution)/shard_map/pallas_call | solution.py:301
  292.1 14.1 %shard_map.238 = bf16[2048,768]{1,0:T(8,128)(2,1)} custom-call(s32[2]{0:T(128)} %pad_add_fusion.place, bf16[2048,2048]{1,0:T(8,128)(2,1)} %shard_map.232.normed.left, f32[1,768]{1,0:T(1,128)} %bitcast.210, f32[2048,128]{1,0:T(8,128)} %bitcast.186, f32[2048,128]{1,0:T(8,128)} %bitcast.187, bf16[4,2,64,768]{3,2,1,0:T(8,128)(2,1)} %copy-done.13, ...), custom_call_target="tpu_custom_call" | custom-call | tf_op jit(solution)/shard_map/pallas_call | solution.py:347
  307.3 2.5 convert_add_fusion.3
  310.8 33.3 %shard_map.239 = (bf16[4,2,256,256]{3,2,1,0:T(8,128)(2,1)}, bf16[4,2,256,768]{3,2,1,0:T(8,128)(2,1)}) custom-call(s32[4]{0:T(128)} %fusion.33.order, bf16[4,2,256,768]{3,2,1,0:T(8,128)(2,1)} %bitcast.155, bf16[4,2,256,768]{3,2,1,0:T(8,128)(2,1)} %bitcast.156, bf16[4,2,256,768]{3,2,1,0:T(8,128)(2,1)} %bitcast.157, bf16[4,2,256,256]{3,2,1,0:T(8,128)(2,1)} %bitcast.195, ...), custom_call_target="tpu_custom_call" | custom-call | tf_op jit(solution)/shard_map/pallas_call | solution.py:617
  344.0 12.6 %shard_map.240 = (bf16[4,2,2,64,768]{4,3,2,1,0:T(8,128)(2,1)}, bf16[4,2,2,64,768]{4,3,2,1,0:T(8,128)(2,1)}) custom-call(s32[2]{0:T(128)} %pad_add_fusion.place, bf16[2048,2048]{1,0:T(8,128)(2,1)} %shard_map.232.normed.left, bf16[2048,768]{1,0:T(8,128)(2,1)} %bitcast.162), custom_call_target="tpu_custom_call" | custom-call | tf_op jit(solution)/shard_map/pallas_call | solution.py:301
  356.9 23.6 %shard_map.241 = (bf16[1024,2048]{1,0:T(8,128)(2,1)}, bf16[1024,2048]{1,0:T(8,128)(2,1)}) custom-call(s32[2]{0:T(128)} %pad_add_fusion.place, bf16[2048,768]{1,0:T(8,128)(2,1)} %bitcast.163, bf16[2048,1024]{1,0:T(8,128)(2,1)} %get-tuple-element.200.right.two, bf16[4,2,64,768]{3,2,1,0:T(8,128)(2,1)} %copy-done.13, bf16[4,2,64,768]{3,2,1,0:T(8,128)(2,1)} %copy-done.26, ...), custom_call_target="tpu_custom_call" | custom-call | tf_op jit(solution)/shard_map/pallas_call | solution.py:390
  380.6 2.5 add_convert_fusion.1
  383.2 4.6 all-to-all-start.3
  388.8 2.5 convert_add_fusion.2
  391.4 2.0 copy-done.5
  394.5 2.6 collective-permute-start.29
  397.3 18.4 %shard_map.242 = (bf16[1024,2048]{1,0:T(8,128)(2,1)}, bf16[1024,2048]{1,0:T(8,128)(2,1)}) custom-call(s32[2]{0:T(128)} %pad_add_fusion.place, bf16[2048,1024]{1,0:T(8,128)(2,1)} %get-tuple-element.203.right.one, bf16[2048,256]{1,0:T(8,128)(2,1)} %bitcast.188, bf16[4,2,64,1024]{3,2,1,0:T(8,128)(2,1)} %copy-done.11, ...), custom_call_target="tpu_custom_call" | custom-call | tf_op jit(solution)/shard_map/pallas_call | solution.py:390
  415.9 27.5 %collective-permute-done.29 = bf16[2,2,2,64,1024]{4,3,2,1,0:T(8,128)(2,1)} collective-permute-done((bf16[2,2,2,64,1024]{4,3,2,1,0:T(8,128)(2,1)}, bf16[2,2,2,64,1024]{4,3,2,1,0:T(8,128)(2,1)}, u32[]{:S(2)}, u32[]{:S(2)}) %collective-permute-start.29) | collective-permute-done | bytes 1048608 | tf_op jit(solution)/shard_map/ppermute | solution.py:41
  444.3 5.4 convert_add_fusion.1
  455.3 2.5 add_convert_fusion
  457.9 4.4 all-to-all-start.4
  462.3 6.8 %convolution_convert_fusion = bf16[256,2048]{1,0:T(8,128)(2,1)} fusion(bf16[2048,256]{1,0:T(8,128)(2,1)S(1)} %bitcast.189, bf16[2048,2048]{1,0:T(8,128)(2,1)} %get-tuple-element.172.left.grad), kind=kOutput, calls=%fused_computation.12 | convolution fusion | flops 2148007936 | bytes 10485760 | tf_op jit(solution)/shard_map/dot_general | solution.py:23
  473.7 3.4 collective-permute-start.31
  478.0 2.7 shard_map.245
  480.7 2.7 dynamic-slice_bitcast_fusion.2
  483.4 12.3 %collective-permute-done.34 = bf16[2,256,1024]{2,1,0:T(8,128)(2,1)} collective-permute-done((bf16[2,256,1024]{2,1,0:T(8,128)(2,1)}, bf16[2,256,1024]{2,1,0:T(8,128)(2,1)}, u32[]{:S(2)}, u32[]{:S(2)}) %collective-permute-start.34) | collective-permute-done | bytes 1048608 | tf_op jit(solution)/shard_map/ppermute | solution.py:41
  495.7 5.0 fusion.13
  500.6 11.7 %collective-permute-done.31 = bf16[2,2,2,64,768]{4,3,2,1,0:T(8,128)(2,1)} collective-permute-done((bf16[2,2,2,64,768]{4,3,2,1,0:T(8,128)(2,1)}, bf16[2,2,2,64,768]{4,3,2,1,0:T(8,128)(2,1)}, u32[]{:S(2)}, u32[]{:S(2)}) %collective-permute-start.31) | collective-permute-done | bytes 786464 | tf_op jit(solution)/shard_map/ppermute | solution.py:41
  512.4 2.1 fusion.22
  517.8 5.4 convert_add_fusion
  529.8 2.3 add_convert_fusion.2
  532.1 4.2 all-to-all-start.5
  536.3 2.7 shard_map.244
  541.3 3.1 collective-permute-start.42
  546.9 7.0 %collective-permute-done.35 = bf16[2,256,1024]{2,1,0:T(8,128)(2,1)} collective-permute-done((bf16[2,256,1024]{2,1,0:T(8,128)(2,1)}, bf16[2,256,1024]{2,1,0:T(8,128)(2,1)}, u32[]{:S(2)}, u32[]{:S(2)}) %collective-permute-start.35) | collective-permute-done | bytes 1048608 | tf_op jit(solution)/shard_map/ppermute | solution.py:41
  553.9 6.6 %collective-permute-done.36 = bf16[2,256,1024]{2,1,0:T(8,128)(2,1)} collective-permute-done((bf16[2,256,1024]{2,1,0:T(8,128)(2,1)}, bf16[2,256,1024]{2,1,0:T(8,128)(2,1)}, u32[]{:S(2)}, u32[]{:S(2)}) %collective-permute-start.36) | collective-permute-done | bytes 1048608 | tf_op jit(solution)/shard_map/ppermute | solution.py:41
  560.5 5.8 fusion.11
  567.5 2.1 convert_reduce_fusion.2
  570.7 4.3 all-to-all-start.6
  574.9 2.1 fusion.24
  578.8 2.1 fusion.25
  583.2 2.5 shard_map.243
  587.6 4.1 collective-permute-done.39
  (262 shorter events, 90.2 us)
Async XLA Ops:
  6.8 18.0 %all-to-all-start.1 = ((f32[32,10,128]{2,1,0:T(8,128)}), f32[32,10,128]{2,1,0:T(8,128)S(1)}, u32[]{:S(2)}, u32[]{:S(2)}) async-start(f32[32,10,128]{2,1,0:T(8,128)} %broadcast_in_dim.17), calls=%async_computation.1 | async-start | bytes 524288 | tf_op jit(solution)/shard_map/all_to_all | solution.py:117
  14.1 14.2 %copy-start.40 = (bf16[64,2048]{1,0:T(8,128)(2,1)S(1)}, bf16[64,2048]{1,0:T(8,128)(2,1)}, u32[]{:S(2)}) copy-start(bf16[64,2048]{1,0:T(8,128)(2,1)} %param.16) | copy-start | bytes 786436
  24.8 24.0 %all-to-all-start = ((bf16[8,64,1024]{2,1,0:T(8,128)(2,1)}), bf16[8,64,1024]{2,1,0:T(8,128)(2,1)S(1)}, u32[]{:S(2)}, u32[]{:S(2)}) async-start(bf16[8,64,1024]{2,1,0:T(8,128)(2,1)} %shard_map.229), calls=%async_computation | async-start | bytes 2097152 | tf_op jit(solution)/shard_map/all_to_all | solution.py:60
  28.3 17.9 %collective-permute-start = (bf16[1,1,64,2048]{3,2,1,0:T(8,128)(2,1)S(1)}, bf16[1,1,64,2048]{3,2,1,0:T(8,128)(2,1)S(1)}, u32[]{:S(2)}, u32[]{:S(2)}) collective-permute-start(bf16[1,1,64,2048]{3,2,1,0:T(8,128)(2,1)S(1)} %bitcast.200), channel_id=1, source_target_pairs={{0,4},{4,0},{1,5},{5,1},{2,6},{6,2},{3,7},{7,3},{8,12},{12,8},{9,1... | collective-permute-start | bytes 786440 | tf_op jit(solution)/shard_map/ppermute | solution.py:41
  28.9 17.3 %collective-permute-start.1 = (bf16[1,1,64,2048]{3,2,1,0:T(8,128)(2,1)S(1)}, bf16[1,1,64,2048]{3,2,1,0:T(8,128)(2,1)S(1)}, u32[]{:S(2)}, u32[]{:S(2)}) collective-permute-start(bf16[1,1,64,2048]{3,2,1,0:T(8,128)(2,1)S(1)} %bitcast.201), channel_id=1, source_target_pairs={{0,1},{1,0},{2,3},{3,2},{4,5},{5,4},{6,7},{7,6},{8,9},{9,8},{10,11... | collective-permute-start | bytes 786440 | tf_op jit(solution)/shard_map/ppermute | solution.py:41
  36.8 19.1 %copy-start = (bf16[1,256,2048]{2,1,0:T(8,128)(2,1)S(1)}, bf16[1,256,2048]{2,1,0:T(8,128)(2,1)}, u32[]{:S(2)}) copy-start(bf16[1,256,2048]{2,1,0:T(8,128)(2,1)} %param.14) | copy-start | bytes 3145732
  48.8 72.4 %copy-start.9 = (bf16[1,256,2048]{2,1,0:T(8,128)(2,1)S(1)}, bf16[1,256,2048]{2,1,0:T(8,128)(2,1)}, u32[]{:S(2)}) copy-start(bf16[1,256,2048]{2,1,0:T(8,128)(2,1)} %param.27) | copy-start | bytes 3145732
  48.8 72.4 %all-to-all-start.2 = ((bf16[8,64,1792]{2,1,0:T(8,128)(2,1)}), bf16[8,64,1792]{2,1,0:T(8,128)(2,1)}, u32[]{:S(2)}, u32[]{:S(2)}) async-start(bf16[8,64,1792]{2,1,0:T(8,128)(2,1)} %pad_maximum_fusion.2), calls=%async_computation.2 | async-start | bytes 3670016 | tf_op jit(solution)/shard_map/all_to_all | solution.py:60
  53.3 49.1 %collective-permute-start.2 = (bf16[4,2,64,1024]{3,2,1,0:T(8,128)(2,1)S(1)}, bf16[4,2,64,1024]{3,2,1,0:T(8,128)(2,1)}, u32[]{:S(2)}, u32[]{:S(2)}) collective-permute-start(bf16[4,2,64,1024]{3,2,1,0:T(8,128)(2,1)S(1)} %bitcast.177), channel_id=1, source_target_pairs={{0,4},{4,0},{1,5},{5,1},{2,6},{6,2},{3,7},{7,3},{8,12},{12,8},{9,1... | collective-permute-start | bytes 3145736 | tf_op jit(solution)/shard_map/ppermute | solution.py:41
  54.9 47.4 %collective-permute-start.3 = (bf16[4,2,64,1024]{3,2,1,0:T(8,128)(2,1)S(1)}, bf16[4,2,64,1024]{3,2,1,0:T(8,128)(2,1)}, u32[]{:S(2)}, u32[]{:S(2)}) collective-permute-start(bf16[4,2,64,1024]{3,2,1,0:T(8,128)(2,1)S(1)} %bitcast.178), channel_id=1, source_target_pairs={{0,1},{1,0},{2,3},{3,2},{4,5},{5,4},{6,7},{7,6},{8,9},{9,8},{10,11... | collective-permute-start | bytes 3145736 | tf_op jit(solution)/shard_map/ppermute | solution.py:41
  55.9 65.2 %collective-permute-start.4 = (bf16[256,2048]{1,0:T(8,128)(2,1)S(1)}, bf16[256,2048]{1,0:T(8,128)(2,1)}, u32[]{:S(2)}, u32[]{:S(2)}) collective-permute-start(bf16[256,2048]{1,0:T(8,128)(2,1)S(1)} %bitcast.159), channel_id=1, source_target_pairs={{0,2},{2,0},{1,3},{3,1},{4,6},{6,4},{5,7},{7,5},{8,10},{10,8},{9,1... | collective-permute-start | bytes 3145736 | tf_op jit(solution)/shard_map/ppermute | solution.py:41
  57.8 63.4 %collective-permute-start.5 = (bf16[256,2048]{1,0:T(8,128)(2,1)S(1)}, bf16[256,2048]{1,0:T(8,128)(2,1)}, u32[]{:S(2)}, u32[]{:S(2)}) collective-permute-start(bf16[256,2048]{1,0:T(8,128)(2,1)S(1)} %bitcast.160), channel_id=1, source_target_pairs={{0,16},{16,0},{1,17},{17,1},{2,18},{18,2},{3,19},{19,3},{4,20},{20... | collective-permute-start | bytes 3145736 | tf_op jit(solution)/shard_map/ppermute | solution.py:41
  60.1 25.5 %collective-permute-start.6 = (bf16[1,1,64,2048]{3,2,1,0:T(8,128)(2,1)}, bf16[1,1,64,2048]{3,2,1,0:T(8,128)(2,1)S(1)}, u32[]{:S(2)}, u32[]{:S(2)}) collective-permute-start(bf16[1,1,64,2048]{3,2,1,0:T(8,128)(2,1)} %copy-done.42), channel_id=1, source_target_pairs={{0,1},{1,0},{2,3},{3,2},{4,5},{5,4},{6,7},{7,6},{8,9},{9,8},{10,11... | collective-permute-start | bytes 786440 | tf_op jit(solution)/shard_map/ppermute | solution.py:41
  85.6 35.5 %copy-start.46 = (bf16[1,1,64,2048]{3,2,1,0:T(8,128)(2,1)}, bf16[1,1,64,2048]{3,2,1,0:T(8,128)(2,1)S(1)}, u32[]{:S(2)}) copy-start(bf16[1,1,64,2048]{3,2,1,0:T(8,128)(2,1)S(1)} %collective-permute-done.6) | copy-start | bytes 786436
  123.9 52.1 %collective-permute-start.10 = (bf16[2,256,2048]{2,1,0:T(8,128)(2,1)}, bf16[2,256,2048]{2,1,0:T(8,128)(2,1)}, u32[]{:S(2)}, u32[]{:S(2)}) collective-permute-start(bf16[2,256,2048]{2,1,0:T(8,128)(2,1)} %pad_maximum_fusion), channel_id=1, source_target_pairs={{0,16},{16,0},{1,17},{17,1},{2,18},{18,2},{3,19},{19,3},{4,20},{20... | collective-permute-start | bytes 6291464 | tf_op jit(solution)/shard_map/ppermute | solution.py:41
  127.0 48.1 %collective-permute-start.7 = (bf16[4,2,64,1024]{3,2,1,0:T(8,128)(2,1)S(1)}, bf16[4,2,64,1024]{3,2,1,0:T(8,128)(2,1)}, u32[]{:S(2)}, u32[]{:S(2)}) collective-permute-start(bf16[4,2,64,1024]{3,2,1,0:T(8,128)(2,1)S(1)} %slice.124.refs_0_), channel_id=1, source_target_pairs={{0,4},{4,0},{1,5},{5,1},{2,6},{6,2},{3,7},{7,3},{8,12},{12,8},{9,1... | collective-permute-start | bytes 3145736 | tf_op jit(solution)/shard_map/ppermute | solution.py:41
  128.7 46.4 %collective-permute-start.8 = (bf16[4,2,64,1024]{3,2,1,0:T(8,128)(2,1)S(1)}, bf16[4,2,64,1024]{3,2,1,0:T(8,128)(2,1)}, u32[]{:S(2)}, u32[]{:S(2)}) collective-permute-start(bf16[4,2,64,1024]{3,2,1,0:T(8,128)(2,1)S(1)} %slice.124.refs_0_), channel_id=1, source_target_pairs={{0,1},{1,0},{2,3},{3,2},{4,5},{5,4},{6,7},{7,6},{8,9},{9,8},{10,11... | collective-permute-start | bytes 3145736 | tf_op jit(solution)/shard_map/ppermute | solution.py:41
  129.7 46.3 %collective-permute-start.11 = (bf16[256,2048]{1,0:T(8,128)(2,1)S(1)}, bf16[256,2048]{1,0:T(8,128)(2,1)}, u32[]{:S(2)}, u32[]{:S(2)}) collective-permute-start(bf16[256,2048]{1,0:T(8,128)(2,1)S(1)} %bitcast.182), channel_id=1, source_target_pairs={{0,2},{2,0},{1,3},{3,1},{4,6},{6,4},{5,7},{7,5},{8,10},{10,8},{9,1... | collective-permute-start | bytes 3145736 | tf_op jit(solution)/shard_map/ppermute | solution.py:41
  130.2 45.9 %collective-permute-start.9 = (bf16[4,2,64,1024]{3,2,1,0:T(8,128)(2,1)}, bf16[4,2,64,1024]{3,2,1,0:T(8,128)(2,1)}, u32[]{:S(2)}, u32[]{:S(2)}) collective-permute-start(bf16[4,2,64,1024]{3,2,1,0:T(8,128)(2,1)} %collective-permute-done.2.refs_1_.refs_5_), channel_id=1, source_target_pairs={{0,1},{1,0},{2,3},{3,2},{4,5},{5,4},{6,7},{7,6},{8,9},{9,8},{10,11... | collective-permute-start | bytes 3145736 | tf_op jit(solution)/shard_map/ppermute | solution.py:41
  143.7 41.0 %copy-start.13 = (bf16[4,2,64,768]{3,2,1,0:T(8,128)(2,1)}, bf16[4,2,64,768]{3,2,1,0:T(8,128)(2,1)S(1)}, u32[]{:S(2)}) copy-start(bf16[4,2,64,768]{3,2,1,0:T(8,128)(2,1)S(1)} %slice.125.refs_0_) | copy-start | bytes 2359300
  175.1 5.3 collective-permute-start.12
  175.1 5.3 collective-permute-start.13
  176.1 4.9 collective-permute-start.14
  179.8 45.4 %copy-start.19 = (bf16[256,2048]{1,0:T(8,128)(2,1)}, bf16[256,2048]{1,0:T(8,128)(2,1)S(1)}, u32[]{:S(2)}) copy-start(bf16[256,2048]{1,0:T(8,128)(2,1)S(1)} %get-tuple-element.159.refs_2_) | copy-start | bytes 3145732
  179.8 2.9 collective-permute-start.15
  182.7 42.5 %collective-permute-start.18 = (bf16[4,2,64,1024]{3,2,1,0:T(8,128)(2,1)}, bf16[4,2,64,1024]{3,2,1,0:T(8,128)(2,1)S(1)}, u32[]{:S(2)}, u32[]{:S(2)}) collective-permute-start(bf16[4,2,64,1024]{3,2,1,0:T(8,128)(2,1)} %collective-permute-done.7.refs_1_), channel_id=1, source_target_pairs={{0,1},{1,0},{2,3},{3,2},{4,5},{5,4},{6,7},{7,6},{8,9},{9,8},{10,11... | collective-permute-start | bytes 3145736 | tf_op jit(solution)/shard_map/ppermute | solution.py:41
  183.7 41.5 %collective-permute-start.19 = (bf16[256,2048]{1,0:T(8,128)(2,1)}, bf16[256,2048]{1,0:T(8,128)(2,1)}, u32[]{:S(2)}, u32[]{:S(2)}) collective-permute-start(bf16[256,2048]{1,0:T(8,128)(2,1)} %collective-permute-done.11.refs_1_), channel_id=1, source_target_pairs={{0,16},{16,0},{1,17},{17,1},{2,18},{18,2},{3,19},{19,3},{4,20},{20... | collective-permute-start | bytes 3145736 | tf_op jit(solution)/shard_map/ppermute | solution.py:41
  184.2 36.2 %collective-permute-start.16 = (bf16[4,2,64,768]{3,2,1,0:T(8,128)(2,1)S(1)}, bf16[4,2,64,768]{3,2,1,0:T(8,128)(2,1)S(1)}, u32[]{:S(2)}, u32[]{:S(2)}) collective-permute-start(bf16[4,2,64,768]{3,2,1,0:T(8,128)(2,1)S(1)} %slice.125.refs_0_), channel_id=1, source_target_pairs={{0,4},{4,0},{1,5},{5,1},{2,6},{6,2},{3,7},{7,3},{8,12},{12,8},{9,1... | collective-permute-start | bytes 2359304 | tf_op jit(solution)/shard_map/ppermute | solution.py:41
  184.8 40.4 %collective-permute-start.17 = (bf16[4,2,64,768]{3,2,1,0:T(8,128)(2,1)S(1)}, bf16[4,2,64,768]{3,2,1,0:T(8,128)(2,1)S(1)}, u32[]{:S(2)}, u32[]{:S(2)}) collective-permute-start(bf16[4,2,64,768]{3,2,1,0:T(8,128)(2,1)S(1)} %slice.125.refs_0_), channel_id=1, source_target_pairs={{0,1},{1,0},{2,3},{3,2},{4,5},{5,4},{6,7},{7,6},{8,9},{9,8},{10,11... | collective-permute-start | bytes 2359304 | tf_op jit(solution)/shard_map/ppermute | solution.py:41
  186.4 39.4 %collective-permute-start.21 = (bf16[256,2048]{1,0:T(8,128)(2,1)}, bf16[256,2048]{1,0:T(8,128)(2,1)}, u32[]{:S(2)}, u32[]{:S(2)}) collective-permute-start(bf16[256,2048]{1,0:T(8,128)(2,1)} %collective-permute-done.11.refs_1_), channel_id=1, source_target_pairs={{0,8},{8,0},{1,9},{9,1},{2,10},{10,2},{3,11},{11,3},{4,12},{12,4},... | collective-permute-start | bytes 3145736 | tf_op jit(solution)/shard_map/ppermute | solution.py:41
  220.4 20.9 %copy-start.26 = (bf16[4,2,64,768]{3,2,1,0:T(8,128)(2,1)}, bf16[4,2,64,768]{3,2,1,0:T(8,128)(2,1)S(1)}, u32[]{:S(2)}) copy-start(bf16[4,2,64,768]{3,2,1,0:T(8,128)(2,1)S(1)} %collective-permute-done.16.refs_1_) | copy-start | bytes 2359300
  220.4 5.4 collective-permute-start.20
  225.2 16.1 %copy-start.27 = (bf16[4,2,64,768]{3,2,1,0:T(8,128)(2,1)}, bf16[4,2,64,768]{3,2,1,0:T(8,128)(2,1)S(1)}, u32[]{:S(2)}) copy-start(bf16[4,2,64,768]{3,2,1,0:T(8,128)(2,1)S(1)} %collective-permute-done.17.refs_2_) | copy-start | bytes 2359300
  225.2 3.1 collective-permute-start.22
  225.2 16.1 %copy-start.23 = (bf16[4,2,64,1024]{3,2,1,0:T(8,128)(2,1)}, bf16[4,2,64,1024]{3,2,1,0:T(8,128)(2,1)S(1)}, u32[]{:S(2)}) copy-start(bf16[4,2,64,1024]{3,2,1,0:T(8,128)(2,1)S(1)} %collective-permute-done.18.refs_3_) | copy-start | bytes 3145732
  225.2 4.5 collective-permute-start.23
  229.7 25.8 %collective-permute-start.24 = (bf16[4,2,64,768]{3,2,1,0:T(8,128)(2,1)S(1)}, bf16[4,2,64,768]{3,2,1,0:T(8,128)(2,1)S(1)}, u32[]{:S(2)}, u32[]{:S(2)}) collective-permute-start(bf16[4,2,64,768]{3,2,1,0:T(8,128)(2,1)S(1)} %collective-permute-done.16.refs_1_), channel_id=1, source_target_pairs={{0,1},{1,0},{2,3},{3,2},{4,5},{5,4},{6,7},{7,6},{8,9},{9,8},{10,11... | collective-permute-start | bytes 2359304 | tf_op jit(solution)/shard_map/ppermute | solution.py:41
  255.5 22.4 %copy-start.28 = (bf16[4,2,64,768]{3,2,1,0:T(8,128)(2,1)}, bf16[4,2,64,768]{3,2,1,0:T(8,128)(2,1)S(1)}, u32[]{:S(2)}) copy-start(bf16[4,2,64,768]{3,2,1,0:T(8,128)(2,1)S(1)} %collective-permute-done.24.refs_3_) | copy-start | bytes 2359300
  255.5 50.7 %collective-permute-start.25 = (bf16[4,2,2,64,1024]{4,3,2,1,0:T(8,128)(2,1)}, bf16[4,2,2,64,1024]{4,3,2,1,0:T(8,128)(2,1)}, u32[]{:S(2)}, u32[]{:S(2)}) collective-permute-start(bf16[4,2,2,64,1024]{4,3,2,1,0:T(8,128)(2,1)} %get-tuple-element.171), channel_id=1, source_target_pairs={{0,1},{1,0},{2,3},{3,2},{4,5},{5,4},{6,7},{7,6},{8,9},{9,8},{10,11... | collective-permute-start | bytes 6291464 | tf_op jit(solution)/shard_map/ppermute | solution.py:41
  292.1 15.2 %copy-start.30 = (bf16[4,2,2,64,1024]{4,3,2,1,0:T(8,128)(2,1)S(1)}, bf16[4,2,2,64,1024]{4,3,2,1,0:T(8,128)(2,1)}, u32[]{:S(2)}) copy-start(bf16[4,2,2,64,1024]{4,3,2,1,0:T(8,128)(2,1)} %get-tuple-element.190) | copy-start | bytes 6291460
  306.2 50.8 %collective-permute-start.26 = (bf16[4,2,2,64,1024]{4,3,2,1,0:T(8,128)(2,1)}, bf16[4,2,2,64,1024]{4,3,2,1,0:T(8,128)(2,1)}, u32[]{:S(2)}, u32[]{:S(2)}) collective-permute-start(bf16[4,2,2,64,1024]{4,3,2,1,0:T(8,128)(2,1)} %get-tuple-element.189), channel_id=1, source_target_pairs={{0,1},{1,0},{2,3},{3,2},{4,5},{5,4},{6,7},{7,6},{8,9},{9,8},{10,11... | collective-permute-start | bytes 6291464 | tf_op jit(solution)/shard_map/ppermute | solution.py:41
  309.9 47.0 %collective-permute-start.27 = (bf16[2,2,2,64,1024]{4,3,2,1,0:T(8,128)(2,1)S(1)}, bf16[2,2,2,64,1024]{4,3,2,1,0:T(8,128)(2,1)}, u32[]{:S(2)}, u32[]{:S(2)}) collective-permute-start(bf16[2,2,2,64,1024]{4,3,2,1,0:T(8,128)(2,1)S(1)} %fusion.16), channel_id=1, source_target_pairs={{0,4},{4,0},{1,5},{5,1},{2,6},{6,2},{3,7},{7,3},{8,12},{12,8},{9,1... | collective-permute-start | bytes 3145736 | tf_op jit(solution)/shard_map/ppermute | solution.py:41
  380.5 62.9 %collective-permute-start.30 = (bf16[1024,2048]{1,0:T(8,128)(2,1)}, bf16[1024,2048]{1,0:T(8,128)(2,1)}, u32[]{:S(2)}, u32[]{:S(2)}) collective-permute-start(bf16[1024,2048]{1,0:T(8,128)(2,1)} %get-tuple-element.202), channel_id=1, source_target_pairs={{0,8},{8,0},{1,9},{9,1},{2,10},{10,2},{3,11},{11,3},{4,12},{12,4},... | collective-permute-start | bytes 12582920 | tf_op jit(solution)/shard_map/ppermute | solution.py:41
  383.2 60.2 %all-to-all-start.3 = ((bf16[8,64,1024]{2,1,0:T(8,128)(2,1)}), bf16[8,64,1024]{2,1,0:T(8,128)(2,1)}, u32[]{:S(2)}, u32[]{:S(2)}) async-start(bf16[8,64,1024]{2,1,0:T(8,128)(2,1)} %bitcast.36), calls=%async_computation.3 | async-start | bytes 2097152 | tf_op jit(solution)/shard_map/all_to_all | solution.py:102
  387.8 55.7 %collective-permute-start.28 = (bf16[4,2,2,64,768]{4,3,2,1,0:T(8,128)(2,1)}, bf16[4,2,2,64,768]{4,3,2,1,0:T(8,128)(2,1)}, u32[]{:S(2)}, u32[]{:S(2)}) collective-permute-start(bf16[4,2,2,64,768]{4,3,2,1,0:T(8,128)(2,1)} %get-tuple-element.194), channel_id=1, source_target_pairs={{0,1},{1,0},{2,3},{3,2},{4,5},{5,4},{6,7},{7,6},{8,9},{9,8},{10,11... | collective-permute-start | bytes 4718600 | tf_op jit(solution)/shard_map/ppermute | solution.py:41
  394.5 49.0 %collective-permute-start.29 = (bf16[2,2,2,64,1024]{4,3,2,1,0:T(8,128)(2,1)}, bf16[2,2,2,64,1024]{4,3,2,1,0:T(8,128)(2,1)}, u32[]{:S(2)}, u32[]{:S(2)}) collective-permute-start(bf16[2,2,2,64,1024]{4,3,2,1,0:T(8,128)(2,1)} %fusion.17), channel_id=1, source_target_pairs={{0,4},{4,0},{1,5},{5,1},{2,6},{6,2},{3,7},{7,3},{8,12},{12,8},{9,1... | collective-permute-start | bytes 3145736 | tf_op jit(solution)/shard_map/ppermute | solution.py:41
  397.3 18.5 %copy-start.6 = (f32[4,2,2,64,1024]{4,3,2,1,0:T(8,128)S(1)}, f32[4,2,2,64,1024]{4,3,2,1,0:T(8,128)}, u32[]{:S(2)}) copy-start(f32[4,2,2,64,1024]{4,3,2,1,0:T(8,128)} %copy-done.5) | copy-start | bytes 12582916
  415.7 28.4 %copy-start.48 = (f32[1,1024]{1,0:T(1,128)S(1)}, f32[1,1024]{1,0:T(1,128)}, u32[]{:S(2)}) copy-start(f32[1,1024]{1,0:T(1,128)} %get-tuple-element.225) | copy-start | bytes 12292
  443.4 68.9 %collective-permute-start.32 = (bf16[1024,2048]{1,0:T(8,128)(2,1)}, bf16[1024,2048]{1,0:T(8,128)(2,1)}, u32[]{:S(2)}, u32[]{:S(2)}) collective-permute-start(bf16[1024,2048]{1,0:T(8,128)(2,1)} %get-tuple-element.209), channel_id=1, source_target_pairs={{0,8},{8,0},{1,9},{9,1},{2,10},{10,2},{3,11},{11,3},{4,12},{12,4},... | collective-permute-start | bytes 12582920 | tf_op jit(solution)/shard_map/ppermute | solution.py:41
  450.9 32.5 %collective-permute-start.33 = (bf16[2,256,1024]{2,1,0:T(8,128)(2,1)}, bf16[2,256,1024]{2,1,0:T(8,128)(2,1)}, u32[]{:S(2)}, u32[]{:S(2)}) collective-permute-start(bf16[2,256,1024]{2,1,0:T(8,128)(2,1)} %slice_bitcast_fusion.7), channel_id=1, source_target_pairs={{0,16},{16,0},{1,17},{17,1},{2,18},{18,2},{3,19},{19,3},{4,20},{20... | collective-permute-start | bytes 3145736 | tf_op jit(solution)/shard_map/ppermute | solution.py:41
  454.5 41.2 %collective-permute-start.34 = (bf16[2,256,1024]{2,1,0:T(8,128)(2,1)}, bf16[2,256,1024]{2,1,0:T(8,128)(2,1)}, u32[]{:S(2)}, u32[]{:S(2)}) collective-permute-start(bf16[2,256,1024]{2,1,0:T(8,128)(2,1)} %slice_bitcast_fusion.6), channel_id=1, source_target_pairs={{0,2},{2,0},{1,3},{3,1},{4,6},{6,4},{5,7},{7,5},{8,10},{10,8},{9,1... | collective-permute-start | bytes 3145736 | tf_op jit(solution)/shard_map/ppermute | solution.py:41
  457.9 54.5 %all-to-all-start.4 = ((bf16[8,64,1024]{2,1,0:T(8,128)(2,1)}), bf16[8,64,1024]{2,1,0:T(8,128)(2,1)}, u32[]{:S(2)}, u32[]{:S(2)}) async-start(bf16[8,64,1024]{2,1,0:T(8,128)(2,1)} %bitcast.192), calls=%async_computation.4 | async-start | bytes 2097152 | tf_op jit(solution)/shard_map/all_to_all | solution.py:102
  473.7 38.7 %collective-permute-start.31 = (bf16[2,2,2,64,768]{4,3,2,1,0:T(8,128)(2,1)}, bf16[2,2,2,64,768]{4,3,2,1,0:T(8,128)(2,1)}, u32[]{:S(2)}, u32[]{:S(2)}) collective-permute-start(bf16[2,2,2,64,768]{4,3,2,1,0:T(8,128)(2,1)} %fusion.21), channel_id=1, source_target_pairs={{0,4},{4,0},{1,5},{5,1},{2,6},{6,2},{3,7},{7,3},{8,12},{12,8},{9,1... | collective-permute-start | bytes 2359304 | tf_op jit(solution)/shard_map/ppermute | solution.py:41
  514.5 29.9 %collective-permute-start.37 = (bf16[256,1024]{1,0:T(8,128)(2,1)}, bf16[256,1024]{1,0:T(8,128)(2,1)}, u32[]{:S(2)}, u32[]{:S(2)}) collective-permute-start(bf16[256,1024]{1,0:T(8,128)(2,1)} %fusion.22), channel_id=1, source_target_pairs={{0,2},{2,0},{1,3},{3,1},{4,6},{6,4},{5,7},{7,5},{8,10},{10,8},{9,1... | collective-permute-start | bytes 1572872 | tf_op jit(solution)/shard_map/ppermute | solution.py:41
  516.3 29.3 %collective-permute-start.38 = (bf16[256,1024]{1,0:T(8,128)(2,1)}, bf16[256,1024]{1,0:T(8,128)(2,1)}, u32[]{:S(2)}, u32[]{:S(2)}) collective-permute-start(bf16[256,1024]{1,0:T(8,128)(2,1)} %fusion.23), channel_id=1, source_target_pairs={{0,16},{16,0},{1,17},{17,1},{2,18},{18,2},{3,19},{19,3},{4,20},{20... | collective-permute-start | bytes 1572872 | tf_op jit(solution)/shard_map/ppermute | solution.py:41
  524.3 29.6 %collective-permute-start.35 = (bf16[2,256,1024]{2,1,0:T(8,128)(2,1)}, bf16[2,256,1024]{2,1,0:T(8,128)(2,1)}, u32[]{:S(2)}, u32[]{:S(2)}) collective-permute-start(bf16[2,256,1024]{2,1,0:T(8,128)(2,1)} %slice_bitcast_fusion.5), channel_id=1, source_target_pairs={{0,16},{16,0},{1,17},{17,1},{2,18},{18,2},{3,19},{19,3},{4,20},{20... | collective-permute-start | bytes 3145736 | tf_op jit(solution)/shard_map/ppermute | solution.py:41
  525.9 13.0 %collective-permute-start.41 = (bf16[1,1,2,1,64,2048]{5,4,3,2,1,0:T(8,128)(2,1)}, bf16[1,1,2,1,64,2048]{5,4,3,2,1,0:T(8,128)(2,1)}, u32[]{:S(2)}, u32[]{:S(2)}) collective-permute-start(bf16[1,1,2,1,64,2048]{5,4,3,2,1,0:T(8,128)(2,1)} %dynamic-slice_bitcast_fusion.3), channel_id=1, source_target_pairs={{0,1},{1,0},{2,3},{3,2},{4,5},{5,4},{6,7},{7,6},{8,9},{9,8},{10,11... | collective-permute-start | bytes 1572872 | tf_op jit(solution)/shard_map/ppermute | solution.py:41
  528.5 32.0 %collective-permute-start.36 = (bf16[2,256,1024]{2,1,0:T(8,128)(2,1)}, bf16[2,256,1024]{2,1,0:T(8,128)(2,1)}, u32[]{:S(2)}, u32[]{:S(2)}) collective-permute-start(bf16[2,256,1024]{2,1,0:T(8,128)(2,1)} %slice_bitcast_fusion.4), channel_id=1, source_target_pairs={{0,2},{2,0},{1,3},{3,1},{4,6},{6,4},{5,7},{7,5},{8,10},{10,8},{9,1... | collective-permute-start | bytes 3145736 | tf_op jit(solution)/shard_map/ppermute | solution.py:41
  532.1 34.2 %all-to-all-start.5 = ((bf16[8,64,768]{2,1,0:T(8,128)(2,1)}), bf16[8,64,768]{2,1,0:T(8,128)(2,1)}, u32[]{:S(2)}, u32[]{:S(2)}) async-start(bf16[8,64,768]{2,1,0:T(8,128)(2,1)} %bitcast.193), calls=%async_computation.5 | async-start | bytes 1572864 | tf_op jit(solution)/shard_map/all_to_all | solution.py:102
  541.3 41.1 %collective-permute-start.42 = (bf16[1,1,1,64,2048]{4,3,2,1,0:T(8,128)(2,1)}, bf16[1,1,1,64,2048]{4,3,2,1,0:T(8,128)(2,1)S(1)}, u32[]{:S(2)}, u32[]{:S(2)}) collective-permute-start(bf16[1,1,1,64,2048]{4,3,2,1,0:T(8,128)(2,1)} %fusion.27), channel_id=1, source_target_pairs={{0,4},{4,0},{1,5},{5,1},{2,6},{6,2},{3,7},{7,3},{8,12},{12,8},{9,1... | collective-permute-start | bytes 786440 | tf_op jit(solution)/shard_map/ppermute | solution.py:41
  569.7 12.7 %copy-start.25 = (f32[1,1,2,1,64,2048]{5,4,3,2,1,0:T(8,128)S(1)}, f32[1,1,2,1,64,2048]{5,4,3,2,1,0:T(8,128)}, u32[]{:S(2)}) copy-start(f32[1,1,2,1,64,2048]{5,4,3,2,1,0:T(8,128)} %copy-done.24) | copy-start | bytes 3145732
  570.7 15.1 %all-to-all-start.6 = ((f32[32,1,640]{2,1,0:T(1,128)}), f32[32,1,640]{2,1,0:T(1,128)S(1)}, u32[]{:S(2)}, u32[]{:S(2)}) async-start(f32[32,1,640]{2,1,0:T(1,128)} %all_to_all.30), calls=%async_computation.6 | async-start | bytes 163840 | tf_op jit(solution)/shard_map/all_to_all | solution.py:881
  577.0 14.7 %collective-permute-start.39 = (bf16[256,1024]{1,0:T(8,128)(2,1)}, bf16[256,1024]{1,0:T(8,128)(2,1)}, u32[]{:S(2)}, u32[]{:S(2)}) collective-permute-start(bf16[256,1024]{1,0:T(8,128)(2,1)} %fusion.24), channel_id=1, source_target_pairs={{0,2},{2,0},{1,3},{3,1},{4,6},{6,4},{5,7},{7,5},{8,10},{10,8},{9,1... | collective-permute-start | bytes 1572872 | tf_op jit(solution)/shard_map/ppermute | solution.py:41
  580.9 14.0 %collective-permute-start.40 = (bf16[256,1024]{1,0:T(8,128)(2,1)}, bf16[256,1024]{1,0:T(8,128)(2,1)}, u32[]{:S(2)}, u32[]{:S(2)}) collective-permute-start(bf16[256,1024]{1,0:T(8,128)(2,1)} %fusion.25), channel_id=1, source_target_pairs={{0,16},{16,0},{1,17},{17,1},{2,18},{18,2},{3,19},{19,3},{4,20},{20... | collective-permute-start | bytes 1572872 | tf_op jit(solution)/shard_map/ppermute | solution.py:41
  (36 other events, 159.6 us)

commit v3 on v2

--- a/solution.py
+++ b/solution.py
@@ -61,20 +61,49 @@
 
 
 def fold_first(keep, other):
-    value = keep.astype(F32) + other.astype(F32)
-    rows, half = value.shape[0] // 4, value.shape[1] // 2
-    value = value.reshape(2, 2, rows, 2 * half)
-    one, two = value[..., :half], value[..., half:]
-    one = one[0] + swap(one[1].astype(BF16), "x").astype(F32)
-    two = two[:, 0] + swap(two[:, 1].astype(BF16), "zl").astype(F32)
-    return one, two
-
-
-def fold_second(halves):
-    one, two = halves
-    one = one[0] + swap(one[1].astype(BF16), "zl").astype(F32)
-    two = two[0] + swap(two[1].astype(BF16), "x").astype(F32)
+    rows, half = keep.shape[0] // 4, keep.shape[1] // 2
+    keep, other = (value.reshape(2, 2, rows, 2 * half) for value in (keep, other))
+
+    def part(x, zl, columns):
+        return keep[x, zl, :, columns].astype(F32) + other[x, zl, :, columns].astype(F32)
+
+    one, two = slice(0, half), slice(half, 2 * half)
+    send_one = jnp.stack([part(1, 0, one), part(1, 1, one)]).astype(BF16)
+    send_two = jnp.stack([part(0, 1, two), part(1, 1, two)]).astype(BF16)
+    other_one, other_two = swap(send_one, "x"), swap(send_two, "zl")
+    return (
+        part(0, 0, one) + other_one[0].astype(F32),
+        (part(0, 1, one) + other_one[1].astype(F32)).astype(BF16),
+        part(0, 0, two) + other_two[0].astype(F32),
+        (part(1, 0, two) + other_two[1].astype(F32)).astype(BF16),
+    )
+
+
+def fold_second(parts):
+    one, send_one, two, send_two = parts
+    one = one + swap(send_one, "zl").astype(F32)
+    two = two + swap(send_two, "x").astype(F32)
     return jnp.concatenate([one, two], 1)
+
+
+def pause_kernel(value, out):
+    out[...] = value[...]
+
+
+def far_swap(value):
+    other = swap(value, "zh")
+    lead = (1,) * (value.ndim - 2)
+    paused = pl.pallas_call(
+        pause_kernel,
+        grid=(1,),
+        in_specs=[pl.BlockSpec(lead + (16, 128), lambda i: (0,) * value.ndim)],
+        out_specs=pl.BlockSpec(lead + (16, 128), lambda i: (0,) * value.ndim),
+        out_shape=jax.ShapeDtypeStruct(lead + (16, 128), BF16),
+        cost_estimate=pl.CostEstimate(
+            flops=60_000_000_000, bytes_accessed=0, transcendentals=0
+        ),
+    )(other)
+    return after(other, paused)
 
 
 def rows_first(part, mesh):
@@ -102,15 +131,19 @@
     return lax.all_to_all(value, ("x", "c", "zl"), 0, 0, tiled=True)
 
 
-def rows_sum(value, mesh):
+def y_swap(send, mesh):
     if mesh.shape["y"] != 2:
-        value = lax.psum_scatter(value.astype(BF16), "y", scatter_dimension=4)
-    else:
-        place = lax.axis_index("y")
-        other = swap(pick(value, 1 - place, 4).astype(BF16), "y")
-        value = pick(value, place, 4).astype(F32) + other.astype(F32)
-    keep, send = zh_halves(value)
-    return keep + swap(send, "zh").astype(F32)
+        return lax.psum_scatter(send, "y", scatter_dimension=1)
+    return swap(send, "y")
+
+
+def y_finish(keep, other, mesh):
+    if mesh.shape["y"] == 2:
+        other = keep.astype(F32) + other.astype(F32)
+    place = lax.axis_index("zh")
+    return pick(other, place, 0).astype(F32) + swap(
+        pick(other, 1 - place, 0).astype(BF16), "zh"
+    ).astype(F32)
 
 
 def spread(value, devices):
@@ -326,6 +359,39 @@
     return zh_halves(value.reshape((2, 2, 2, 2) + value.shape[3:]))
 
 
+def output_grad_kernel(place, left, right, keep, send):
+    zh, rows, n = keep.shape
+    value = dot(left[...], right[...], 0, 0).astype(BF16).reshape(zh, 2, rows, n)
+    own = place[1] == 0
+    keep[...] = jnp.where(own, value[:, 0], value[:, 1])
+    send[...] = jnp.where(own, value[:, 1], value[:, 0])
+
+
+def output_grad(left, right, mesh):
+    count, wide = left.shape
+    width = right.shape[1]
+    y = mesh.shape["y"]
+    rows = wide // (2 * y)
+    if y != 2:
+        full = dot(left, right, 0, 0).astype(BF16).reshape(2, y, rows, width)
+        return full, full
+    block = width // 4
+    out = pl.BlockSpec((2, rows, block), lambda i: (0, 0, i))
+    return pl.pallas_call(
+        output_grad_kernel,
+        grid=(4,),
+        in_specs=[
+            SCALARS,
+            pl.BlockSpec((count, wide), lambda i: (0, 0), pipeline_mode=pl.Buffered(1)),
+            pl.BlockSpec((count, block), lambda i: (0, i)),
+        ],
+        out_specs=[out, out],
+        out_shape=[jax.ShapeDtypeStruct((2, rows, width), BF16)] * 2,
+        compiler_params=params(),
+        cost_estimate=cost(5),
+    )(own_place(), left, right)
+
+
 def joint_kernel(place, normed, bias, cosine, sine, *refs):
     count = len(refs) - 3
     pieces, (out, weight, sems) = refs[:count], refs[count:]
@@ -447,10 +513,13 @@
     )(*blocks, *rest)
 
 
-def split_kernel(value, out):
-    n = out.shape[2]
+def split_kernel(up, down, joint, out):
+    n = up.shape[1] // 8
     for i in range(8):
-        out[i] = value[:, i * n : (i + 1) * n]
+        out[i, :, :n] = up[:, i * n : (i + 1) * n]
+        out[i, :, n : 2 * n] = down[:, i * n : (i + 1) * n]
+    for place, own, whole in head_places():
+        out[place, :, 2 * n + own : 2 * n + own + PAIR] = joint[:, whole : whole + PAIR]
 
 
 def join_kernel(value, out):
@@ -459,13 +528,15 @@
         out[:, i * n : (i + 1) * n] = value[i].astype(F32)
 
 
-def by_columns(weight):
-    rows, n = weight.shape[0], weight.shape[1] // 8
+def by_columns(up, down, joint):
+    rows = up.shape[0]
+    wide = (up.shape[1] + down.shape[1] + joint.shape[1]) // 8
     return pl.pallas_call(
         split_kernel,
-        out_shape=jax.ShapeDtypeStruct((8, rows, n), weight.dtype),
-        cost_estimate=cost(2),
-    )(weight)
+        out_shape=jax.ShapeDtypeStruct((8, rows, wide), up.dtype),
+        compiler_params=params(),
+        cost_estimate=cost(4),
+    )(up, down, joint)
 
 
 def from_columns(value):
@@ -487,23 +558,9 @@
                         yield (x * 2 + c) * 2 + zl, (third * 2 + zh) * PAIR, (third * 16 + pair) * PAIR
 
 
-def split_heads_kernel(value, out):
-    for place, own, whole in head_places():
-        out[place, :, own : own + PAIR] = value[:, whole : whole + PAIR]
-
-
 def join_heads_kernel(value, out):
     for place, own, whole in head_places():
         out[:, whole : whole + PAIR] = value[place, :, own : own + PAIR].astype(F32)
-
-
-def by_heads(weight):
-    rows, n = weight.shape[0], weight.shape[1] // 8
-    return pl.pallas_call(
-        split_heads_kernel,
-        out_shape=jax.ShapeDtypeStruct((8, rows, n), weight.dtype),
-        cost_estimate=cost(2),
-    )(weight)
 
 
 def from_heads(value):
@@ -694,26 +751,25 @@
     small = jnp.pad(small, (0, lines * 128 - small.shape[0])).reshape(lines, 128)
     block = 2 * rows
     output_part = output_weight.reshape(1, 1, own_rows, width)
-    up_part = exchange(by_columns(up_weight))
+    parts = exchange(by_columns(up_weight, down_weight, joint_weight))
     output_far, output_side = rows_first(output_part, mesh)
-    others = jnp.concatenate([by_columns(down_weight), by_heads(joint_weight)], 2)
-    small = spread(small, devices)
-    up_part, output_far, output_side, others, token, small = fence(
-        up_part, output_far, output_side, others, own_tokens, small
-    )
+    parts, output_far, output_side, token, small = fence(
+        parts, output_far, output_side, own_tokens, small
+    )
+    up_part = parts[..., :units]
 
     up_far, up_side = rows_first(up_part, mesh)
     token_near, token_far = swap(token, "zl"), swap(token, "x")
-    output_last = rows_last(output_far, mesh)
-    others = exchange(others)
-    up_far, up_side, token_near, token_far, output_last, grad, others = fence(
-        up_far, up_side, token_near, token_far, output_last, own_grad, others
-    )
-    down_part, joint_part = others[..., :units], others[..., units:]
+    grad_far = swap(own_grad, "x")
+    small = spread(small, devices)
+    down_part, joint_part = parts[..., units : 2 * units], parts[..., 2 * units :]
+    up_far, up_side, token_near, token_far, grad_far, grad, down_part, joint_part, small = fence(
+        up_far, up_side, token_near, token_far, grad_far, own_grad, down_part, joint_part, small
+    )
 
     down_far, down_side = rows_first(down_part, mesh)
     up_last = rows_last(up_far, mesh)
-    both = swap(jnp.stack([token_near, grad]), "x")
+    token_last = swap(token_near, "x")
     grad_near = swap(grad, "zl")
     small = small.reshape(devices, lines * 128)
     joint_full, up_full, output_full, down_full, gain_full, shift_full = (
@@ -739,34 +795,35 @@
     segr = jnp.broadcast_to(seg[:, :, None], (4, 2, 8, rows))
     rel = jnp.arange(4, dtype=jnp.int32)
     order = (2 * ((rel % 2) ^ ix) + ((rel // 2) ^ ic)).astype(jnp.int32)
-    output_mine = rows_sorted(
-        rows_pieces(output_part, output_far, output_side, output_last, mesh), mesh
-    )
     (
-        down_far, down_side, up_last, both, joint_part, grad_near,
-        cosine, sine, segc, segr, output_mine, gain_row, shift_row, up_bias_mine,
+        down_far, down_side, up_last, token_last, joint_part, grad_near,
+        cosine, sine, segc, segr, output_far, gain_row, shift_row, up_bias_mine,
     ) = fence(
-        down_far, down_side, up_last, both, joint_part, grad_near,
-        cosine, sine, segc, segr, output_mine, gain_row, shift_row, up_bias_mine,
-    )
-    tokens = (token, token_near, token_far, both[0])
+        down_far, down_side, up_last, token_last, joint_part, grad_near,
+        cosine, sine, segc, segr, output_far, gain_row, shift_row, up_bias_mine,
+    )
+    tokens = (token, token_near, token_far, token_last)
     tokens += tuple(swap(v, "c") for v in tokens)
-    tokens, down_far, joint_part, grad, grad_near, grad_far = fence(
-        tokens, down_far, joint_part, grad, grad_near, both[1]
+    tokens, down_far, joint_part, grad, grad_near, output_far = fence(
+        tokens, down_far, joint_part, grad, grad_near, output_far
     )
 
     joint_far, joint_side = rows_first(joint_part, mesh)
     down_last = rows_last(down_far, mesh)
     grad_last = swap(grad_near, "x")
+    output_last = rows_last(output_far, mesh)
     (normed,) = rows_of_team(norm_kernel, tokens, (gain_row, shift_row), (width,))
     up_mine = rows_pieces(up_part, up_far, up_side, up_last, mesh)
     up_pre, hidden_low = up_forward(normed, up_bias_mine, up_mine, block)
-    joint_far, joint_side, down_last, grad_last, hidden_low, normed = fence(
-        joint_far, joint_side, down_last, grad_last, hidden_low, normed
+    joint_far, joint_side, down_last, grad_last, output_last, hidden_low, normed = fence(
+        joint_far, joint_side, down_last, grad_last, output_last, hidden_low, normed
+    )
+    output_mine = rows_sorted(
+        rows_pieces(output_part, output_far, output_side, output_last, mesh), mesh
     )
     grads = (grad, grad_near, grad_far, grad_last)
     grads += tuple(swap(v, "c") for v in grads)
-    grads, joint_far = fence(grads, joint_far)
+    grads, joint_far, output_mine = fence(grads, joint_far, output_mine)
 
     joint_last = rows_last(joint_far, mesh)
     grad_all, attended_grad = rows_of_team(
@@ -824,28 +881,31 @@
     out_keep, out_send = pair_product(
         after(hidden_low, back_send), down_mine, attended_low, (output_mine,), (1, 0), block, 19
     )
+    output_keep, output_send = output_grad(after(attended_low, out_send), grad_all, mesh)
+    joint_other, up_other, up_keep, down_moved, back_send, out_send, output_send = fence(
+        joint_other, up_other, up_keep, down_moved, back_send, out_send, output_send
+    )
+
+    joint_keep, joint_send = sum_halves(joint_keep, joint_other, mesh)
     back_other = swap(back_send, "c")
-    joint_other, up_other, up_keep, down_moved, back_keep, back_other, out_send = fence(
-        joint_other, up_other, up_keep, down_moved, back_keep, back_other, out_send
-    )
-
-    joint_keep, joint_send = sum_halves(joint_keep, joint_other, mesh)
-    joint_other = swap(joint_send, "zh")
+    joint_send, back_other, out_send, output_send, up_other = fence(
+        joint_send, back_other, out_send, output_send, up_other
+    )
+    joint_other = far_swap(joint_send)
+    output_other = y_swap(output_send, mesh)
     up_moved = to_owner(up_keep + up_other.astype(F32))
     out_other = swap(out_send, "c")
     back = fold_first(back_keep, back_other)
-    output_grad = dot(attended_low, grad_all, 0, 0).astype(BF16)
-    joint_other, joint_keep, up_moved, out_other, back, output_grad = fence(
-        joint_other, joint_keep, up_moved, out_other, back, output_grad
+    joint_other, joint_keep, up_moved, out_other, back, output_other = fence(
+        joint_other, joint_keep, up_moved, out_other, back, output_other
     )
 
     joint_moved = to_owner(joint_keep + joint_other.astype(F32))
     produced = fold_second(back)
     out = fold_first(out_keep, out_other)
-    output_weight_grad = rows_sum(
-        output_grad.reshape(1, 1, 2, 1, mesh.shape["y"], own_rows, width), mesh
-    ).reshape(own_rows, width)
+    output_weight_grad = y_finish(output_keep, output_other, mesh).reshape(own_rows, width)
     joint_moved, out, produced = fence(joint_moved, out, produced)
+    produced = after(produced, out[1], out[3])
     layer_sum = fold_second(out)
     layer_out = (own_tokens.astype(F32) + output_full + down_full + layer_sum).astype(BF16)
     own_wide = own_tokens.astype(F32)
@@ -878,7 +938,7 @@
         jnp.sum(produced, 0),
     ]
     sums = jnp.concatenate([v.reshape(devices, -1) for v in sums], 1)
-    sums = lax.all_to_all(sums, ALL, 0, 0, tiled=True)
+    sums = lax.all_to_all(after(sums, layer_sum), ALL, 0, 0, tiled=True)
     sums = jnp.sum(sums, 0)
     joint_bias_grad = sums[: cuts[1]]
     up_bias_grad = sums[cuts[1] : cuts[2]]

time: 610 us -> 568 us (0.931)
  local copies, waits for them, and re-layouts: 48.2 us -> 29.8 us
  starting transfers between devices: 76.6 us -> 66.3 us
  matrix products: 6.81 us -> 0 us
    ppermute x43 -> x44, waiting for transfers between devices: 187 us -> 142 us  [swap(): return lax.ppermute(value, axis, [(0, 1), (1, 0)])]
    all_to_all x1, waiting for transfers between devices: 8.33 us -> 41.4 us  [spread(): lax.all_to_all(jnp.broadcast_to(value[None], (devices,) + value.shape), A...]
    add x7 -> x6, other arithmetic: 25.3 us -> 11.9 us  [the longest x2 6.24 us: part(): keep[x, zl, :, columns].astype(F32) + other[x, zl, :, columns].astype(F32)]
    convert_element_type x8 -> x1, local copies, waits for them, and re-layouts: 11.8 us -> 0.73 us  [y_finish(): pick(other, 1 - place, 0).astype(BF16)]
    convert_element_type x0 -> x2, other arithmetic: none -> 10.1 us  [fold_first(): (part(1, 0, two) + other_two[1].astype(F32)).astype(BF16)]
    dot_general x1 -> x0, matrix products: 6.81 us -> none  [dot(): lax.dot_general(left, right, (((left_dim,), (right_dim,)), ((), ())), pre...]
    ppermute x43 -> x44, starting transfers between devices: 43.8 us -> 42.4 us  [swap(): return lax.ppermute(value, axis, [(0, 1), (1, 0)])]
  transfers between devices with their start and end apart: 50 -> 50, of which waited for: 22 -> 22; matrix products, arithmetic and copies ran while one was open for 16% -> 14% of each run, Pallas kernels for 30% -> 37%
where the time goes in v3:
time: 568 us; the launch traced here: 557 us
  Pallas kernels  207 us (36%)
  waiting for transfers between devices  192 us (34%)
  starting transfers between devices  66.3 us (12%)
  other arithmetic  59.6 us (10%)
  local copies, waits for them, and re-layouts  29.8 us (5%)
    ppermute x44, waiting for transfers between devices, swap(): return lax.ppermute(value, axis, [(0, 1), (1, 0)])  142 us
    ppermute x44, starting transfers between devices, swap(): return lax.ppermute(value, axis, [(0, 1), (1, 0)])  42.4 us
    pallas_call x2, Pallas kernels, pair_product(): pl.pallas_call(functools.partial(pair_kernel, dims, (len(first), len(seco...  41.5 us
    all_to_all x1, waiting for transfers between devices, spread(): lax.all_to_all(jnp.broadcast_to(value[None], (devices,) + value.shape), A...  41.4 us
    pallas_call x3, Pallas kernels, weight_grad(): pl.pallas_call(weight_grad_kernel, grid=(8,), in_specs=[SCALARS] + specs,...  40.9 us
    pallas_call x1, Pallas kernels, attend(): pl.pallas_call(attend_kernel, grid_spec=pltpu.PrefetchScalarGridSpec(num_...  33.2 us
    pallas_call x2, Pallas kernels, rows_of_team(): pl.pallas_call(kernel, grid=(8,), in_specs=[pl.BlockSpec(value.shape, lam...  21.9 us
    pallas_call x1, Pallas kernels, hidden_backward(): pl.pallas_call(hidden_grad_kernel, grid=(count // block,), in_specs=[SCAL...  19.8 us
  transfers between devices with their start and end apart: 50, of which 22 were waited for; matrix products, arithmetic and copies ran while one was open for 14% of the time, Pallas kernels for 37%

profile of v3, /device:TPU:0, one launch (start us, length us, event | category | flops | bytes accessed | tf_op | source)
XLA Modules:
  0.0 556.9 jit_solution(1306550273110674955)
XLA Ops:
  0.6 3.6 shard_map.229
  4.3 5.4 all-to-all-start
  9.7 2.7 collective-permute-start
  12.3 1.5 collective-permute-start.1
  13.9 2.0 collective-permute-start.6
  16.0 31.3 %collective-permute-done = bf16[1,1,64,2048]{3,2,1,0:T(8,128)(2,1)S(1)} collective-permute-done((bf16[1,1,64,2048]{3,2,1,0:T(8,128)(2,1)S(1)}, bf16[1,1,64,2048]{3,2,1,0:T(8,128)(2,1)S(1)}, u32[]{:S(2)}, u32[]{:S(2)}) %collective-permute-start) | collective-permute-done | bytes 262176 | tf_op jit(solution)/shard_map/ppermute | solution.py:41
  47.3 2.6 all-to-all-done
  49.9 1.5 copy-done.2
  51.4 1.9 fusion.36
  54.3 1.5 collective-permute-start.3
  55.8 1.6 collective-permute-start.4
  57.4 1.7 collective-permute-start.5
  59.8 2.8 all-to-all-start.1
  62.7 2.1 slice.173.refs_0_
  64.8 2.1 collective-permute-done.6.refs_2_
  66.9 41.4 %all-to-all-done.1 = f32[32,10,128]{2,1,0:T(8,128)S(1)} async-done(((f32[32,10,128]{2,1,0:T(8,128)}), f32[32,10,128]{2,1,0:T(8,128)S(1)}, u32[]{:S(2)}, u32[]{:S(2)}) %all-to-all-start.1) | async-done | bytes 163872 | tf_op jit(solution)/shard_map/all_to_all | solution.py:150
  113.1 1.9 collective-permute-start.11
  115.2 1.6 fusion.29
  122.9 3.0 pad_maximum_fusion.1
  125.9 31.7 %collective-permute-done.7.refs_1_ = bf16[4,2,64,1024]{3,2,1,0:T(8,128)(2,1)} collective-permute-done((bf16[4,2,64,1024]{3,2,1,0:T(8,128)(2,1)S(1)}, bf16[4,2,64,1024]{3,2,1,0:T(8,128)(2,1)}, u32[]{:S(2)}, u32[]{:S(2)}) %collective-permute-start.7) | collective-permute-done | bytes 1048608 | tf_op jit(solution)/shard_map/ppermute | solution.py:41
  170.1 11.3 %shard_map.230.normed.left = bf16[2048,2048]{1,0:T(8,128)(2,1)} custom-call(bf16[256,2048]{1,0:T(8,128)(2,1)} %bitcast.167, bf16[256,2048]{1,0:T(8,128)(2,1)} %collective-permute-done.4.refs_1_, bf16[256,2048]{1,0:T(8,128)(2,1)} %collective-permute-done.5.refs_2_, bf16[256,2048]{1,0:T(8,128)(2,1)} %collective-permute-done.10.refs_3_, ...), custom_call_target="tpu_custom_call" | custom-call | tf_op jit(solution)/shard_map/pallas_call | solution.py:502
  181.4 17.5 %shard_map.231 = (f32[2048,1024]{1,0:T(8,128)}, bf16[2048,1024]{1,0:T(8,128)(2,1)}) custom-call(s32[2]{0:T(128)} %pad_add_fusion.place, bf16[2048,2048]{1,0:T(8,128)(2,1)} %shard_map.230.normed.left, f32[1,1024]{1,0:T(1,128)} %dynamic-slice_bitcast_fusion.4.bias, bf16[4,2,64,1024]{3,2,1,0:T(8,128)(2,1)} %copy-done.4, ...), custom_call_target="tpu_custom_call" | custom-call | tf_op jit(solution)/shard_map/pallas_call | solution.py:237
  198.9 14.1 %collective-permute-done.20 = bf16[1,1,64,2048]{3,2,1,0:T(8,128)(2,1)} collective-permute-done((bf16[1,1,64,2048]{3,2,1,0:T(8,128)(2,1)S(1)}, bf16[1,1,64,2048]{3,2,1,0:T(8,128)(2,1)}, u32[]{:S(2)}, u32[]{:S(2)}) %collective-permute-start.20) | collective-permute-done | bytes 262176 | tf_op jit(solution)/shard_map/ppermute | solution.py:41
  217.1 1.6 collective-permute-done.21.refs_4_
  219.0 1.5 collective-permute-done.24.refs_7_
  221.7 10.5 %shard_map.232 = (bf16[2048,2048]{1,0:T(8,128)(2,1)}, bf16[2048,256]{1,0:T(8,128)(2,1)}) custom-call(bf16[256,2048]{1,0:T(8,128)(2,1)} %bitcast.194, bf16[256,2048]{1,0:T(8,128)(2,1)} %collective-permute-done.11.refs_1_, bf16[256,2048]{1,0:T(8,128)(2,1)} %collective-permute-done.6.refs_2_, bf16[256,2048]{1,0:T(8,128)(2,1)} %collective-permute-done.19.refs_3_, ...), custom_call_target="tpu_custom_call" | custom-call | tf_op jit(solution)/shard_map/pallas_call | solution.py:502
  232.2 14.2 %shard_map.233 = (bf16[4,2,2,64,1024]{4,3,2,1,0:T(8,128)(2,1)}, bf16[4,2,2,64,1024]{4,3,2,1,0:T(8,128)(2,1)}) custom-call(s32[2]{0:T(128)} %pad_add_fusion.place, bf16[2048,2048]{1,0:T(8,128)(2,1)} %get-tuple-element.191.left.grad.right, bf16[2048,1024]{1,0:T(8,128)(2,1)} %get-tuple-element.221.right.one), custom_call_target="tpu_custom_call" | custom-call | tf_op jit(solution)/shard_map/pallas_call | solution.py:334
  248.8 19.8 %shard_map.234 = (bf16[2048,1024]{1,0:T(8,128)(2,1)}, f32[1,1024]{1,0:T(1,128)}) custom-call(s32[2]{0:T(128)} %pad_add_fusion.place, bf16[2048,2048]{1,0:T(8,128)(2,1)} %get-tuple-element.191.left.grad.right, f32[2048,1024]{1,0:T(8,128)} %get-tuple-element.192.pre, bf16[4,2,64,1024]{3,2,1,0:T(8,128)(2,1)} %copy-done.5, ...), custom_call_target="tpu_custom_call" | custom-call | tf_op jit(solution)/shard_map/pallas_call | solution.py:279
  268.6 14.2 %shard_map.235 = (bf16[4,2,2,64,1024]{4,3,2,1,0:T(8,128)(2,1)}, bf16[4,2,2,64,1024]{4,3,2,1,0:T(8,128)(2,1)}) custom-call(s32[2]{0:T(128)} %pad_add_fusion.place, bf16[2048,2048]{1,0:T(8,128)(2,1)} %shard_map.230.normed.left, bf16[2048,1024]{1,0:T(8,128)(2,1)} %get-tuple-element.219.right.two), custom_call_target="tpu_custom_call" | custom-call | tf_op jit(solution)/shard_map/pallas_call | solution.py:334
  282.8 14.1 %shard_map.236 = bf16[2048,768]{1,0:T(8,128)(2,1)} custom-call(s32[2]{0:T(128)} %pad_add_fusion.place, bf16[2048,2048]{1,0:T(8,128)(2,1)} %shard_map.230.normed.left, f32[1,768]{1,0:T(1,128)} %bitcast.213, f32[2048,128]{1,0:T(8,128)} %bitcast.184, f32[2048,128]{1,0:T(8,128)} %bitcast.185, bf16[4,2,64,768]{3,2,1,0:T(8,128)(2,1)} %slice.173.refs_0_, ...), custom_call_target="tpu_custom_call" | custom-call | tf_op jit(solution)/shard_map/pallas_call | solution.py:413
  298.1 2.5 convert_add_fusion.1
  301.4 33.2 %shard_map.237 = (bf16[4,2,256,256]{3,2,1,0:T(8,128)(2,1)}, bf16[4,2,256,768]{3,2,1,0:T(8,128)(2,1)}) custom-call(s32[4]{0:T(128)} %fusion.34.order, bf16[4,2,256,768]{3,2,1,0:T(8,128)(2,1)} %bitcast.164, bf16[4,2,256,768]{3,2,1,0:T(8,128)(2,1)} %bitcast.165, bf16[4,2,256,768]{3,2,1,0:T(8,128)(2,1)} %bitcast.166, bf16[4,2,256,256]{3,2,1,0:T(8,128)(2,1)} %bitcast.200, ...), custom_call_target="tpu_custom_call" | custom-call | tf_op jit(solution)/shard_map/pallas_call | solution.py:674
  334.6 12.5 %shard_map.238 = (bf16[4,2,2,64,768]{4,3,2,1,0:T(8,128)(2,1)}, bf16[4,2,2,64,768]{4,3,2,1,0:T(8,128)(2,1)}) custom-call(s32[2]{0:T(128)} %pad_add_fusion.place, bf16[2048,2048]{1,0:T(8,128)(2,1)} %shard_map.230.normed.left, bf16[2048,768]{1,0:T(8,128)(2,1)} %bitcast.171), custom_call_target="tpu_custom_call" | custom-call | tf_op jit(solution)/shard_map/pallas_call | solution.py:334
  349.3 3.9 all-to-all-start.2
  354.4 2.5 convert_add_fusion
  358.1 1.9 collective-permute-start.30
  360.0 23.4 %shard_map.239 = (bf16[1024,2048]{1,0:T(8,128)(2,1)}, bf16[1024,2048]{1,0:T(8,128)(2,1)}) custom-call(s32[2]{0:T(128)} %pad_add_fusion.place, bf16[2048,768]{1,0:T(8,128)(2,1)} %bitcast.172, bf16[2048,1024]{1,0:T(8,128)(2,1)} %get-tuple-element.219.right.two, bf16[4,2,64,768]{3,2,1,0:T(8,128)(2,1)} %slice.173.refs_0_, bf16[4,2,64,768]{3,2,1,0:T(8,128)(2,1)} %copy-done.19, ...), custom_call_target="tpu_custom_call" | custom-call | tf_op jit(solution)/shard_map/pallas_call | solution.py:456
  383.3 18.2 %shard_map.240 = (bf16[1024,2048]{1,0:T(8,128)(2,1)}, bf16[1024,2048]{1,0:T(8,128)(2,1)}) custom-call(s32[2]{0:T(128)} %pad_add_fusion.place, bf16[2048,1024]{1,0:T(8,128)(2,1)} %get-tuple-element.221.right.one, bf16[2048,256]{1,0:T(8,128)(2,1)} %bitcast.197, bf16[4,2,64,1024]{3,2,1,0:T(8,128)(2,1)} %copy-done.5, ...), custom_call_target="tpu_custom_call" | custom-call | tf_op jit(solution)/shard_map/pallas_call | solution.py:456
  401.5 6.9 %shard_map.241 = (bf16[2,64,2048]{2,1,0:T(8,128)(2,1)}, bf16[2,64,2048]{2,1,0:T(8,128)(2,1)}) custom-call(s32[2]{0:T(128)} %pad_add_fusion.place, bf16[2048,256]{1,0:T(8,128)(2,1)} %bitcast.198, bf16[2048,2048]{1,0:T(8,128)(2,1)} %get-tuple-element.191.left.grad.right), custom_call_target="tpu_custom_call" | custom-call | tf_op jit(solution)/shard_map/pallas_call | solution.py:380
  409.6 2.3 convert_add_fusion.2
  412.9 3.2 collective-permute-done.31
  416.4 3.3 add_convert_fusion
  419.8 4.3 all-to-all-start.3
  424.0 3.1 fusion.22
  428.2 1.9 collective-permute-start.34
  437.7 2.4 convert_reduce_fusion
  440.3 2.7 shard_map.244
  443.0 1.6 dynamic-slice_bitcast_fusion.2
  444.6 31.1 %collective-permute-done.32 = bf16[2,2,2,64,768]{4,3,2,1,0:T(8,128)(2,1)} collective-permute-done((bf16[2,2,2,64,768]{4,3,2,1,0:T(8,128)(2,1)S(1)}, bf16[2,2,2,64,768]{4,3,2,1,0:T(8,128)(2,1)}, u32[]{:S(2)}, u32[]{:S(2)}) %collective-permute-start.32) | collective-permute-done | bytes 786464 | tf_op jit(solution)/shard_map/ppermute | solution.py:41
  475.6 2.4 collective-permute-done.35
  478.0 5.2 fusion.17
  485.9 3.1 fusion.26
  492.6 2.3 add_convert_fusion.2
  494.9 4.5 all-to-all-start.4
  503.5 2.7 shard_map.243
  508.9 12.9 %collective-permute-done.37 = bf16[2,256,1024]{2,1,0:T(8,128)(2,1)} collective-permute-done((bf16[2,256,1024]{2,1,0:T(8,128)(2,1)}, bf16[2,256,1024]{2,1,0:T(8,128)(2,1)}, u32[]{:S(2)}, u32[]{:S(2)}) %collective-permute-start.37) | collective-permute-done | bytes 1048608 | tf_op jit(solution)/shard_map/ppermute | solution.py:41
  521.8 4.7 collective-permute-done.38
  526.5 4.8 fusion.15
  531.4 2.1 all-to-all-done.4.value
  535.8 2.1 convert_reduce_fusion.2
  539.0 3.2 all-to-all-start.5
  542.1 1.9 bitcast_add_fusion
  544.0 2.5 shard_map.242
  546.5 3.8 all-to-all-done.5
  (252 shorter events, 73.6 us)
Async XLA Ops:
  4.3 45.6 %all-to-all-start = ((bf16[8,64,2816]{2,1,0:T(8,128)(2,1)}), bf16[8,64,2816]{2,1,0:T(8,128)(2,1)S(1)}, u32[]{:S(2)}, u32[]{:S(2)}) async-start(bf16[8,64,2816]{2,1,0:T(8,128)(2,1)} %shard_map.229), calls=%async_computation | async-start | bytes 5767168 | tf_op jit(solution)/shard_map/all_to_all | solution.py:60
  9.7 37.6 %collective-permute-start = (bf16[1,1,64,2048]{3,2,1,0:T(8,128)(2,1)S(1)}, bf16[1,1,64,2048]{3,2,1,0:T(8,128)(2,1)S(1)}, u32[]{:S(2)}, u32[]{:S(2)}) collective-permute-start(bf16[1,1,64,2048]{3,2,1,0:T(8,128)(2,1)S(1)} %bitcast.205), channel_id=1, source_target_pairs={{0,4},{4,0},{1,5},{5,1},{2,6},{6,2},{3,7},{7,3},{8,12},{12,8},{9,1... | collective-permute-start | bytes 786440 | tf_op jit(solution)/shard_map/ppermute | solution.py:41
  12.3 35.0 %collective-permute-start.1 = (bf16[1,1,64,2048]{3,2,1,0:T(8,128)(2,1)S(1)}, bf16[1,1,64,2048]{3,2,1,0:T(8,128)(2,1)}, u32[]{:S(2)}, u32[]{:S(2)}) collective-permute-start(bf16[1,1,64,2048]{3,2,1,0:T(8,128)(2,1)S(1)} %bitcast.206), channel_id=1, source_target_pairs={{0,1},{1,0},{2,3},{3,2},{4,5},{5,4},{6,7},{7,6},{8,9},{9,8},{10,11... | collective-permute-start | bytes 786440 | tf_op jit(solution)/shard_map/ppermute | solution.py:41
  13.9 53.0 %collective-permute-start.6 = (bf16[256,2048]{1,0:T(8,128)(2,1)}, bf16[256,2048]{1,0:T(8,128)(2,1)}, u32[]{:S(2)}, u32[]{:S(2)}) collective-permute-start(bf16[256,2048]{1,0:T(8,128)(2,1)} %bitcast.192), channel_id=1, source_target_pairs={{0,16},{16,0},{1,17},{17,1},{2,18},{18,2},{3,19},{19,3},{4,20},{20... | collective-permute-start | bytes 3145736 | tf_op jit(solution)/shard_map/ppermute | solution.py:41
  47.3 12.6 %copy-start.32 = (bf16[1,1,64,2048]{3,2,1,0:T(8,128)(2,1)}, bf16[1,1,64,2048]{3,2,1,0:T(8,128)(2,1)S(1)}, u32[]{:S(2)}) copy-start(bf16[1,1,64,2048]{3,2,1,0:T(8,128)(2,1)S(1)} %collective-permute-done) | copy-start | bytes 786436
  53.3 63.5 %copy-start.4 = (bf16[4,2,64,1024]{3,2,1,0:T(8,128)(2,1)}, bf16[4,2,64,1024]{3,2,1,0:T(8,128)(2,1)S(1)}, u32[]{:S(2)}) copy-start(bf16[4,2,64,1024]{3,2,1,0:T(8,128)(2,1)S(1)} %get-tuple-element.283.refs_0_.refs_4_) | copy-start | bytes 3145732
  53.4 63.5 %copy-start.5 = (bf16[4,2,64,1024]{3,2,1,0:T(8,128)(2,1)}, bf16[4,2,64,1024]{3,2,1,0:T(8,128)(2,1)S(1)}, u32[]{:S(2)}) copy-start(bf16[4,2,64,1024]{3,2,1,0:T(8,128)(2,1)S(1)} %get-tuple-element.141.refs_0_) | copy-start | bytes 3145732
  53.4 54.9 %collective-permute-start.2 = (bf16[4,2,64,1024]{3,2,1,0:T(8,128)(2,1)S(1)}, bf16[4,2,64,1024]{3,2,1,0:T(8,128)(2,1)}, u32[]{:S(2)}, u32[]{:S(2)}) collective-permute-start(bf16[4,2,64,1024]{3,2,1,0:T(8,128)(2,1)S(1)} %get-tuple-element.283.refs_0_.refs_4_), channel_id=1, source_target_pairs={{0,4},{4,0},{1,5},{5,1},{2,6},{6,2},{3,7},{7,3},{8,12},{12,8},{9,1... | collective-permute-start | bytes 3145736 | tf_op jit(solution)/shard_map/ppermute | solution.py:41
  54.3 54.0 %collective-permute-start.3 = (bf16[4,2,64,1024]{3,2,1,0:T(8,128)(2,1)S(1)}, bf16[4,2,64,1024]{3,2,1,0:T(8,128)(2,1)}, u32[]{:S(2)}, u32[]{:S(2)}) collective-permute-start(bf16[4,2,64,1024]{3,2,1,0:T(8,128)(2,1)S(1)} %get-tuple-element.283.refs_0_.refs_4_), channel_id=1, source_target_pairs={{0,1},{1,0},{2,3},{3,2},{4,5},{5,4},{6,7},{7,6},{8,9},{9,8},{10,11... | collective-permute-start | bytes 3145736 | tf_op jit(solution)/shard_map/ppermute | solution.py:41
  55.8 52.4 %collective-permute-start.4 = (bf16[256,2048]{1,0:T(8,128)(2,1)S(1)}, bf16[256,2048]{1,0:T(8,128)(2,1)}, u32[]{:S(2)}, u32[]{:S(2)}) collective-permute-start(bf16[256,2048]{1,0:T(8,128)(2,1)S(1)} %bitcast.168), channel_id=1, source_target_pairs={{0,2},{2,0},{1,3},{3,1},{4,6},{6,4},{5,7},{7,5},{8,10},{10,8},{9,1... | collective-permute-start | bytes 3145736 | tf_op jit(solution)/shard_map/ppermute | solution.py:41
  57.4 50.8 %collective-permute-start.5 = (bf16[256,2048]{1,0:T(8,128)(2,1)S(1)}, bf16[256,2048]{1,0:T(8,128)(2,1)}, u32[]{:S(2)}, u32[]{:S(2)}) collective-permute-start(bf16[256,2048]{1,0:T(8,128)(2,1)S(1)} %bitcast.169), channel_id=1, source_target_pairs={{0,16},{16,0},{1,17},{17,1},{2,18},{18,2},{3,19},{19,3},{4,20},{20... | collective-permute-start | bytes 3145736 | tf_op jit(solution)/shard_map/ppermute | solution.py:41
  59.8 48.4 %all-to-all-start.1 = ((f32[32,10,128]{2,1,0:T(8,128)}), f32[32,10,128]{2,1,0:T(8,128)S(1)}, u32[]{:S(2)}, u32[]{:S(2)}) async-start(f32[32,10,128]{2,1,0:T(8,128)} %broadcast_in_dim.14), calls=%async_computation.1 | async-start | bytes 524288 | tf_op jit(solution)/shard_map/all_to_all | solution.py:150
  109.0 48.6 %collective-permute-start.7 = (bf16[4,2,64,1024]{3,2,1,0:T(8,128)(2,1)S(1)}, bf16[4,2,64,1024]{3,2,1,0:T(8,128)(2,1)}, u32[]{:S(2)}, u32[]{:S(2)}) collective-permute-start(bf16[4,2,64,1024]{3,2,1,0:T(8,128)(2,1)S(1)} %get-tuple-element.141.refs_0_), channel_id=1, source_target_pairs={{0,4},{4,0},{1,5},{5,1},{2,6},{6,2},{3,7},{7,3},{8,12},{12,8},{9,1... | collective-permute-start | bytes 3145736 | tf_op jit(solution)/shard_map/ppermute | solution.py:41
  110.3 47.3 %collective-permute-start.8 = (bf16[4,2,64,1024]{3,2,1,0:T(8,128)(2,1)S(1)}, bf16[4,2,64,1024]{3,2,1,0:T(8,128)(2,1)}, u32[]{:S(2)}, u32[]{:S(2)}) collective-permute-start(bf16[4,2,64,1024]{3,2,1,0:T(8,128)(2,1)S(1)} %get-tuple-element.141.refs_0_), channel_id=1, source_target_pairs={{0,1},{1,0},{2,3},{3,2},{4,5},{5,4},{6,7},{7,6},{8,9},{9,8},{10,11... | collective-permute-start | bytes 3145736 | tf_op jit(solution)/shard_map/ppermute | solution.py:41
  111.3 46.9 %collective-permute-start.10 = (bf16[256,2048]{1,0:T(8,128)(2,1)}, bf16[256,2048]{1,0:T(8,128)(2,1)}, u32[]{:S(2)}, u32[]{:S(2)}) collective-permute-start(bf16[256,2048]{1,0:T(8,128)(2,1)} %collective-permute-done.4.refs_1_), channel_id=1, source_target_pairs={{0,16},{16,0},{1,17},{17,1},{2,18},{18,2},{3,19},{19,3},{4,20},{20... | collective-permute-start | bytes 3145736 | tf_op jit(solution)/shard_map/ppermute | solution.py:41
  112.1 46.1 %collective-permute-start.9 = (bf16[4,2,64,1024]{3,2,1,0:T(8,128)(2,1)}, bf16[4,2,64,1024]{3,2,1,0:T(8,128)(2,1)}, u32[]{:S(2)}, u32[]{:S(2)}) collective-permute-start(bf16[4,2,64,1024]{3,2,1,0:T(8,128)(2,1)} %collective-permute-done.2.refs_1_.refs_5_), channel_id=1, source_target_pairs={{0,1},{1,0},{2,3},{3,2},{4,5},{5,4},{6,7},{7,6},{8,9},{9,8},{10,11... | collective-permute-start | bytes 3145736 | tf_op jit(solution)/shard_map/ppermute | solution.py:41
  113.1 46.2 %collective-permute-start.11 = (bf16[256,2048]{1,0:T(8,128)(2,1)}, bf16[256,2048]{1,0:T(8,128)(2,1)}, u32[]{:S(2)}, u32[]{:S(2)}) collective-permute-start(bf16[256,2048]{1,0:T(8,128)(2,1)} %bitcast.193), channel_id=1, source_target_pairs={{0,2},{2,0},{1,3},{3,1},{4,6},{6,4},{5,7},{7,5},{8,10},{10,8},{9,1... | collective-permute-start | bytes 3145736 | tf_op jit(solution)/shard_map/ppermute | solution.py:41
  122.9 44.6 %copy-start.6 = (bf16[4,2,64,768]{3,2,1,0:T(8,128)(2,1)S(1)}, bf16[4,2,64,768]{3,2,1,0:T(8,128)(2,1)}, u32[]{:S(2)}) copy-start(bf16[4,2,64,768]{3,2,1,0:T(8,128)(2,1)} %slice.173.refs_0_) | copy-start | bytes 2359300
  122.9 45.5 %copy-start.33 = (bf16[1,1,64,2048]{3,2,1,0:T(8,128)(2,1)S(1)}, bf16[1,1,64,2048]{3,2,1,0:T(8,128)(2,1)}, u32[]{:S(2)}) copy-start(bf16[1,1,64,2048]{3,2,1,0:T(8,128)(2,1)} %copy-done.32) | copy-start | bytes 786436
  157.6 4.1 collective-permute-start.12
  157.6 4.4 collective-permute-start.13
  158.1 5.4 collective-permute-start.14
  161.3 3.6 collective-permute-start.15
  165.0 48.6 %collective-permute-start.18 = (bf16[4,2,64,1024]{3,2,1,0:T(8,128)(2,1)}, bf16[4,2,64,1024]{3,2,1,0:T(8,128)(2,1)S(1)}, u32[]{:S(2)}, u32[]{:S(2)}) collective-permute-start(bf16[4,2,64,1024]{3,2,1,0:T(8,128)(2,1)} %collective-permute-done.7.refs_1_), channel_id=1, source_target_pairs={{0,1},{1,0},{2,3},{3,2},{4,5},{5,4},{6,7},{7,6},{8,9},{9,8},{10,11... | collective-permute-start | bytes 3145736 | tf_op jit(solution)/shard_map/ppermute | solution.py:41
  166.2 48.2 %collective-permute-start.19 = (bf16[256,2048]{1,0:T(8,128)(2,1)}, bf16[256,2048]{1,0:T(8,128)(2,1)}, u32[]{:S(2)}, u32[]{:S(2)}) collective-permute-start(bf16[256,2048]{1,0:T(8,128)(2,1)} %collective-permute-done.11.refs_1_), channel_id=1, source_target_pairs={{0,16},{16,0},{1,17},{17,1},{2,18},{18,2},{3,19},{19,3},{4,20},{20... | collective-permute-start | bytes 3145736 | tf_op jit(solution)/shard_map/ppermute | solution.py:41
  167.4 45.5 %collective-permute-start.16 = (bf16[4,2,64,768]{3,2,1,0:T(8,128)(2,1)S(1)}, bf16[4,2,64,768]{3,2,1,0:T(8,128)(2,1)S(1)}, u32[]{:S(2)}, u32[]{:S(2)}) collective-permute-start(bf16[4,2,64,768]{3,2,1,0:T(8,128)(2,1)S(1)} %copy-done.6), channel_id=1, source_target_pairs={{0,4},{4,0},{1,5},{5,1},{2,6},{6,2},{3,7},{7,3},{8,12},{12,8},{9,1... | collective-permute-start | bytes 2359304 | tf_op jit(solution)/shard_map/ppermute | solution.py:41
  167.4 46.0 %collective-permute-start.17 = (bf16[4,2,64,768]{3,2,1,0:T(8,128)(2,1)S(1)}, bf16[4,2,64,768]{3,2,1,0:T(8,128)(2,1)S(1)}, u32[]{:S(2)}, u32[]{:S(2)}) collective-permute-start(bf16[4,2,64,768]{3,2,1,0:T(8,128)(2,1)S(1)} %copy-done.6), channel_id=1, source_target_pairs={{0,1},{1,0},{2,3},{3,2},{4,5},{5,4},{6,7},{7,6},{8,9},{9,8},{10,11... | collective-permute-start | bytes 2359304 | tf_op jit(solution)/shard_map/ppermute | solution.py:41
  168.4 44.5 %collective-permute-start.20 = (bf16[1,1,64,2048]{3,2,1,0:T(8,128)(2,1)S(1)}, bf16[1,1,64,2048]{3,2,1,0:T(8,128)(2,1)}, u32[]{:S(2)}, u32[]{:S(2)}) collective-permute-start(bf16[1,1,64,2048]{3,2,1,0:T(8,128)(2,1)S(1)} %copy-done.33), channel_id=1, source_target_pairs={{0,1},{1,0},{2,3},{3,2},{4,5},{5,4},{6,7},{7,6},{8,9},{9,8},{10,11... | collective-permute-start | bytes 786440 | tf_op jit(solution)/shard_map/ppermute | solution.py:41
  181.4 32.1 %copy-start.14 = (bf16[1,256,2048]{2,1,0:T(8,128)(2,1)S(1)}, bf16[1,256,2048]{2,1,0:T(8,128)(2,1)}, u32[]{:S(2)}) copy-start(bf16[1,256,2048]{2,1,0:T(8,128)(2,1)} %param.27) | copy-start | bytes 3145732
  181.4 33.1 %copy-start.31 = (bf16[64,2048]{1,0:T(8,128)(2,1)S(1)}, bf16[64,2048]{1,0:T(8,128)(2,1)}, u32[]{:S(2)}) copy-start(bf16[64,2048]{1,0:T(8,128)(2,1)} %param.16) | copy-start | bytes 786436
  213.0 4.2 collective-permute-start.23
  213.0 6.0 %collective-permute-start.22 = (bf16[256,2048]{1,0:T(8,128)(2,1)}, bf16[256,2048]{1,0:T(8,128)(2,1)}, u32[]{:S(2)}, u32[]{:S(2)}) collective-permute-start(bf16[256,2048]{1,0:T(8,128)(2,1)} %collective-permute-done.11.refs_1_), channel_id=1, source_target_pairs={{0,8},{8,0},{1,9},{9,1},{2,10},{10,2},{3,11},{11,3},{4,12},{12,4},... | collective-permute-start | bytes 3145736 | tf_op jit(solution)/shard_map/ppermute | solution.py:41
  213.5 5.3 collective-permute-start.21
  214.4 6.1 %collective-permute-start.24 = (bf16[256,2048]{1,0:T(8,128)(2,1)}, bf16[256,2048]{1,0:T(8,128)(2,1)}, u32[]{:S(2)}, u32[]{:S(2)}) collective-permute-start(bf16[256,2048]{1,0:T(8,128)(2,1)} %collective-permute-done.19.refs_3_), channel_id=1, source_target_pairs={{0,8},{8,0},{1,9},{9,1},{2,10},{10,2},{3,11},{11,3},{4,12},{12,4},... | collective-permute-start | bytes 3145736 | tf_op jit(solution)/shard_map/ppermute | solution.py:41
  220.5 25.9 %collective-permute-start.25 = (bf16[4,2,64,768]{3,2,1,0:T(8,128)(2,1)S(1)}, bf16[4,2,64,768]{3,2,1,0:T(8,128)(2,1)S(1)}, u32[]{:S(2)}, u32[]{:S(2)}) collective-permute-start(bf16[4,2,64,768]{3,2,1,0:T(8,128)(2,1)S(1)} %collective-permute-done.16.refs_1_), channel_id=1, source_target_pairs={{0,1},{1,0},{2,3},{3,2},{4,5},{5,4},{6,7},{7,6},{8,9},{9,8},{10,11... | collective-permute-start | bytes 2359304 | tf_op jit(solution)/shard_map/ppermute | solution.py:41
  246.4 22.2 %copy-start.21 = (bf16[4,2,64,768]{3,2,1,0:T(8,128)(2,1)}, bf16[4,2,64,768]{3,2,1,0:T(8,128)(2,1)S(1)}, u32[]{:S(2)}) copy-start(bf16[4,2,64,768]{3,2,1,0:T(8,128)(2,1)S(1)} %collective-permute-done.25.refs_3_) | copy-start | bytes 2359300
  246.4 50.4 %collective-permute-start.26 = (bf16[4,2,2,64,1024]{4,3,2,1,0:T(8,128)(2,1)}, bf16[4,2,2,64,1024]{4,3,2,1,0:T(8,128)(2,1)}, u32[]{:S(2)}, u32[]{:S(2)}) collective-permute-start(bf16[4,2,2,64,1024]{4,3,2,1,0:T(8,128)(2,1)} %get-tuple-element.190), channel_id=1, source_target_pairs={{0,1},{1,0},{2,3},{3,2},{4,5},{5,4},{6,7},{7,6},{8,9},{9,8},{10,11... | collective-permute-start | bytes 6291464 | tf_op jit(solution)/shard_map/ppermute | solution.py:41
  282.8 15.3 %copy-start.23 = (bf16[4,2,2,64,1024]{4,3,2,1,0:T(8,128)(2,1)S(1)}, bf16[4,2,2,64,1024]{4,3,2,1,0:T(8,128)(2,1)}, u32[]{:S(2)}) copy-start(bf16[4,2,2,64,1024]{4,3,2,1,0:T(8,128)(2,1)} %get-tuple-element.209) | copy-start | bytes 6291460
  296.9 51.0 %collective-permute-start.27 = (bf16[4,2,2,64,1024]{4,3,2,1,0:T(8,128)(2,1)}, bf16[4,2,2,64,1024]{4,3,2,1,0:T(8,128)(2,1)}, u32[]{:S(2)}, u32[]{:S(2)}) collective-permute-start(bf16[4,2,2,64,1024]{4,3,2,1,0:T(8,128)(2,1)} %get-tuple-element.208), channel_id=1, source_target_pairs={{0,1},{1,0},{2,3},{3,2},{4,5},{5,4},{6,7},{7,6},{8,9},{9,8},{10,11... | collective-permute-start | bytes 6291464 | tf_op jit(solution)/shard_map/ppermute | solution.py:41
  300.8 47.1 %collective-permute-start.28 = (bf16[2,2,2,64,1024]{4,3,2,1,0:T(8,128)(2,1)S(1)}, bf16[2,2,2,64,1024]{4,3,2,1,0:T(8,128)(2,1)S(1)}, u32[]{:S(2)}, u32[]{:S(2)}) collective-permute-start(bf16[2,2,2,64,1024]{4,3,2,1,0:T(8,128)(2,1)S(1)} %fusion.12), channel_id=1, source_target_pairs={{0,4},{4,0},{1,5},{5,1},{2,6},{6,2},{3,7},{7,3},{8,12},{12,8},{9,1... | collective-permute-start | bytes 3145736 | tf_op jit(solution)/shard_map/ppermute | solution.py:41
  349.3 59.3 %all-to-all-start.2 = ((bf16[8,64,1024]{2,1,0:T(8,128)(2,1)}), bf16[8,64,1024]{2,1,0:T(8,128)(2,1)S(1)}, u32[]{:S(2)}, u32[]{:S(2)}) async-start(bf16[8,64,1024]{2,1,0:T(8,128)(2,1)} %bitcast.31), calls=%async_computation.2 | async-start | bytes 2097152 | tf_op jit(solution)/shard_map/all_to_all | solution.py:131
  353.1 55.5 %collective-permute-start.29 = (bf16[4,2,2,64,768]{4,3,2,1,0:T(8,128)(2,1)}, bf16[4,2,2,64,768]{4,3,2,1,0:T(8,128)(2,1)}, u32[]{:S(2)}, u32[]{:S(2)}) collective-permute-start(bf16[4,2,2,64,768]{4,3,2,1,0:T(8,128)(2,1)} %get-tuple-element.213), channel_id=1, source_target_pairs={{0,1},{1,0},{2,3},{3,2},{4,5},{5,4},{6,7},{7,6},{8,9},{9,8},{10,11... | collective-permute-start | bytes 4718600 | tf_op jit(solution)/shard_map/ppermute | solution.py:41
  358.1 50.5 %collective-permute-start.30 = (bf16[2,2,2,64,1024]{4,3,2,1,0:T(8,128)(2,1)}, bf16[2,2,2,64,1024]{4,3,2,1,0:T(8,128)(2,1)}, u32[]{:S(2)}, u32[]{:S(2)}) collective-permute-start(bf16[2,2,2,64,1024]{4,3,2,1,0:T(8,128)(2,1)} %fusion.13), channel_id=1, source_target_pairs={{0,4},{4,0},{1,5},{5,1},{2,6},{6,2},{3,7},{7,3},{8,12},{12,8},{9,1... | collective-permute-start | bytes 3145736 | tf_op jit(solution)/shard_map/ppermute | solution.py:41
  408.6 7.4 %collective-permute-start.31 = (bf16[1024,2048]{1,0:T(8,128)(2,1)}, bf16[1024,2048]{1,0:T(8,128)(2,1)S(1)}, u32[]{:S(2)}, u32[]{:S(2)}) collective-permute-start(bf16[1024,2048]{1,0:T(8,128)(2,1)} %get-tuple-element.227), channel_id=1, source_target_pairs={{0,8},{8,0},{1,9},{9,1},{2,10},{10,2},{3,11},{11,3},{4,12},{12,4},... | collective-permute-start | bytes 12582920 | tf_op jit(solution)/shard_map/ppermute | solution.py:41
  416.1 67.2 %collective-permute-start.33 = (bf16[1024,2048]{1,0:T(8,128)(2,1)}, bf16[1024,2048]{1,0:T(8,128)(2,1)}, u32[]{:S(2)}, u32[]{:S(2)}) collective-permute-start(bf16[1024,2048]{1,0:T(8,128)(2,1)} %get-tuple-element.234), channel_id=1, source_target_pairs={{0,8},{8,0},{1,9},{9,1},{2,10},{10,2},{3,11},{11,3},{4,12},{12,4},... | collective-permute-start | bytes 12582920 | tf_op jit(solution)/shard_map/ppermute | solution.py:41
  419.8 63.4 %all-to-all-start.3 = ((bf16[8,64,1024]{2,1,0:T(8,128)(2,1)}), bf16[8,64,1024]{2,1,0:T(8,128)(2,1)}, u32[]{:S(2)}, u32[]{:S(2)}) async-start(bf16[8,64,1024]{2,1,0:T(8,128)(2,1)} %bitcast.196), calls=%async_computation.3 | async-start | bytes 2097152 | tf_op jit(solution)/shard_map/all_to_all | solution.py:131
  428.2 47.4 %collective-permute-start.34 = (bf16[2,256,1024]{2,1,0:T(8,128)(2,1)}, bf16[2,256,1024]{2,1,0:T(8,128)(2,1)}, u32[]{:S(2)}, u32[]{:S(2)}) collective-permute-start(bf16[2,256,1024]{2,1,0:T(8,128)(2,1)} %pad_maximum_fusion.3), channel_id=1, source_target_pairs={{0,16},{16,0},{1,17},{17,1},{2,18},{18,2},{3,19},{19,3},{4,20},{20... | collective-permute-start | bytes 3145736 | tf_op jit(solution)/shard_map/ppermute | solution.py:41
  431.2 46.8 %collective-permute-start.35 = (bf16[2,256,1024]{2,1,0:T(8,128)(2,1)}, bf16[2,256,1024]{2,1,0:T(8,128)(2,1)}, u32[]{:S(2)}, u32[]{:S(2)}) collective-permute-start(bf16[2,256,1024]{2,1,0:T(8,128)(2,1)} %pad_maximum_fusion.4), channel_id=1, source_target_pairs={{0,2},{2,0},{1,3},{3,1},{4,6},{6,4},{5,7},{7,5},{8,10},{10,8},{9,1... | collective-permute-start | bytes 3145736 | tf_op jit(solution)/shard_map/ppermute | solution.py:41
  432.7 42.9 %collective-permute-start.32 = (bf16[2,2,2,64,768]{4,3,2,1,0:T(8,128)(2,1)S(1)}, bf16[2,2,2,64,768]{4,3,2,1,0:T(8,128)(2,1)}, u32[]{:S(2)}, u32[]{:S(2)}) collective-permute-start(bf16[2,2,2,64,768]{4,3,2,1,0:T(8,128)(2,1)S(1)} %copy-done.29), channel_id=1, source_target_pairs={{0,4},{4,0},{1,5},{5,1},{2,6},{6,2},{3,7},{7,3},{8,12},{12,8},{9,1... | collective-permute-start | bytes 2359304 | tf_op jit(solution)/shard_map/ppermute | solution.py:41
  436.9 46.3 %collective-permute-start.36 = (bf16[2,64,2048]{2,1,0:T(8,128)(2,1)}, bf16[2,64,2048]{2,1,0:T(8,128)(2,1)}, u32[]{:S(2)}, u32[]{:S(2)}) collective-permute-start(bf16[2,64,2048]{2,1,0:T(8,128)(2,1)} %get-tuple-element.237), channel_id=1, source_target_pairs={{0,1},{1,0},{2,3},{3,2},{4,5},{5,4},{6,7},{7,6},{8,9},{9,8},{10,11... | collective-permute-start | bytes 1572872 | tf_op jit(solution)/shard_map/ppermute | solution.py:41
  483.2 23.0 %collective-permute-start.39 = (bf16[256,1024]{1,0:T(8,128)(2,1)}, bf16[256,1024]{1,0:T(8,128)(2,1)}, u32[]{:S(2)}, u32[]{:S(2)}) collective-permute-start(bf16[256,1024]{1,0:T(8,128)(2,1)} %get-tuple-element.243), channel_id=1, source_target_pairs={{0,2},{2,0},{1,3},{3,1},{4,6},{6,4},{5,7},{7,5},{8,10},{10,8},{9,1... | collective-permute-start | bytes 1572872 | tf_op jit(solution)/shard_map/ppermute | solution.py:41
  484.4 23.1 %collective-permute-start.40 = (bf16[256,1024]{1,0:T(8,128)(2,1)S(1)}, bf16[256,1024]{1,0:T(8,128)(2,1)}, u32[]{:S(2)}, u32[]{:S(2)}) collective-permute-start(bf16[256,1024]{1,0:T(8,128)(2,1)S(1)} %get-tuple-element.245), channel_id=1, source_target_pairs={{0,16},{16,0},{1,17},{17,1},{2,18},{18,2},{3,19},{19,3},{4,20},{20... | collective-permute-start | bytes 1572872 | tf_op jit(solution)/shard_map/ppermute | solution.py:41
  490.0 31.8 %collective-permute-start.37 = (bf16[2,256,1024]{2,1,0:T(8,128)(2,1)}, bf16[2,256,1024]{2,1,0:T(8,128)(2,1)}, u32[]{:S(2)}, u32[]{:S(2)}) collective-permute-start(bf16[2,256,1024]{2,1,0:T(8,128)(2,1)} %pad_maximum_fusion.5), channel_id=1, source_target_pairs={{0,16},{16,0},{1,17},{17,1},{2,18},{18,2},{3,19},{19,3},{4,20},{20... | collective-permute-start | bytes 3145736 | tf_op jit(solution)/shard_map/ppermute | solution.py:41
  491.7 34.9 %collective-permute-start.38 = (bf16[2,256,1024]{2,1,0:T(8,128)(2,1)}, bf16[2,256,1024]{2,1,0:T(8,128)(2,1)}, u32[]{:S(2)}, u32[]{:S(2)}) collective-permute-start(bf16[2,256,1024]{2,1,0:T(8,128)(2,1)} %pad_maximum_fusion.6), channel_id=1, source_target_pairs={{0,2},{2,0},{1,3},{3,1},{4,6},{6,4},{5,7},{7,5},{8,10},{10,8},{9,1... | collective-permute-start | bytes 3145736 | tf_op jit(solution)/shard_map/ppermute | solution.py:41
  494.9 38.6 %all-to-all-start.4 = ((bf16[8,64,768]{2,1,0:T(8,128)(2,1)}), bf16[8,64,768]{2,1,0:T(8,128)(2,1)}, u32[]{:S(2)}, u32[]{:S(2)}) async-start(bf16[8,64,768]{2,1,0:T(8,128)(2,1)} %bitcast.50), calls=%async_computation.4 | async-start | bytes 1572864 | tf_op jit(solution)/shard_map/all_to_all | solution.py:131
  502.4 39.7 %collective-permute-start.43 = (bf16[64,2048]{1,0:T(8,128)(2,1)}, bf16[64,2048]{1,0:T(8,128)(2,1)S(1)}, u32[]{:S(2)}, u32[]{:S(2)}) collective-permute-start(bf16[64,2048]{1,0:T(8,128)(2,1)} %fusion.28), channel_id=1, source_target_pairs={{0,4},{4,0},{1,5},{5,1},{2,6},{6,2},{3,7},{7,3},{8,12},{12,8},{9,1... | collective-permute-start | bytes 786440 | tf_op jit(solution)/shard_map/ppermute | solution.py:41
  508.8 17.8 %copy-start.12 = (bf16[1024,2048]{1,0:T(8,128)(2,1)S(1)}, bf16[1024,2048]{1,0:T(8,128)(2,1)}, u32[]{:S(2)}) copy-start(bf16[1024,2048]{1,0:T(8,128)(2,1)} %get-tuple-element.240) | copy-start | bytes 12582916
  508.9 25.9 %copy-start.34 = (f32[2048]{0:T(1024)S(1)}, f32[2048]{0:T(1024)}, u32[]{:S(2)}) copy-start(f32[2048]{0:T(1024)} %mul.84) | copy-start | bytes 24580
  508.9 25.9 %copy-start.38 = (f32[256]{0:T(256)S(1)}, f32[256]{0:T(256)}, u32[]{:S(2)}) copy-start(f32[256]{0:T(256)} %copy-done.37) | copy-start | bytes 3076
  508.9 25.9 %copy-start.39 = (f32[256]{0:T(256)S(1)}, f32[256]{0:T(256)}, u32[]{:S(2)}) copy-start(f32[256]{0:T(256)} %add_rsqrt_fusion) | copy-start | bytes 3076
  533.5 18.6 %collective-permute-start.41 = (bf16[256,1024]{1,0:T(8,128)(2,1)}, bf16[256,1024]{1,0:T(8,128)(2,1)}, u32[]{:S(2)}, u32[]{:S(2)}) collective-permute-start(bf16[256,1024]{1,0:T(8,128)(2,1)} %get-tuple-element.247), channel_id=1, source_target_pairs={{0,2},{2,0},{1,3},{3,1},{4,6},{6,4},{5,7},{7,5},{8,10},{10,8},{9,1... | collective-permute-start | bytes 1572872 | tf_op jit(solution)/shard_map/ppermute | solution.py:41
  533.5 19.9 %collective-permute-start.42 = (bf16[256,1024]{1,0:T(8,128)(2,1)}, bf16[256,1024]{1,0:T(8,128)(2,1)}, u32[]{:S(2)}, u32[]{:S(2)}) collective-permute-start(bf16[256,1024]{1,0:T(8,128)(2,1)} %get-tuple-element.249), channel_id=1, source_target_pairs={{0,16},{16,0},{1,17},{17,1},{2,18},{18,2},{3,19},{19,3},{4,20},{20... | collective-permute-start | bytes 1572872 | tf_op jit(solution)/shard_map/ppermute | solution.py:41
  538.2 14.0 %copy-start.9 = (f32[256,1024]{1,0:T(8,128)S(1)}, f32[256,1024]{1,0:T(8,128)}, u32[]{:S(2)}) copy-start(f32[256,1024]{1,0:T(8,128)} %get-tuple-element.246) | copy-start | bytes 3145732
  539.0 11.3 %all-to-all-start.5 = ((f32[32,1,640]{2,1,0:T(1,128)}), f32[32,1,640]{2,1,0:T(1,128)S(1)}, u32[]{:S(2)}, u32[]{:S(2)}) async-start(f32[32,1,640]{2,1,0:T(1,128)} %all_to_all.26), calls=%async_computation.5 | async-start | bytes 163840 | tf_op jit(solution)/shard_map/all_to_all | solution.py:941
  (36 other events, 214.5 us)

commit v4 on v3

--- a/solution.py
+++ b/solution.py
@@ -888,9 +888,7 @@
 
     joint_keep, joint_send = sum_halves(joint_keep, joint_other, mesh)
     back_other = swap(back_send, "c")
-    joint_send, back_other, out_send, output_send, up_other = fence(
-        joint_send, back_other, out_send, output_send, up_other
-    )
+    joint_send, back_other = fence(joint_send, back_other)
     joint_other = far_swap(joint_send)
     output_other = y_swap(output_send, mesh)
     up_moved = to_owner(up_keep + up_other.astype(F32))

time: 568 us -> 561 us (0.988)
  waiting for transfers between devices: 192 us -> 185 us
    ppermute x44, waiting for transfers between devices: 142 us -> 136 us  [swap(): return lax.ppermute(value, axis, [(0, 1), (1, 0)])]
  transfers between devices with their start and end apart: 50 -> 50, of which waited for: 22 -> 21; matrix products, arithmetic and copies ran while one was open for 14% -> 14% of each run, Pallas kernels for 37% -> 37%
where the time goes in v4:
time: 561 us; the launch traced here: 550 us
  Pallas kernels  207 us (37%)
  waiting for transfers between devices  185 us (33%)
  starting transfers between devices  67.5 us (12%)
  other arithmetic  57.8 us (10%)
  local copies, waits for them, and re-layouts  30.2 us (5%)
    ppermute x44, waiting for transfers between devices, swap(): return lax.ppermute(value, axis, [(0, 1), (1, 0)])  136 us
    ppermute x44, starting transfers between devices, swap(): return lax.ppermute(value, axis, [(0, 1), (1, 0)])  42.9 us
    pallas_call x2, Pallas kernels, pair_product(): pl.pallas_call(functools.partial(pair_kernel, dims, (len(first), len(seco...  41.5 us
    all_to_all x1, waiting for transfers between devices, spread(): lax.all_to_all(jnp.broadcast_to(value[None], (devices,) + value.shape), A...  41.4 us
    pallas_call x3, Pallas kernels, weight_grad(): pl.pallas_call(weight_grad_kernel, grid=(8,), in_specs=[SCALARS] + specs,...  41 us
    pallas_call x1, Pallas kernels, attend(): pl.pallas_call(attend_kernel, grid_spec=pltpu.PrefetchScalarGridSpec(num_...  33.2 us
    pallas_call x2, Pallas kernels, rows_of_team(): pl.pallas_call(kernel, grid=(8,), in_specs=[pl.BlockSpec(value.shape, lam...  21.9 us
    pallas_call x1, Pallas kernels, hidden_backward(): pl.pallas_call(hidden_grad_kernel, grid=(count // block,), in_specs=[SCAL...  19.8 us
  transfers between devices with their start and end apart: 50, of which 21 were waited for; matrix products, arithmetic and copies ran while one was open for 14% of the time, Pallas kernels for 37%

profile of v4, /device:TPU:0, one launch (start us, length us, event | category | flops | bytes accessed | tf_op | source)
XLA Modules:
  0.0 550.1 jit_solution(4029524283591219730)
XLA Ops:
  0.6 3.6 shard_map.229
  4.3 5.4 all-to-all-start
  9.7 2.7 collective-permute-start
  12.3 1.5 collective-permute-start.1
  13.9 2.0 collective-permute-start.6
  16.0 31.3 %collective-permute-done = bf16[1,1,64,2048]{3,2,1,0:T(8,128)(2,1)S(1)} collective-permute-done((bf16[1,1,64,2048]{3,2,1,0:T(8,128)(2,1)S(1)}, bf16[1,1,64,2048]{3,2,1,0:T(8,128)(2,1)S(1)}, u32[]{:S(2)}, u32[]{:S(2)}) %collective-permute-start) | collective-permute-done | bytes 262176 | tf_op jit(solution)/shard_map/ppermute | solution.py:41
  47.3 2.6 all-to-all-done
  49.9 1.6 copy-done.2
  51.4 1.9 fusion.36
  54.3 1.5 collective-permute-start.3
  55.8 1.6 collective-permute-start.4
  57.4 1.7 collective-permute-start.5
  59.9 2.8 all-to-all-start.1
  62.7 2.1 slice.173.refs_0_
  64.8 2.1 collective-permute-done.6.refs_2_
  66.9 41.4 %all-to-all-done.1 = f32[32,10,128]{2,1,0:T(8,128)S(1)} async-done(((f32[32,10,128]{2,1,0:T(8,128)}), f32[32,10,128]{2,1,0:T(8,128)S(1)}, u32[]{:S(2)}, u32[]{:S(2)}) %all-to-all-start.1) | async-done | bytes 163872 | tf_op jit(solution)/shard_map/all_to_all | solution.py:150
  113.1 1.9 collective-permute-start.11
  115.2 1.6 fusion.29
  122.9 3.0 pad_maximum_fusion.1
  125.9 31.8 %collective-permute-done.7.refs_1_ = bf16[4,2,64,1024]{3,2,1,0:T(8,128)(2,1)} collective-permute-done((bf16[4,2,64,1024]{3,2,1,0:T(8,128)(2,1)S(1)}, bf16[4,2,64,1024]{3,2,1,0:T(8,128)(2,1)}, u32[]{:S(2)}, u32[]{:S(2)}) %collective-permute-start.7) | collective-permute-done | bytes 1048608 | tf_op jit(solution)/shard_map/ppermute | solution.py:41
  170.1 11.3 %shard_map.230.normed.left = bf16[2048,2048]{1,0:T(8,128)(2,1)} custom-call(bf16[256,2048]{1,0:T(8,128)(2,1)} %bitcast.167, bf16[256,2048]{1,0:T(8,128)(2,1)} %collective-permute-done.4.refs_1_, bf16[256,2048]{1,0:T(8,128)(2,1)} %collective-permute-done.5.refs_2_, bf16[256,2048]{1,0:T(8,128)(2,1)} %collective-permute-done.10.refs_3_, ...), custom_call_target="tpu_custom_call" | custom-call | tf_op jit(solution)/shard_map/pallas_call | solution.py:502
  181.4 17.5 %shard_map.231 = (f32[2048,1024]{1,0:T(8,128)}, bf16[2048,1024]{1,0:T(8,128)(2,1)}) custom-call(s32[2]{0:T(128)} %pad_add_fusion.place, bf16[2048,2048]{1,0:T(8,128)(2,1)} %shard_map.230.normed.left, f32[1,1024]{1,0:T(1,128)} %dynamic-slice_bitcast_fusion.4.bias, bf16[4,2,64,1024]{3,2,1,0:T(8,128)(2,1)} %copy-done.4, ...), custom_call_target="tpu_custom_call" | custom-call | tf_op jit(solution)/shard_map/pallas_call | solution.py:237
  198.9 14.1 %collective-permute-done.20 = bf16[1,1,64,2048]{3,2,1,0:T(8,128)(2,1)} collective-permute-done((bf16[1,1,64,2048]{3,2,1,0:T(8,128)(2,1)S(1)}, bf16[1,1,64,2048]{3,2,1,0:T(8,128)(2,1)}, u32[]{:S(2)}, u32[]{:S(2)}) %collective-permute-start.20) | collective-permute-done | bytes 262176 | tf_op jit(solution)/shard_map/ppermute | solution.py:41
  217.2 1.6 collective-permute-done.21.refs_4_
  219.0 1.5 collective-permute-done.24.refs_7_
  221.7 10.6 %shard_map.232 = (bf16[2048,2048]{1,0:T(8,128)(2,1)}, bf16[2048,256]{1,0:T(8,128)(2,1)}) custom-call(bf16[256,2048]{1,0:T(8,128)(2,1)} %bitcast.192, bf16[256,2048]{1,0:T(8,128)(2,1)} %collective-permute-done.11.refs_1_, bf16[256,2048]{1,0:T(8,128)(2,1)} %collective-permute-done.6.refs_2_, bf16[256,2048]{1,0:T(8,128)(2,1)} %collective-permute-done.19.refs_3_, ...), custom_call_target="tpu_custom_call" | custom-call | tf_op jit(solution)/shard_map/pallas_call | solution.py:502
  232.2 14.2 %shard_map.233 = (bf16[4,2,2,64,1024]{4,3,2,1,0:T(8,128)(2,1)}, bf16[4,2,2,64,1024]{4,3,2,1,0:T(8,128)(2,1)}) custom-call(s32[2]{0:T(128)} %pad_add_fusion.place, bf16[2048,2048]{1,0:T(8,128)(2,1)} %get-tuple-element.188.left.grad.right, bf16[2048,1024]{1,0:T(8,128)(2,1)} %get-tuple-element.218.right.one), custom_call_target="tpu_custom_call" | custom-call | tf_op jit(solution)/shard_map/pallas_call | solution.py:334
  248.9 19.8 %shard_map.234 = (bf16[2048,1024]{1,0:T(8,128)(2,1)}, f32[1,1024]{1,0:T(1,128)}) custom-call(s32[2]{0:T(128)} %pad_add_fusion.place, bf16[2048,2048]{1,0:T(8,128)(2,1)} %get-tuple-element.188.left.grad.right, f32[2048,1024]{1,0:T(8,128)} %get-tuple-element.189.pre, bf16[4,2,64,1024]{3,2,1,0:T(8,128)(2,1)} %copy-done.5, ...), custom_call_target="tpu_custom_call" | custom-call | tf_op jit(solution)/shard_map/pallas_call | solution.py:279
  268.7 14.2 %shard_map.235 = (bf16[4,2,2,64,1024]{4,3,2,1,0:T(8,128)(2,1)}, bf16[4,2,2,64,1024]{4,3,2,1,0:T(8,128)(2,1)}) custom-call(s32[2]{0:T(128)} %pad_add_fusion.place, bf16[2048,2048]{1,0:T(8,128)(2,1)} %shard_map.230.normed.left, bf16[2048,1024]{1,0:T(8,128)(2,1)} %get-tuple-element.216.right.two), custom_call_target="tpu_custom_call" | custom-call | tf_op jit(solution)/shard_map/pallas_call | solution.py:334
  282.9 14.0 %shard_map.236 = bf16[2048,768]{1,0:T(8,128)(2,1)} custom-call(s32[2]{0:T(128)} %pad_add_fusion.place, bf16[2048,2048]{1,0:T(8,128)(2,1)} %shard_map.230.normed.left, f32[1,768]{1,0:T(1,128)} %bitcast.211, f32[2048,128]{1,0:T(8,128)} %bitcast.184, f32[2048,128]{1,0:T(8,128)} %bitcast.185, bf16[4,2,64,768]{3,2,1,0:T(8,128)(2,1)} %slice.173.refs_0_, ...), custom_call_target="tpu_custom_call" | custom-call | tf_op jit(solution)/shard_map/pallas_call | solution.py:413
  298.1 2.5 convert_add_fusion.1
  301.4 33.2 %shard_map.237 = (bf16[4,2,256,256]{3,2,1,0:T(8,128)(2,1)}, bf16[4,2,256,768]{3,2,1,0:T(8,128)(2,1)}) custom-call(s32[4]{0:T(128)} %fusion.34.order, bf16[4,2,256,768]{3,2,1,0:T(8,128)(2,1)} %bitcast.164, bf16[4,2,256,768]{3,2,1,0:T(8,128)(2,1)} %bitcast.165, bf16[4,2,256,768]{3,2,1,0:T(8,128)(2,1)} %bitcast.166, bf16[4,2,256,256]{3,2,1,0:T(8,128)(2,1)} %bitcast.198, ...), custom_call_target="tpu_custom_call" | custom-call | tf_op jit(solution)/shard_map/pallas_call | solution.py:674
  334.6 12.6 %shard_map.238 = (bf16[4,2,2,64,768]{4,3,2,1,0:T(8,128)(2,1)}, bf16[4,2,2,64,768]{4,3,2,1,0:T(8,128)(2,1)}) custom-call(s32[2]{0:T(128)} %pad_add_fusion.place, bf16[2048,2048]{1,0:T(8,128)(2,1)} %shard_map.230.normed.left, bf16[2048,768]{1,0:T(8,128)(2,1)} %bitcast.171), custom_call_target="tpu_custom_call" | custom-call | tf_op jit(solution)/shard_map/pallas_call | solution.py:334
  349.3 4.6 all-to-all-start.2
  355.1 2.5 convert_add_fusion
  358.8 1.9 collective-permute-start.30
  360.7 23.4 %shard_map.239 = (bf16[1024,2048]{1,0:T(8,128)(2,1)}, bf16[1024,2048]{1,0:T(8,128)(2,1)}) custom-call(s32[2]{0:T(128)} %pad_add_fusion.place, bf16[2048,768]{1,0:T(8,128)(2,1)} %bitcast.172, bf16[2048,1024]{1,0:T(8,128)(2,1)} %get-tuple-element.216.right.two, bf16[4,2,64,768]{3,2,1,0:T(8,128)(2,1)} %slice.173.refs_0_, bf16[4,2,64,768]{3,2,1,0:T(8,128)(2,1)} %copy-done.18, ...), custom_call_target="tpu_custom_call" | custom-call | tf_op jit(solution)/shard_map/pallas_call | solution.py:456
  384.1 18.2 %shard_map.240 = (bf16[1024,2048]{1,0:T(8,128)(2,1)}, bf16[1024,2048]{1,0:T(8,128)(2,1)}) custom-call(s32[2]{0:T(128)} %pad_add_fusion.place, bf16[2048,1024]{1,0:T(8,128)(2,1)} %get-tuple-element.218.right.one, bf16[2048,256]{1,0:T(8,128)(2,1)} %bitcast.195, bf16[4,2,64,1024]{3,2,1,0:T(8,128)(2,1)} %copy-done.5, ...), custom_call_target="tpu_custom_call" | custom-call | tf_op jit(solution)/shard_map/pallas_call | solution.py:456
  402.3 6.9 %shard_map.241 = (bf16[2,64,2048]{2,1,0:T(8,128)(2,1)}, bf16[2,64,2048]{2,1,0:T(8,128)(2,1)}) custom-call(s32[2]{0:T(128)} %pad_add_fusion.place, bf16[2048,256]{1,0:T(8,128)(2,1)} %bitcast.196, bf16[2048,2048]{1,0:T(8,128)(2,1)} %get-tuple-element.188.left.grad.right), custom_call_target="tpu_custom_call" | custom-call | tf_op jit(solution)/shard_map/pallas_call | solution.py:380
  410.7 2.6 add_convert_fusion
  413.2 4.4 all-to-all-start.3
  417.6 1.9 convert_add_fusion.2
  419.6 1.7 copy-done.3
  421.3 2.5 fusion.22
  424.9 1.9 collective-permute-start.34
  434.3 2.4 convert_reduce_fusion
  436.9 2.7 shard_map.244
  439.6 1.6 dynamic-slice_bitcast_fusion.2
  441.2 28.0 %collective-permute-done.32 = bf16[2,2,2,64,768]{4,3,2,1,0:T(8,128)(2,1)} collective-permute-done((bf16[2,2,2,64,768]{4,3,2,1,0:T(8,128)(2,1)S(1)}, bf16[2,2,2,64,768]{4,3,2,1,0:T(8,128)(2,1)}, u32[]{:S(2)}, u32[]{:S(2)}) %collective-permute-start.32) | collective-permute-done | bytes 786464 | tf_op jit(solution)/shard_map/ppermute | solution.py:41
  469.2 2.3 collective-permute-done.35
  471.4 5.2 fusion.17
  479.2 3.1 fusion.26
  486.1 2.2 add_convert_fusion.2
  488.3 4.5 all-to-all-start.4
  497.1 2.7 shard_map.243
  502.5 12.7 %collective-permute-done.37 = bf16[2,256,1024]{2,1,0:T(8,128)(2,1)} collective-permute-done((bf16[2,256,1024]{2,1,0:T(8,128)(2,1)}, bf16[2,256,1024]{2,1,0:T(8,128)(2,1)}, u32[]{:S(2)}, u32[]{:S(2)}) %collective-permute-start.37) | collective-permute-done | bytes 1048608 | tf_op jit(solution)/shard_map/ppermute | solution.py:41
  515.2 4.8 collective-permute-done.38
  520.0 4.8 fusion.15
  524.8 1.7 all-to-all-done.4.value
  529.1 2.1 convert_reduce_fusion.2
  532.2 3.1 all-to-all-start.5
  535.3 1.9 bitcast_add_fusion
  537.2 2.5 shard_map.242
  539.7 3.7 all-to-all-done.5
  (250 shorter events, 72.7 us)
Async XLA Ops:
  4.3 45.6 %all-to-all-start = ((bf16[8,64,2816]{2,1,0:T(8,128)(2,1)}), bf16[8,64,2816]{2,1,0:T(8,128)(2,1)S(1)}, u32[]{:S(2)}, u32[]{:S(2)}) async-start(bf16[8,64,2816]{2,1,0:T(8,128)(2,1)} %shard_map.229), calls=%async_computation | async-start | bytes 5767168 | tf_op jit(solution)/shard_map/all_to_all | solution.py:60
  9.7 37.6 %collective-permute-start = (bf16[1,1,64,2048]{3,2,1,0:T(8,128)(2,1)S(1)}, bf16[1,1,64,2048]{3,2,1,0:T(8,128)(2,1)S(1)}, u32[]{:S(2)}, u32[]{:S(2)}) collective-permute-start(bf16[1,1,64,2048]{3,2,1,0:T(8,128)(2,1)S(1)} %bitcast.203), channel_id=1, source_target_pairs={{0,4},{4,0},{1,5},{5,1},{2,6},{6,2},{3,7},{7,3},{8,12},{12,8},{9,1... | collective-permute-start | bytes 786440 | tf_op jit(solution)/shard_map/ppermute | solution.py:41
  12.3 35.0 %collective-permute-start.1 = (bf16[1,1,64,2048]{3,2,1,0:T(8,128)(2,1)S(1)}, bf16[1,1,64,2048]{3,2,1,0:T(8,128)(2,1)}, u32[]{:S(2)}, u32[]{:S(2)}) collective-permute-start(bf16[1,1,64,2048]{3,2,1,0:T(8,128)(2,1)S(1)} %bitcast.204), channel_id=1, source_target_pairs={{0,1},{1,0},{2,3},{3,2},{4,5},{5,4},{6,7},{7,6},{8,9},{9,8},{10,11... | collective-permute-start | bytes 786440 | tf_op jit(solution)/shard_map/ppermute | solution.py:41
  13.9 53.0 %collective-permute-start.6 = (bf16[256,2048]{1,0:T(8,128)(2,1)}, bf16[256,2048]{1,0:T(8,128)(2,1)}, u32[]{:S(2)}, u32[]{:S(2)}) collective-permute-start(bf16[256,2048]{1,0:T(8,128)(2,1)} %bitcast.190), channel_id=1, source_target_pairs={{0,16},{16,0},{1,17},{17,1},{2,18},{18,2},{3,19},{19,3},{4,20},{20... | collective-permute-start | bytes 3145736 | tf_op jit(solution)/shard_map/ppermute | solution.py:41
  47.3 12.6 %copy-start.31 = (bf16[1,1,64,2048]{3,2,1,0:T(8,128)(2,1)}, bf16[1,1,64,2048]{3,2,1,0:T(8,128)(2,1)S(1)}, u32[]{:S(2)}) copy-start(bf16[1,1,64,2048]{3,2,1,0:T(8,128)(2,1)S(1)} %collective-permute-done) | copy-start | bytes 786436
  53.3 63.5 %copy-start.4 = (bf16[4,2,64,1024]{3,2,1,0:T(8,128)(2,1)}, bf16[4,2,64,1024]{3,2,1,0:T(8,128)(2,1)S(1)}, u32[]{:S(2)}) copy-start(bf16[4,2,64,1024]{3,2,1,0:T(8,128)(2,1)S(1)} %get-tuple-element.277.refs_0_.refs_4_) | copy-start | bytes 3145732
  53.4 63.5 %copy-start.5 = (bf16[4,2,64,1024]{3,2,1,0:T(8,128)(2,1)}, bf16[4,2,64,1024]{3,2,1,0:T(8,128)(2,1)S(1)}, u32[]{:S(2)}) copy-start(bf16[4,2,64,1024]{3,2,1,0:T(8,128)(2,1)S(1)} %get-tuple-element.138.refs_0_) | copy-start | bytes 3145732
  53.4 54.8 %collective-permute-start.2 = (bf16[4,2,64,1024]{3,2,1,0:T(8,128)(2,1)S(1)}, bf16[4,2,64,1024]{3,2,1,0:T(8,128)(2,1)}, u32[]{:S(2)}, u32[]{:S(2)}) collective-permute-start(bf16[4,2,64,1024]{3,2,1,0:T(8,128)(2,1)S(1)} %get-tuple-element.277.refs_0_.refs_4_), channel_id=1, source_target_pairs={{0,4},{4,0},{1,5},{5,1},{2,6},{6,2},{3,7},{7,3},{8,12},{12,8},{9,1... | collective-permute-start | bytes 3145736 | tf_op jit(solution)/shard_map/ppermute | solution.py:41
  54.3 54.0 %collective-permute-start.3 = (bf16[4,2,64,1024]{3,2,1,0:T(8,128)(2,1)S(1)}, bf16[4,2,64,1024]{3,2,1,0:T(8,128)(2,1)}, u32[]{:S(2)}, u32[]{:S(2)}) collective-permute-start(bf16[4,2,64,1024]{3,2,1,0:T(8,128)(2,1)S(1)} %get-tuple-element.277.refs_0_.refs_4_), channel_id=1, source_target_pairs={{0,1},{1,0},{2,3},{3,2},{4,5},{5,4},{6,7},{7,6},{8,9},{9,8},{10,11... | collective-permute-start | bytes 3145736 | tf_op jit(solution)/shard_map/ppermute | solution.py:41
  55.8 52.4 %collective-permute-start.4 = (bf16[256,2048]{1,0:T(8,128)(2,1)S(1)}, bf16[256,2048]{1,0:T(8,128)(2,1)}, u32[]{:S(2)}, u32[]{:S(2)}) collective-permute-start(bf16[256,2048]{1,0:T(8,128)(2,1)S(1)} %bitcast.168), channel_id=1, source_target_pairs={{0,2},{2,0},{1,3},{3,1},{4,6},{6,4},{5,7},{7,5},{8,10},{10,8},{9,1... | collective-permute-start | bytes 3145736 | tf_op jit(solution)/shard_map/ppermute | solution.py:41
  57.4 50.8 %collective-permute-start.5 = (bf16[256,2048]{1,0:T(8,128)(2,1)S(1)}, bf16[256,2048]{1,0:T(8,128)(2,1)}, u32[]{:S(2)}, u32[]{:S(2)}) collective-permute-start(bf16[256,2048]{1,0:T(8,128)(2,1)S(1)} %bitcast.169), channel_id=1, source_target_pairs={{0,16},{16,0},{1,17},{17,1},{2,18},{18,2},{3,19},{19,3},{4,20},{20... | collective-permute-start | bytes 3145736 | tf_op jit(solution)/shard_map/ppermute | solution.py:41
  59.9 48.4 %all-to-all-start.1 = ((f32[32,10,128]{2,1,0:T(8,128)}), f32[32,10,128]{2,1,0:T(8,128)S(1)}, u32[]{:S(2)}, u32[]{:S(2)}) async-start(f32[32,10,128]{2,1,0:T(8,128)} %broadcast_in_dim.14), calls=%async_computation.1 | async-start | bytes 524288 | tf_op jit(solution)/shard_map/all_to_all | solution.py:150
  109.0 48.7 %collective-permute-start.7 = (bf16[4,2,64,1024]{3,2,1,0:T(8,128)(2,1)S(1)}, bf16[4,2,64,1024]{3,2,1,0:T(8,128)(2,1)}, u32[]{:S(2)}, u32[]{:S(2)}) collective-permute-start(bf16[4,2,64,1024]{3,2,1,0:T(8,128)(2,1)S(1)} %get-tuple-element.138.refs_0_), channel_id=1, source_target_pairs={{0,4},{4,0},{1,5},{5,1},{2,6},{6,2},{3,7},{7,3},{8,12},{12,8},{9,1... | collective-permute-start | bytes 3145736 | tf_op jit(solution)/shard_map/ppermute | solution.py:41
  110.4 47.3 %collective-permute-start.8 = (bf16[4,2,64,1024]{3,2,1,0:T(8,128)(2,1)S(1)}, bf16[4,2,64,1024]{3,2,1,0:T(8,128)(2,1)}, u32[]{:S(2)}, u32[]{:S(2)}) collective-permute-start(bf16[4,2,64,1024]{3,2,1,0:T(8,128)(2,1)S(1)} %get-tuple-element.138.refs_0_), channel_id=1, source_target_pairs={{0,1},{1,0},{2,3},{3,2},{4,5},{5,4},{6,7},{7,6},{8,9},{9,8},{10,11... | collective-permute-start | bytes 3145736 | tf_op jit(solution)/shard_map/ppermute | solution.py:41
  111.3 46.9 %collective-permute-start.10 = (bf16[256,2048]{1,0:T(8,128)(2,1)}, bf16[256,2048]{1,0:T(8,128)(2,1)}, u32[]{:S(2)}, u32[]{:S(2)}) collective-permute-start(bf16[256,2048]{1,0:T(8,128)(2,1)} %collective-permute-done.4.refs_1_), channel_id=1, source_target_pairs={{0,16},{16,0},{1,17},{17,1},{2,18},{18,2},{3,19},{19,3},{4,20},{20... | collective-permute-start | bytes 3145736 | tf_op jit(solution)/shard_map/ppermute | solution.py:41
  112.1 46.2 %collective-permute-start.9 = (bf16[4,2,64,1024]{3,2,1,0:T(8,128)(2,1)}, bf16[4,2,64,1024]{3,2,1,0:T(8,128)(2,1)}, u32[]{:S(2)}, u32[]{:S(2)}) collective-permute-start(bf16[4,2,64,1024]{3,2,1,0:T(8,128)(2,1)} %collective-permute-done.2.refs_1_.refs_5_), channel_id=1, source_target_pairs={{0,1},{1,0},{2,3},{3,2},{4,5},{5,4},{6,7},{7,6},{8,9},{9,8},{10,11... | collective-permute-start | bytes 3145736 | tf_op jit(solution)/shard_map/ppermute | solution.py:41
  113.1 46.3 %collective-permute-start.11 = (bf16[256,2048]{1,0:T(8,128)(2,1)}, bf16[256,2048]{1,0:T(8,128)(2,1)}, u32[]{:S(2)}, u32[]{:S(2)}) collective-permute-start(bf16[256,2048]{1,0:T(8,128)(2,1)} %bitcast.191), channel_id=1, source_target_pairs={{0,2},{2,0},{1,3},{3,1},{4,6},{6,4},{5,7},{7,5},{8,10},{10,8},{9,1... | collective-permute-start | bytes 3145736 | tf_op jit(solution)/shard_map/ppermute | solution.py:41
  122.9 44.6 %copy-start.6 = (bf16[4,2,64,768]{3,2,1,0:T(8,128)(2,1)S(1)}, bf16[4,2,64,768]{3,2,1,0:T(8,128)(2,1)}, u32[]{:S(2)}) copy-start(bf16[4,2,64,768]{3,2,1,0:T(8,128)(2,1)} %slice.173.refs_0_) | copy-start | bytes 2359300
  122.9 45.5 %copy-start.32 = (bf16[1,1,64,2048]{3,2,1,0:T(8,128)(2,1)S(1)}, bf16[1,1,64,2048]{3,2,1,0:T(8,128)(2,1)}, u32[]{:S(2)}) copy-start(bf16[1,1,64,2048]{3,2,1,0:T(8,128)(2,1)} %copy-done.31) | copy-start | bytes 786436
  157.7 4.1 collective-permute-start.12
  157.7 4.4 collective-permute-start.13
  158.2 5.4 collective-permute-start.14
  161.4 3.6 collective-permute-start.15
  165.1 48.6 %collective-permute-start.18 = (bf16[4,2,64,1024]{3,2,1,0:T(8,128)(2,1)}, bf16[4,2,64,1024]{3,2,1,0:T(8,128)(2,1)S(1)}, u32[]{:S(2)}, u32[]{:S(2)}) collective-permute-start(bf16[4,2,64,1024]{3,2,1,0:T(8,128)(2,1)} %collective-permute-done.7.refs_1_), channel_id=1, source_target_pairs={{0,1},{1,0},{2,3},{3,2},{4,5},{5,4},{6,7},{7,6},{8,9},{9,8},{10,11... | collective-permute-start | bytes 3145736 | tf_op jit(solution)/shard_map/ppermute | solution.py:41
  166.2 48.3 %collective-permute-start.19 = (bf16[256,2048]{1,0:T(8,128)(2,1)}, bf16[256,2048]{1,0:T(8,128)(2,1)}, u32[]{:S(2)}, u32[]{:S(2)}) collective-permute-start(bf16[256,2048]{1,0:T(8,128)(2,1)} %collective-permute-done.11.refs_1_), channel_id=1, source_target_pairs={{0,16},{16,0},{1,17},{17,1},{2,18},{18,2},{3,19},{19,3},{4,20},{20... | collective-permute-start | bytes 3145736 | tf_op jit(solution)/shard_map/ppermute | solution.py:41
  167.5 45.6 %collective-permute-start.16 = (bf16[4,2,64,768]{3,2,1,0:T(8,128)(2,1)S(1)}, bf16[4,2,64,768]{3,2,1,0:T(8,128)(2,1)S(1)}, u32[]{:S(2)}, u32[]{:S(2)}) collective-permute-start(bf16[4,2,64,768]{3,2,1,0:T(8,128)(2,1)S(1)} %copy-done.6), channel_id=1, source_target_pairs={{0,4},{4,0},{1,5},{5,1},{2,6},{6,2},{3,7},{7,3},{8,12},{12,8},{9,1... | collective-permute-start | bytes 2359304 | tf_op jit(solution)/shard_map/ppermute | solution.py:41
  167.5 46.1 %collective-permute-start.17 = (bf16[4,2,64,768]{3,2,1,0:T(8,128)(2,1)S(1)}, bf16[4,2,64,768]{3,2,1,0:T(8,128)(2,1)S(1)}, u32[]{:S(2)}, u32[]{:S(2)}) collective-permute-start(bf16[4,2,64,768]{3,2,1,0:T(8,128)(2,1)S(1)} %copy-done.6), channel_id=1, source_target_pairs={{0,1},{1,0},{2,3},{3,2},{4,5},{5,4},{6,7},{7,6},{8,9},{9,8},{10,11... | collective-permute-start | bytes 2359304 | tf_op jit(solution)/shard_map/ppermute | solution.py:41
  168.4 44.6 %collective-permute-start.20 = (bf16[1,1,64,2048]{3,2,1,0:T(8,128)(2,1)S(1)}, bf16[1,1,64,2048]{3,2,1,0:T(8,128)(2,1)}, u32[]{:S(2)}, u32[]{:S(2)}) collective-permute-start(bf16[1,1,64,2048]{3,2,1,0:T(8,128)(2,1)S(1)} %copy-done.32), channel_id=1, source_target_pairs={{0,1},{1,0},{2,3},{3,2},{4,5},{5,4},{6,7},{7,6},{8,9},{9,8},{10,11... | collective-permute-start | bytes 786440 | tf_op jit(solution)/shard_map/ppermute | solution.py:41
  181.4 32.1 %copy-start.13 = (bf16[1,256,2048]{2,1,0:T(8,128)(2,1)S(1)}, bf16[1,256,2048]{2,1,0:T(8,128)(2,1)}, u32[]{:S(2)}) copy-start(bf16[1,256,2048]{2,1,0:T(8,128)(2,1)} %param.27) | copy-start | bytes 3145732
  181.4 33.2 %copy-start.30 = (bf16[64,2048]{1,0:T(8,128)(2,1)S(1)}, bf16[64,2048]{1,0:T(8,128)(2,1)}, u32[]{:S(2)}) copy-start(bf16[64,2048]{1,0:T(8,128)(2,1)} %param.16) | copy-start | bytes 786436
  213.0 4.2 collective-permute-start.23
  213.1 6.0 %collective-permute-start.22 = (bf16[256,2048]{1,0:T(8,128)(2,1)}, bf16[256,2048]{1,0:T(8,128)(2,1)}, u32[]{:S(2)}, u32[]{:S(2)}) collective-permute-start(bf16[256,2048]{1,0:T(8,128)(2,1)} %collective-permute-done.11.refs_1_), channel_id=1, source_target_pairs={{0,8},{8,0},{1,9},{9,1},{2,10},{10,2},{3,11},{11,3},{4,12},{12,4},... | collective-permute-start | bytes 3145736 | tf_op jit(solution)/shard_map/ppermute | solution.py:41
  213.6 5.3 collective-permute-start.21
  214.4 6.1 %collective-permute-start.24 = (bf16[256,2048]{1,0:T(8,128)(2,1)}, bf16[256,2048]{1,0:T(8,128)(2,1)}, u32[]{:S(2)}, u32[]{:S(2)}) collective-permute-start(bf16[256,2048]{1,0:T(8,128)(2,1)} %collective-permute-done.19.refs_3_), channel_id=1, source_target_pairs={{0,8},{8,0},{1,9},{9,1},{2,10},{10,2},{3,11},{11,3},{4,12},{12,4},... | collective-permute-start | bytes 3145736 | tf_op jit(solution)/shard_map/ppermute | solution.py:41
  220.5 25.9 %collective-permute-start.25 = (bf16[4,2,64,768]{3,2,1,0:T(8,128)(2,1)S(1)}, bf16[4,2,64,768]{3,2,1,0:T(8,128)(2,1)S(1)}, u32[]{:S(2)}, u32[]{:S(2)}) collective-permute-start(bf16[4,2,64,768]{3,2,1,0:T(8,128)(2,1)S(1)} %collective-permute-done.16.refs_1_), channel_id=1, source_target_pairs={{0,1},{1,0},{2,3},{3,2},{4,5},{5,4},{6,7},{7,6},{8,9},{9,8},{10,11... | collective-permute-start | bytes 2359304 | tf_op jit(solution)/shard_map/ppermute | solution.py:41
  246.4 22.2 %copy-start.20 = (bf16[4,2,64,768]{3,2,1,0:T(8,128)(2,1)}, bf16[4,2,64,768]{3,2,1,0:T(8,128)(2,1)S(1)}, u32[]{:S(2)}) copy-start(bf16[4,2,64,768]{3,2,1,0:T(8,128)(2,1)S(1)} %collective-permute-done.25.refs_3_) | copy-start | bytes 2359300
  246.4 50.5 %collective-permute-start.26 = (bf16[4,2,2,64,1024]{4,3,2,1,0:T(8,128)(2,1)}, bf16[4,2,2,64,1024]{4,3,2,1,0:T(8,128)(2,1)}, u32[]{:S(2)}, u32[]{:S(2)}) collective-permute-start(bf16[4,2,2,64,1024]{4,3,2,1,0:T(8,128)(2,1)} %get-tuple-element.187), channel_id=1, source_target_pairs={{0,1},{1,0},{2,3},{3,2},{4,5},{5,4},{6,7},{7,6},{8,9},{9,8},{10,11... | collective-permute-start | bytes 6291464 | tf_op jit(solution)/shard_map/ppermute | solution.py:41
  282.9 15.3 %copy-start.22 = (bf16[4,2,2,64,1024]{4,3,2,1,0:T(8,128)(2,1)S(1)}, bf16[4,2,2,64,1024]{4,3,2,1,0:T(8,128)(2,1)}, u32[]{:S(2)}) copy-start(bf16[4,2,2,64,1024]{4,3,2,1,0:T(8,128)(2,1)} %get-tuple-element.206) | copy-start | bytes 6291460
  296.9 51.0 %collective-permute-start.27 = (bf16[4,2,2,64,1024]{4,3,2,1,0:T(8,128)(2,1)}, bf16[4,2,2,64,1024]{4,3,2,1,0:T(8,128)(2,1)}, u32[]{:S(2)}, u32[]{:S(2)}) collective-permute-start(bf16[4,2,2,64,1024]{4,3,2,1,0:T(8,128)(2,1)} %get-tuple-element.205), channel_id=1, source_target_pairs={{0,1},{1,0},{2,3},{3,2},{4,5},{5,4},{6,7},{7,6},{8,9},{9,8},{10,11... | collective-permute-start | bytes 6291464 | tf_op jit(solution)/shard_map/ppermute | solution.py:41
  300.8 47.1 %collective-permute-start.28 = (bf16[2,2,2,64,1024]{4,3,2,1,0:T(8,128)(2,1)S(1)}, bf16[2,2,2,64,1024]{4,3,2,1,0:T(8,128)(2,1)S(1)}, u32[]{:S(2)}, u32[]{:S(2)}) collective-permute-start(bf16[2,2,2,64,1024]{4,3,2,1,0:T(8,128)(2,1)S(1)} %fusion.12), channel_id=1, source_target_pairs={{0,4},{4,0},{1,5},{5,1},{2,6},{6,2},{3,7},{7,3},{8,12},{12,8},{9,1... | collective-permute-start | bytes 3145736 | tf_op jit(solution)/shard_map/ppermute | solution.py:41
  349.3 60.1 %all-to-all-start.2 = ((bf16[8,64,1024]{2,1,0:T(8,128)(2,1)}), bf16[8,64,1024]{2,1,0:T(8,128)(2,1)}, u32[]{:S(2)}, u32[]{:S(2)}) async-start(bf16[8,64,1024]{2,1,0:T(8,128)(2,1)} %bitcast.31), calls=%async_computation.2 | async-start | bytes 2097152 | tf_op jit(solution)/shard_map/all_to_all | solution.py:131
  353.9 55.5 %collective-permute-start.29 = (bf16[4,2,2,64,768]{4,3,2,1,0:T(8,128)(2,1)}, bf16[4,2,2,64,768]{4,3,2,1,0:T(8,128)(2,1)}, u32[]{:S(2)}, u32[]{:S(2)}) collective-permute-start(bf16[4,2,2,64,768]{4,3,2,1,0:T(8,128)(2,1)} %get-tuple-element.210), channel_id=1, source_target_pairs={{0,1},{1,0},{2,3},{3,2},{4,5},{5,4},{6,7},{7,6},{8,9},{9,8},{10,11... | collective-permute-start | bytes 4718600 | tf_op jit(solution)/shard_map/ppermute | solution.py:41
  358.8 50.6 %collective-permute-start.30 = (bf16[2,2,2,64,1024]{4,3,2,1,0:T(8,128)(2,1)}, bf16[2,2,2,64,1024]{4,3,2,1,0:T(8,128)(2,1)}, u32[]{:S(2)}, u32[]{:S(2)}) collective-permute-start(bf16[2,2,2,64,1024]{4,3,2,1,0:T(8,128)(2,1)} %fusion.13), channel_id=1, source_target_pairs={{0,4},{4,0},{1,5},{5,1},{2,6},{6,2},{3,7},{7,3},{8,12},{12,8},{9,1... | collective-permute-start | bytes 3145736 | tf_op jit(solution)/shard_map/ppermute | solution.py:41
  409.4 11.9 %collective-permute-start.31 = (bf16[1024,2048]{1,0:T(8,128)(2,1)}, bf16[1024,2048]{1,0:T(8,128)(2,1)}, u32[]{:S(2)}, u32[]{:S(2)}) collective-permute-start(bf16[1024,2048]{1,0:T(8,128)(2,1)} %get-tuple-element.224), channel_id=1, source_target_pairs={{0,8},{8,0},{1,9},{9,1},{2,10},{10,2},{3,11},{11,3},{4,12},{12,4},... | collective-permute-start | bytes 12582920 | tf_op jit(solution)/shard_map/ppermute | solution.py:41
  409.5 67.2 %collective-permute-start.33 = (bf16[1024,2048]{1,0:T(8,128)(2,1)}, bf16[1024,2048]{1,0:T(8,128)(2,1)}, u32[]{:S(2)}, u32[]{:S(2)}) collective-permute-start(bf16[1024,2048]{1,0:T(8,128)(2,1)} %get-tuple-element.228), channel_id=1, source_target_pairs={{0,8},{8,0},{1,9},{9,1},{2,10},{10,2},{3,11},{11,3},{4,12},{12,4},... | collective-permute-start | bytes 12582920 | tf_op jit(solution)/shard_map/ppermute | solution.py:41
  413.2 63.5 %all-to-all-start.3 = ((bf16[8,64,1024]{2,1,0:T(8,128)(2,1)}), bf16[8,64,1024]{2,1,0:T(8,128)(2,1)}, u32[]{:S(2)}, u32[]{:S(2)}) async-start(bf16[8,64,1024]{2,1,0:T(8,128)(2,1)} %bitcast.194), calls=%async_computation.3 | async-start | bytes 2097152 | tf_op jit(solution)/shard_map/all_to_all | solution.py:131
  424.9 44.3 %collective-permute-start.34 = (bf16[2,256,1024]{2,1,0:T(8,128)(2,1)}, bf16[2,256,1024]{2,1,0:T(8,128)(2,1)}, u32[]{:S(2)}, u32[]{:S(2)}) collective-permute-start(bf16[2,256,1024]{2,1,0:T(8,128)(2,1)} %pad_maximum_fusion.3), channel_id=1, source_target_pairs={{0,16},{16,0},{1,17},{17,1},{2,18},{18,2},{3,19},{19,3},{4,20},{20... | collective-permute-start | bytes 3145736 | tf_op jit(solution)/shard_map/ppermute | solution.py:41
  427.9 43.6 %collective-permute-start.35 = (bf16[2,256,1024]{2,1,0:T(8,128)(2,1)}, bf16[2,256,1024]{2,1,0:T(8,128)(2,1)}, u32[]{:S(2)}, u32[]{:S(2)}) collective-permute-start(bf16[2,256,1024]{2,1,0:T(8,128)(2,1)} %pad_maximum_fusion.4), channel_id=1, source_target_pairs={{0,2},{2,0},{1,3},{3,1},{4,6},{6,4},{5,7},{7,5},{8,10},{10,8},{9,1... | collective-permute-start | bytes 3145736 | tf_op jit(solution)/shard_map/ppermute | solution.py:41
  429.4 39.8 %collective-permute-start.32 = (bf16[2,2,2,64,768]{4,3,2,1,0:T(8,128)(2,1)S(1)}, bf16[2,2,2,64,768]{4,3,2,1,0:T(8,128)(2,1)}, u32[]{:S(2)}, u32[]{:S(2)}) collective-permute-start(bf16[2,2,2,64,768]{4,3,2,1,0:T(8,128)(2,1)S(1)} %fusion.19), channel_id=1, source_target_pairs={{0,4},{4,0},{1,5},{5,1},{2,6},{6,2},{3,7},{7,3},{8,12},{12,8},{9,1... | collective-permute-start | bytes 2359304 | tf_op jit(solution)/shard_map/ppermute | solution.py:41
  433.5 43.2 %collective-permute-start.36 = (bf16[2,64,2048]{2,1,0:T(8,128)(2,1)}, bf16[2,64,2048]{2,1,0:T(8,128)(2,1)}, u32[]{:S(2)}, u32[]{:S(2)}) collective-permute-start(bf16[2,64,2048]{2,1,0:T(8,128)(2,1)} %get-tuple-element.231), channel_id=1, source_target_pairs={{0,1},{1,0},{2,3},{3,2},{4,5},{5,4},{6,7},{7,6},{8,9},{9,8},{10,11... | collective-permute-start | bytes 1572872 | tf_op jit(solution)/shard_map/ppermute | solution.py:41
  476.7 23.1 %collective-permute-start.39 = (bf16[256,1024]{1,0:T(8,128)(2,1)}, bf16[256,1024]{1,0:T(8,128)(2,1)}, u32[]{:S(2)}, u32[]{:S(2)}) collective-permute-start(bf16[256,1024]{1,0:T(8,128)(2,1)} %get-tuple-element.237), channel_id=1, source_target_pairs={{0,2},{2,0},{1,3},{3,1},{4,6},{6,4},{5,7},{7,5},{8,10},{10,8},{9,1... | collective-permute-start | bytes 1572872 | tf_op jit(solution)/shard_map/ppermute | solution.py:41
  477.7 23.3 %collective-permute-start.40 = (bf16[256,1024]{1,0:T(8,128)(2,1)S(1)}, bf16[256,1024]{1,0:T(8,128)(2,1)}, u32[]{:S(2)}, u32[]{:S(2)}) collective-permute-start(bf16[256,1024]{1,0:T(8,128)(2,1)S(1)} %get-tuple-element.239), channel_id=1, source_target_pairs={{0,16},{16,0},{1,17},{17,1},{2,18},{18,2},{3,19},{19,3},{4,20},{20... | collective-permute-start | bytes 1572872 | tf_op jit(solution)/shard_map/ppermute | solution.py:41
  483.4 31.8 %collective-permute-start.37 = (bf16[2,256,1024]{2,1,0:T(8,128)(2,1)}, bf16[2,256,1024]{2,1,0:T(8,128)(2,1)}, u32[]{:S(2)}, u32[]{:S(2)}) collective-permute-start(bf16[2,256,1024]{2,1,0:T(8,128)(2,1)} %pad_maximum_fusion.5), channel_id=1, source_target_pairs={{0,16},{16,0},{1,17},{17,1},{2,18},{18,2},{3,19},{19,3},{4,20},{20... | collective-permute-start | bytes 3145736 | tf_op jit(solution)/shard_map/ppermute | solution.py:41
  485.0 35.0 %collective-permute-start.38 = (bf16[2,256,1024]{2,1,0:T(8,128)(2,1)}, bf16[2,256,1024]{2,1,0:T(8,128)(2,1)}, u32[]{:S(2)}, u32[]{:S(2)}) collective-permute-start(bf16[2,256,1024]{2,1,0:T(8,128)(2,1)} %pad_maximum_fusion.6), channel_id=1, source_target_pairs={{0,2},{2,0},{1,3},{3,1},{4,6},{6,4},{5,7},{7,5},{8,10},{10,8},{9,1... | collective-permute-start | bytes 3145736 | tf_op jit(solution)/shard_map/ppermute | solution.py:41
  488.3 38.3 %all-to-all-start.4 = ((bf16[8,64,768]{2,1,0:T(8,128)(2,1)}), bf16[8,64,768]{2,1,0:T(8,128)(2,1)}, u32[]{:S(2)}, u32[]{:S(2)}) async-start(bf16[8,64,768]{2,1,0:T(8,128)(2,1)} %bitcast.50), calls=%async_computation.4 | async-start | bytes 1572864 | tf_op jit(solution)/shard_map/all_to_all | solution.py:131
  495.9 39.5 %collective-permute-start.43 = (bf16[64,2048]{1,0:T(8,128)(2,1)}, bf16[64,2048]{1,0:T(8,128)(2,1)S(1)}, u32[]{:S(2)}, u32[]{:S(2)}) collective-permute-start(bf16[64,2048]{1,0:T(8,128)(2,1)} %fusion.28), channel_id=1, source_target_pairs={{0,4},{4,0},{1,5},{5,1},{2,6},{6,2},{3,7},{7,3},{8,12},{12,8},{9,1... | collective-permute-start | bytes 786440 | tf_op jit(solution)/shard_map/ppermute | solution.py:41
  502.3 17.7 %copy-start.11 = (bf16[1024,2048]{1,0:T(8,128)(2,1)S(1)}, bf16[1024,2048]{1,0:T(8,128)(2,1)}, u32[]{:S(2)}) copy-start(bf16[1024,2048]{1,0:T(8,128)(2,1)} %get-tuple-element.234) | copy-start | bytes 12582916
  502.5 25.6 %copy-start.33 = (f32[2048]{0:T(1024)S(1)}, f32[2048]{0:T(1024)}, u32[]{:S(2)}) copy-start(f32[2048]{0:T(1024)} %mul.84) | copy-start | bytes 24580
  502.5 25.6 %copy-start.37 = (f32[256]{0:T(256)S(1)}, f32[256]{0:T(256)}, u32[]{:S(2)}) copy-start(f32[256]{0:T(256)} %copy-done.36) | copy-start | bytes 3076
  502.5 25.6 %copy-start.38 = (f32[256]{0:T(256)S(1)}, f32[256]{0:T(256)}, u32[]{:S(2)}) copy-start(f32[256]{0:T(256)} %add_rsqrt_fusion) | copy-start | bytes 3076
  526.6 18.7 %collective-permute-start.41 = (bf16[256,1024]{1,0:T(8,128)(2,1)}, bf16[256,1024]{1,0:T(8,128)(2,1)}, u32[]{:S(2)}, u32[]{:S(2)}) collective-permute-start(bf16[256,1024]{1,0:T(8,128)(2,1)} %get-tuple-element.241), channel_id=1, source_target_pairs={{0,2},{2,0},{1,3},{3,1},{4,6},{6,4},{5,7},{7,5},{8,10},{10,8},{9,1... | collective-permute-start | bytes 1572872 | tf_op jit(solution)/shard_map/ppermute | solution.py:41
  526.6 19.9 %collective-permute-start.42 = (bf16[256,1024]{1,0:T(8,128)(2,1)}, bf16[256,1024]{1,0:T(8,128)(2,1)}, u32[]{:S(2)}, u32[]{:S(2)}) collective-permute-start(bf16[256,1024]{1,0:T(8,128)(2,1)} %get-tuple-element.243), channel_id=1, source_target_pairs={{0,16},{16,0},{1,17},{17,1},{2,18},{18,2},{3,19},{19,3},{4,20},{20... | collective-permute-start | bytes 1572872 | tf_op jit(solution)/shard_map/ppermute | solution.py:41
  531.4 13.9 %copy-start.8 = (f32[256,1024]{1,0:T(8,128)S(1)}, f32[256,1024]{1,0:T(8,128)}, u32[]{:S(2)}) copy-start(f32[256,1024]{1,0:T(8,128)} %get-tuple-element.240) | copy-start | bytes 3145732
  532.2 11.2 %all-to-all-start.5 = ((f32[32,1,640]{2,1,0:T(1,128)}), f32[32,1,640]{2,1,0:T(1,128)S(1)}, u32[]{:S(2)}, u32[]{:S(2)}) async-start(f32[32,1,640]{2,1,0:T(1,128)} %all_to_all.26), calls=%async_computation.5 | async-start | bytes 163840 | tf_op jit(solution)/shard_map/all_to_all | solution.py:939
  (35 other events, 203.8 us)
